TPU v7x, 32 devices: a whole 2x2x4 slice. The times are simulated.
32 devices in a mesh: smp: 8 (over z, x), col: 2 (over core), slab: 2 (over y).
Axes of the slice: x: 2, y: 2, z: 4, core: 2. Of those that a mesh axis runs over, the one named last changes fastest.
Arguments:
- jacobian: bfloat16 [256, 32, 16384], P('smp', 'slab', 'col'), may hold values from -0.005722046 to 0.005722046
- local_energy: float32 [256], P('smp'), may hold values from -6 to 6
Outputs:
- update: float32 [32, 16384], P('slab', ('col', 'smp'))
All inputs are finite; a program needn't handle non-finite values.
Results may differ from a plain program's by a relative error of at most 0.0085.
Values may be sent and summed in bfloat16 or wider, within the bound.
No kernel may reach another device: no remote copies, remote signals or barrier semaphores. Data moves between devices by JAX's collectives and lax.ppermute only.
A program may use at most 192 MiB of HBM per device.

v0:
```python
import jax
import jax.numpy as jnp
from jax import lax
from jax.sharding import PartitionSpec as P

SLABS = 32
SLAB_COLS = 16384


def shards(jacobian, local_energy):
    energies = lax.all_gather(local_energy, "smp", axis=0, tiled=True)
    samples = energies.shape[0]
    root_count = jnp.sqrt(jnp.float32(samples))
    eps = (energies - jnp.mean(energies)) / root_count
    columns = lax.all_to_all(jacobian, "smp", split_axis=2, concat_axis=0, tiled=True)
    slab_count = columns.shape[1]
    width = columns.shape[2]
    values = columns.astype(jnp.float32)
    mean_row = jnp.mean(values, axis=0, keepdims=True)
    centered = (
        ((values - mean_row) / root_count).astype(jnp.bfloat16).reshape(samples, slab_count * width)
    )
    partial_gram = jnp.dot(centered, centered.T, preferred_element_type=jnp.float32)
    gram = lax.psum(partial_gram, ("smp", "col", "slab"))
    shift = 0.01 * jnp.trace(gram) / samples
    factor = jnp.linalg.cholesky(gram + shift * jnp.eye(samples, dtype=jnp.float32))
    middle = lax.linalg.triangular_solve(factor, eps[:, None], left_side=True, lower=True)
    coeffs = lax.linalg.triangular_solve(
        factor, middle, left_side=True, lower=True, transpose_a=True
    )[:, 0]
    delta = jnp.dot(coeffs, centered.astype(jnp.float32), precision=lax.Precision.HIGHEST)
    squared = lax.psum(jnp.sum(delta * delta), ("smp", "col", "slab"))
    limit = 0.3 * jnp.sqrt(jnp.float32(SLABS * SLAB_COLS))
    scaled = -jnp.minimum(1.0, limit / jnp.sqrt(squared)) * delta
    return scaled.reshape(slab_count, width)


def solution(mesh):
    in_specs = (P("smp", "slab", "col"), P("smp"))
    out_specs = P("slab", ("col", "smp"))
    return jax.shard_map(shards, mesh=mesh, in_specs=in_specs, out_specs=out_specs, check_vma=False)
```

profile of v0, /device:TPU:0, one launch (start us, length us, event | category | flops | bytes accessed | tf_op | source)
XLA Modules:
  0.0 628.6 jit_solution(12909296307691293898)
XLA Ops:
  6.5 45.6 %copy.29 = bf16[32,16,8192]{0,1,2:T(8,128)(2,1)} copy(bf16[32,16,8192]{2,1,0:T(8,128)(2,1)} %param.2) | data formatting | bytes 16777216 | tf_op args[0]
  52.1 35.2 %reshape.105 = bf16[8,2,262144]{2,1,0:T(2,128)(2,1)} reshape(bf16[8192,16,32]{2,1,0:T(8,128)(2,1)} %bitcast.89) | data formatting | bytes 16777216
  87.3 7.4 %all-to-all-start = ((bf16[8,2,262144]{2,1,0:T(2,128)(2,1)}), bf16[8,2,262144]{2,1,0:T(2,128)(2,1)}, u32[]{:S(2)}, u32[]{:S(2)}) async-start(bf16[8,2,262144]{2,1,0:T(2,128)(2,1)} %reshape.105), calls=%async_computation | async-start | bytes 16777216 | tf_op jit(solution)/shard_map/all_to_all | solution.py:15
  94.8 0.6 dynamic-slice.3
  96.0 0.2 dynamic-update-slice.11
  96.3 162.3 %all-reduce.1 = f32[256]{0:T(256)S(1)} all-reduce(f32[256]{0:T(256)S(1)} %dynamic-update-slice.11), channel_id=1, replica_groups=mesh['smp'=8,'col'=2,'slab'=2] {'smp'}, use_global_device_ids=true, to_apply=%add.1 | all-reduce | flops 256 | bytes 2048
  258.6 0.6 reduce_sum.39
  259.8 18.2 %all-to-all-done = bf16[8,2,262144]{2,1,0:T(2,128)(2,1)} async-done(((bf16[8,2,262144]{2,1,0:T(2,128)(2,1)}), bf16[8,2,262144]{2,1,0:T(2,128)(2,1)}, u32[]{:S(2)}, u32[]{:S(2)}) %all-to-all-start) | async-done | bytes 8388640 | tf_op jit(solution)/shard_map/all_to_all | solution.py:15
  278.0 20.9 %reshape.106 = bf16[8192,16,32]{2,1,0:T(8,128)(2,1)} reshape(bf16[8,2,262144]{2,1,0:T(2,128)(2,1)} %all-to-all-done) | data formatting | bytes 16777216
  298.8 39.4 %copy.30 = f32[32,16,8,1024]{3,1,0,2:T(8,128)} copy(bf16[32,16,8,1024]{0,1,3,2:T(8,128)(2,1)} %bitcast.88) | data formatting | bytes 25165824 | tf_op jit(solution)/shard_map/convert_element_type | solution.py:18
  338.3 6.7 %bitcast_reduce_fusion = f32[16,1024]{1,0:T(8,128)S(1)} fusion(f32[32,16,8,1024]{3,1,0,2:T(8,128)} %copy.30), kind=kLoop, calls=%fused_computation.3 | loop fusion | flops 4177920 | bytes 16842752 | tf_op jit(solution)/shard_map/reduce_sum | solution.py:19
  344.9 7.7 %fusion.1 = bf16[8,32,16,1024]{3,2,1,0:T(8,128)(2,1)S(1)} fusion(f32[32,16,8,1024]{3,1,0,2:T(8,128)} %copy.30, f32[16,1024]{1,0:T(8,128)S(1)} %broadcast_multiply_fusion.1), kind=kLoop, calls=%fused_computation.5 | loop fusion | flops 12582912 | bytes 25231360 | tf_op jit(solution)/shard_map/convert_element_type | solution.py:21
  352.7 3.2 copy-done
  355.9 18.2 %fusion.4 = f32[256,256]{0,1:T(8,128)} fusion(bf16[256,16,1024]{2,1,0:T(8,128)(2,1)S(1)} %bitcast.90), kind=kOutput, calls=%fused_computation.8 | convolution fusion | flops 2147483648 | bytes 8650752 | tf_op jit(solution)/shard_map/dot_general | solution.py:23
  374.2 15.9 %copy.42 = bf16[32,8,16,1024]{3,1,2,0:T(8,128)(2,1)} copy(bf16[32,8,16,1024]{3,2,1,0:T(8,128)(2,1)} %bitcast.91) | data formatting | bytes 16777216
  390.0 117.7 %all-reduce.4.cloned.1.call-done = f32[256,256]{0,1:T(8,128)} async-done(((f32[256,256]{0,1:T(8,128)}), f32[256,256]{0,1:T(8,128)}) %all-reduce.4.cloned.1.call-update) | async-done | bytes 262160 | tf_op jit(solution)/shard_map/psum | solution.py:24
  507.8 1.6 select_reduce_fusion
  509.9 1.0 select_add_fusion
  510.9 0.1 copy.34
  511.0 1.0 fusion.11
  512.0 11.7 %cholesky.49 = f32[128,128]{1,0:T(8,128)S(1)} custom-call(f32[128,128]{1,0:T(8,128)S(1)} %cholesky.115), custom_call_target="Cholesky" | custom-call | tf_op jit(solution)/shard_map/jit(cholesky)/cholesky | solution.py:26
  523.8 9.8 %custom-call.16 = f32[1,128,128]{1,2,0:T(8,128)S(1)} custom-call(f32[1,128,128]{2,1,0:T(8,128)S(1)} %get-tuple-element.40), custom_call_target="InvertDiagBlocksLowerTriangular" | custom-call | tf_op jit(solution)/shard_map/jit(cholesky)/cholesky | solution.py:26
  533.6 0.2 fusion.12
  533.8 0.3 convolution_subtract_fusion
  534.1 12.0 %cholesky.103 = f32[128,128]{1,0:T(8,128)S(1)} custom-call(f32[128,128]{1,0:T(8,128)S(1)} %convolution_subtract_fusion), custom_call_target="Cholesky" | custom-call | tf_op jit(solution)/shard_map/jit(cholesky)/cholesky | solution.py:26
  546.1 0.1 copy.37
  546.2 0.1 copy.36
  546.3 0.1 copy.35
  546.4 0.7 compare_reduce_fusion
  548.3 0.1 triangular_solve.75
  548.4 4.0 while.1
  548.4 0.6 fusion.35
  549.0 1.3 dynamic-slice.8
  550.3 0.1 copy.48
  550.4 0.6 fusion.35
  551.0 1.3 dynamic-slice.8
  552.3 0.1 copy.48
  552.4 19.7 %custom-call.17 = f32[2,128,128]{1,2,0:T(8,128)S(1)} custom-call(f32[2,128,128]{2,1,0:T(8,128)S(1)} %get-tuple-element.12), custom_call_target="InvertDiagBlocksLowerTriangular" | custom-call | tf_op jit(solution)/shard_map/triangular_solve | solution.py:28
  572.1 0.2 fusion.15
  572.2 0.2 fusion.10
  572.4 0.2 convolution_bitcast_fusion.3
  572.6 0.2 convolution_bitcast_fusion.2
  572.8 0.2 fusion.8
  573.0 0.2 convolution_bitcast_fusion
  573.2 6.8 %fusion.18 = f32[1,16384]{1,0:T(1,128)S(1)} fusion(bf16[256,16384]{1,0:T(8,128)(2,1)} %bitcast.92, f32[128,1]{0,1:T(1,128)S(1)} %convolution_bitcast_fusion.2, f32[128,1]{0,1:T(1,128)S(1)} %convolution_bitcast_fusion), kind=kOutput, calls=%fused_computation.44 | convolution fusion | flops 50331904 | bytes 8455168 | tf_op jit(solution)/shard_map/dot_general | solution.py:31
  580.0 0.6 multiply_reduce_fusion
  580.6 39.4 %psum.15 = f32[]{:T(128)} all-reduce(f32[]{:T(128)} %multiply_reduce_fusion), channel_id=1, replica_groups=mesh['smp'=8,'col'=2,'slab'=2] {'smp','col','slab'}, use_global_device_ids=true, to_apply=%region_9.10 | all-reduce | flops 1 | bytes 8 | tf_op jit(solution)/shard_map/psum | solution.py:32
  620.7 0.6 reshape.64
  (24 shorter events, 0.3 us)
Async XLA Ops:
  87.3 7.4 %copy-start.2 = (u32[32]{0:T(128)S(1)}, u32[32]{0:T(128)}, u32[]{:S(2)}) copy-start(u32[32]{0:T(128)} %constant.125) | copy-start | bytes 388
  87.3 8.7 %copy-start.1 = (f32[32]{0:T(128)S(1)}, f32[32]{0:T(128)}, u32[]{:S(2)}) copy-start(f32[32]{0:T(128)} %param.3) | copy-start | bytes 388
  87.3 190.6 %all-to-all-start = ((bf16[8,2,262144]{2,1,0:T(2,128)(2,1)}), bf16[8,2,262144]{2,1,0:T(2,128)(2,1)}, u32[]{:S(2)}, u32[]{:S(2)}) async-start(bf16[8,2,262144]{2,1,0:T(2,128)(2,1)} %reshape.105), calls=%async_computation | async-start | bytes 16777216 | tf_op jit(solution)/shard_map/all_to_all | solution.py:15
  94.7 413.1 %all-reduce.4.cloned.1.call-start = ((), (), s32[]{:S(2)}) async-start(), calls=%async_computation.1 | async-start | bytes 524288 | tf_op jit(solution)/shard_map/psum | solution.py:24
  352.7 3.2 copy-start
Sparse Core Ops, SparseCore 0:
  374.3 133.4 all-reduce.3
where the time goes:
time: 637 us; the launch traced here: 629 us
  blocking collectives  202 us (32%)
  local copies, waits for them, and re-layouts  166 us (26%)
  waiting for transfers between devices  136 us (21%)
  other arithmetic  73.1 us (11%)
  matrix products  26.6 us (4%)
  between operations  17.8 us (3%)
  starting transfers between devices  7.42 us (1%)
    unnamed x1, blocking collectives  162 us
    unnamed x13, local copies, waits for them, and re-layouts  122 us
    psum x1, waiting for transfers between devices, shards(): gram = lax.psum(partial_gram, ('smp', 'col', 'slab'))  118 us
    convert_element_type x1, local copies, waits for them, and re-layouts, shards(): values = columns.astype(jnp.float32)  39.4 us
    psum x1, blocking collectives, shards(): squared = lax.psum(jnp.sum(delta * delta), ('smp', 'col', 'slab'))  39.4 us
    another operation x6, other arithmetic, shards(): jnp.linalg.cholesky(gram + shift * jnp.eye(samples, dtype=jnp.float32))  34.2 us
    another operation x3, other arithmetic, shards(): lax.linalg.triangular_solve(factor, middle, left_side=True, lower=True, t...  19.7 us
    dot_general x1, matrix products, shards(): jnp.dot(centered, centered.T, preferred_element_type=jnp.float32)  18.2 us
  transfers between devices with their start and end apart: 2, of which 2 were waited for; matrix products, arithmetic and copies ran while one was open for 3% of the time, Pallas kernels for 0%

commit v1 on v0

v1 whole, which is shorter than its diff:
```python
import functools

import jax
import jax.numpy as jnp
from jax import lax
from jax.experimental import pallas as pl
from jax.experimental.pallas import tpu as pltpu
from jax.sharding import PartitionSpec as P

BLOCK = 64
LANES = 128
EXTRA = 16
F32 = jnp.float32
BF16 = jnp.bfloat16
HIGHEST = lax.Precision.HIGHEST
VMEM_LIMIT = 48 * 1024 * 1024


def mm(a, b, ca, cb):
    return lax.dot_general(
        a, b, (((ca,), (cb,)), ((), ())), precision=HIGHEST, preferred_element_type=F32
    )


def call(kernel, out_shape, grid_spec=None, **kw):
    if grid_spec is not None:
        kw["grid_spec"] = grid_spec
    return pl.pallas_call(
        kernel,
        out_shape=out_shape,
        compiler_params=pltpu.CompilerParams(vmem_limit_bytes=VMEM_LIMIT),
        cost_estimate=pl.CostEstimate(flops=0, bytes_accessed=0, transcendentals=0),
        **kw,
    )


def pack_kernel(early, apart, dest, j_ref, sum_ref, dev_ref, *packed):
    del dest
    rows, slabs, width = j_ref.shape
    first = slabs * early
    step = pl.program_id(0)
    x = j_ref[...].astype(F32)
    total = jnp.sum(x, axis=0)
    sum_ref[0] = total
    spread = x - (total * (1.0 / rows))[None]
    spread = jnp.sum(spread * spread, axis=0)

    @pl.when(step == 0)
    def _():
        dev_ref[...] = spread

    @pl.when(step > 0)
    def _():
        dev_ref[...] += spread

    y = jnp.swapaxes(x, 0, 1)
    y1 = y[:, :early].reshape(first, width).astype(BF16)
    y2 = y[:, early:].reshape(slabs * (rows - early), width).astype(BF16)
    if not apart:
        packed[0][0, :first, :] = y1
        packed[0][0, first:, :] = y2
        return
    for k in range(len(packed) // 2):

        @pl.when(step == k)
        def _():
            packed[2 * k][...] = y1
            packed[2 * k + 1][...] = y2


def pack(jacobian, dests, width, early, apart):
    rows, slabs, _ = jacobian.shape
    count = dests.shape[0]
    if apart:
        heights = (slabs * early, slabs * (rows - early)) * count
        shapes = [pltpu.HBM((h, width), BF16) for h in heights]
        specs = [pl.BlockSpec((h, width), lambda i, d: (0, 0)) for h in heights]
    else:
        shapes = [pltpu.HBM((count, slabs * rows, width), BF16)]
        specs = [pl.BlockSpec((1, slabs * rows, width), lambda i, d: (i, 0, 0))]
    return call(
        functools.partial(pack_kernel, early, apart),
        [
            pltpu.HBM((count, slabs, width), F32),
            pltpu.HBM((slabs, width), F32),
        ]
        + shapes,
        pltpu.PrefetchScalarGridSpec(
            num_scalar_prefetch=1,
            grid=(count,),
            in_specs=[pl.BlockSpec((rows, slabs, width), lambda i, d: (0, 0, d[i]))],
            out_specs=[
                pl.BlockSpec((1, slabs, width), lambda i, d: (i, 0, 0)),
                pl.BlockSpec((slabs, width), lambda i, d: (0, 0)),
            ]
            + specs,
        ),
    )(dests, jacobian)


def place(parts, count, scale, source, mean_row, near_ref, far_refs, half, scratch):
    near = parts - len(far_refs)
    for k in range(parts):
        x = near_ref[k] if k < near else far_refs[k - near][...]
        x = x.astype(F32)[half * count : (half + 1) * count]
        at = pl.multiple_of(source[k] * count, 8)
        scratch[pl.ds(at, count), :] = (x - mean_row) * scale


def early_kernel(parts, count, late_total, scale, source, near_ref, *refs):
    far_refs = refs[: parts // 2]
    mean_ref, extra_ref, c_ref, gram_ref, scratch = refs[parts // 2 :]
    step = pl.program_id(0)
    total = count * parts

    @pl.when(step == 0)
    def _():
        gram_ref[...] = jnp.zeros_like(gram_ref)
        gram_ref[total : total + EXTRA, :] = extra_ref[...]

    for half in range(2):
        mean_row = mean_ref[pl.ds(2 * step + half, 1), :]
        place(parts, count, scale, source, mean_row, near_ref, far_refs, half, scratch)
        c = scratch[...].astype(BF16)
        c_ref[half] = c
        gram_ref[:total, late_total:] += lax.dot_general(
            c, c, (((1,), (1,)), ((), ())), preferred_element_type=F32
        )


def late_kernel(parts, count, scale, source, near_ref, *refs):
    far_refs = refs[: parts // 2]
    mean_ref, c1_ref, c2_ref, gram_ref, scratch, total = refs[parts // 2 :]
    step = pl.program_id(0)

    @pl.when(step == 0)
    def _():
        total[...] = jnp.zeros_like(total)

    for half in range(2):
        mean_row = mean_ref[pl.ds(2 * step + half, 1), :]
        place(parts, count, scale, source, mean_row, near_ref, far_refs, half, scratch)
        c = scratch[...].astype(BF16)
        c2_ref[half] = c
        both = jnp.concatenate([c, c1_ref[half]], axis=0)
        total[...] += lax.dot_general(
            both, c, (((1,), (1,)), ((), ())), preferred_element_type=F32
        )

    @pl.when(step == pl.num_programs(0) - 1)
    def _():
        gram_ref[...] = total[...].T


def early_gram(near, far, source, mean, extra, count, late_total, scale):
    parts = 2 * len(far)
    slabs, width = mean.shape
    total = count * parts
    lanes = total + late_total
    return call(
        functools.partial(early_kernel, parts, count, late_total, scale),
        (
            jax.ShapeDtypeStruct((slabs, total, width), BF16),
            jax.ShapeDtypeStruct((total + EXTRA, lanes), F32),
        ),
        pltpu.PrefetchScalarGridSpec(
            num_scalar_prefetch=1,
            grid=(slabs // 2,),
            in_specs=[pl.BlockSpec((parts // 2, 2 * count, width), lambda i, s: (0, i, 0))]
            + [pl.BlockSpec((2 * count, width), lambda i, s: (i, 0))] * len(far)
            + [
                pl.BlockSpec((slabs, width), lambda i, s: (0, 0)),
                pl.BlockSpec((EXTRA, lanes), lambda i, s: (0, 0)),
            ],
            out_specs=[
                pl.BlockSpec((2, total, width), lambda i, s: (i, 0, 0)),
                pl.BlockSpec((total + EXTRA, lanes), lambda i, s: (0, 0)),
            ],
            scratch_shapes=[pltpu.VMEM((total, width), F32)],
        ),
    )(source, near, *far, mean, extra)


def late_gram(near, far, source, mean, c1, count, scale):
    parts = 2 * len(far)
    slabs, width = mean.shape
    total = count * parts
    first = c1.shape[1]
    lanes = total + first

    skip = (near.shape[1] - slabs * count) // (2 * count)
    return call(
        functools.partial(late_kernel, parts, count, scale),
        (
            jax.ShapeDtypeStruct((slabs, total, width), BF16),
            jax.ShapeDtypeStruct((total, lanes), F32),
        ),
        pltpu.PrefetchScalarGridSpec(
            num_scalar_prefetch=1,
            grid=(slabs // 2,),
            in_specs=[pl.BlockSpec((parts // 2, 2 * count, width), lambda i, s: (0, skip + i, 0))]
            + [pl.BlockSpec((2 * count, width), lambda i, s: (i, 0))] * len(far)
            + [
                pl.BlockSpec((slabs, width), lambda i, s: (0, 0)),
                pl.BlockSpec((2, first, width), lambda i, s: (i, 0, 0)),
            ],
            out_specs=[
                pl.BlockSpec((2, total, width), lambda i, s: (i, 0, 0)),
                pl.BlockSpec((total, lanes), lambda i, s: (0, 0)),
            ],
            scratch_shapes=[pltpu.VMEM((total, width), F32), pltpu.VMEM((lanes, total), F32)],
        ),
    )(source, near, *far, mean, c1)


def inverse_factor(block):
    size = block.shape[0]
    lane = lax.broadcasted_iota(jnp.int32, (8, 2 * size), 1)
    sub = lax.broadcasted_iota(jnp.int32, (8, 2 * size), 0)
    wide = jnp.concatenate([block, jnp.zeros_like(block)], axis=1)
    tiles = []
    for t in range(size // 8):
        unit = jnp.where(lane - size == sub + 8 * t, 1.0, 0.0)
        tiles.append(wide[8 * t : 8 * t + 8] + unit)
    for k in range(size):
        t, r = divmod(k, 8)
        row = tiles[t][r : r + 1]
        row = row * (1.0 / row[:, k : k + 1])
        for u in range(t, size // 8):
            column = tiles[u][:, k : k + 1]
            if u == t:
                column = jnp.where(sub[:, :1] > r, column, 0.0)
            tiles[u] = tiles[u] - column * row
    out = []
    for t in range(size // 8):
        pivot = jnp.sum(jnp.where(lane == sub + 8 * t, tiles[t], 0.0), axis=1, keepdims=True)
        out.append((tiles[t] * lax.rsqrt(pivot))[:, size:])
    return jnp.concatenate(out, axis=0)


def factor_kernel(total, late_total, samples, g_ref, x_ref, aux_ref, work):
    lanes = g_ref.shape[1]
    root = float(samples) ** 0.5
    e1 = g_ref[total : total + 8, :]
    energies = e1[0:1]
    mean = jnp.sum(energies, axis=1, keepdims=True) * (1.0 / samples)
    eps = (energies - mean) * (1.0 / root)
    shift = jnp.sum(e1[1:2], axis=1, keepdims=True) * (0.01 / samples / samples)
    n = total // BLOCK
    diag = lax.broadcasted_iota(jnp.int32, (BLOCK, BLOCK), 0) == lax.broadcasted_iota(
        jnp.int32, (BLOCK, BLOCK), 1
    )

    def start(i, j):
        block = g_ref[BLOCK * i : BLOCK * (i + 1), late_total + BLOCK * j : late_total + BLOCK * (j + 1)]
        return jnp.where(diag, block + shift, block) if i == j else block

    work[...] = jnp.zeros_like(work)
    low = {}
    inv = {}
    for j in range(n):
        for i in range(j, n):
            block = start(i, j)
            for k in range(j):
                block = block - mm(low[i, k], low[j, k], 1, 1)
            if i == j:
                inv[j, j] = inverse_factor(block)
            else:
                low[i, j] = mm(block, inv[j, j], 1, 1)
    for i in range(n):
        for j in range(i):
            total_ij = mm(low[i, j], inv[j, j], 1, 0)
            for k in range(j + 1, i):
                total_ij = total_ij + mm(low[i, k], inv[k, j], 1, 0)
            inv[i, j] = -mm(inv[i, i], total_ij, 1, 0)
        for j in range(i + 1):
            at = late_total + BLOCK * j
            work[late_total + BLOCK * i : late_total + BLOCK * (i + 1), at : at + BLOCK] = inv[i, j]
    x_ref[...] = work[...]
    eps_rows = jnp.broadcast_to(eps, (8, lanes))
    z = mm(eps_rows, work[...], 1, 1)
    sub = lax.broadcasted_iota(jnp.int32, (8, lanes), 0)
    aux_ref[...] = jnp.where(
        sub == 0, z, jnp.where(sub == 1, eps_rows, jnp.broadcast_to(shift, (8, lanes)))
    )


def factor(summed, total, late_total, samples):
    lanes = total + late_total
    return call(
        functools.partial(factor_kernel, total, late_total, samples),
        (
            jax.ShapeDtypeStruct((lanes, lanes), F32),
            jax.ShapeDtypeStruct((8, lanes), F32),
        ),
        scratch_shapes=[pltpu.VMEM((lanes, lanes), F32)],
    )(summed)


def solve_kernel(total, late_total, limit, p2_ref, g_ref, x_ref, aux_ref, out_ref):
    lanes = total + late_total
    strip = p2_ref[...]
    aux = aux_ref[...]
    shift = aux[2:3, :1]
    lane = lax.broadcasted_iota(jnp.int32, (late_total, lanes), 1)
    cross = jnp.where(lane >= late_total, strip, 0.0)
    inverse = x_ref[...]
    w = mm(cross, inverse, 1, 1)
    schur = strip[:, :late_total] - mm(w, w, 1, 1)
    n = late_total // BLOCK
    diag = lax.broadcasted_iota(jnp.int32, (BLOCK, BLOCK), 0) == lax.broadcasted_iota(
        jnp.int32, (BLOCK, BLOCK), 1
    )
    low = {}
    inv = {}
    for j in range(n):
        for i in range(j, n):
            block = schur[BLOCK * i : BLOCK * (i + 1), BLOCK * j : BLOCK * (j + 1)]
            for k in range(j):
                block = block - mm(low[i, k], low[j, k], 1, 1)
            if i == j:
                inv[j] = inverse_factor(jnp.where(diag, block + shift, block))
            else:
                low[i, j] = mm(block, inv[j], 1, 1)
    z_row = jnp.broadcast_to(aux[0:1], (8, lanes))
    rhs = jnp.broadcast_to(aux[1:2, :late_total], (8, late_total)) - mm(z_row, w, 1, 1)
    zs = []
    for i in range(n):
        block = rhs[:, BLOCK * i : BLOCK * (i + 1)]
        for k in range(i):
            block = block - mm(zs[k], low[i, k], 1, 1)
        zs.append(mm(block, inv[i], 1, 1))
    xs = [None] * n
    for i in reversed(range(n)):
        block = zs[i]
        for k in range(i + 1, n):
            block = block - mm(xs[k], low[k, i], 1, 0)
        xs[i] = mm(block, inv[i], 1, 0)
    x2 = jnp.concatenate(xs, axis=1) if n > 1 else xs[0]
    x1 = mm(z_row - mm(x2, w, 1, 0), inverse, 1, 0)
    x1_early = x1[:, late_total:]
    by_cross = mm(x2, cross, 1, 0) * 2.0
    early = mm(x1_early, g_ref[:total, :], 1, 0)
    late = mm(x2, strip[:, :late_total], 1, 0)
    size2 = jnp.sum((by_cross + early) * x1, axis=1, keepdims=True) + jnp.sum(
        late * x2, axis=1, keepdims=True
    )
    clip = jnp.minimum(1.0, limit / jnp.sqrt(jnp.maximum(size2, 0.0)))
    out_ref[...] = x1 * -clip
    out_ref[:, :late_total] = x2 * -clip


def solve(p2, summed, inverse, aux, total, late_total, limit):
    lanes = total + late_total
    return call(
        functools.partial(solve_kernel, total, late_total, limit),
        jax.ShapeDtypeStruct((8, lanes), F32),
    )(p2, summed, inverse, aux)


def update_kernel(late_total, x_ref, c1_ref, c2_ref, out_ref):
    x = x_ref[...]
    high = x.astype(BF16)
    rest = x - high.astype(F32)
    mid = rest.astype(BF16)
    low = (rest - mid.astype(F32)).astype(BF16)
    sub = lax.broadcasted_iota(jnp.int32, x.shape, 0)
    split = jnp.where(
        sub == 0, high.astype(F32), jnp.where(sub == 1, mid.astype(F32), low.astype(F32))
    )
    split = jnp.where(sub < 3, split, 0.0).astype(BF16)
    for half in range(c1_ref.shape[0]):
        both = jnp.concatenate([c2_ref[half], c1_ref[half]], axis=0)
        parts = jnp.dot(split, both, preferred_element_type=F32)
        out_ref[half : half + 1, :] = jnp.sum(parts, axis=0, keepdims=True)


def update(x, c1, c2):
    slabs, total, width = c1.shape
    late_total = c2.shape[1]
    lanes = total + late_total
    group = 8
    return call(
        functools.partial(update_kernel, late_total),
        jax.ShapeDtypeStruct((slabs, width), F32),
        pl.GridSpec(
            grid=(slabs // group,),
            in_specs=[
                pl.BlockSpec((8, lanes), lambda i: (0, 0)),
                pl.BlockSpec((group, total, width), lambda i: (i, 0, 0)),
                pl.BlockSpec((group, late_total, width), lambda i: (i, 0, 0)),
            ],
            out_specs=pl.BlockSpec((group, width), lambda i: (i, 0)),
        ),
    )(x, c1, c2)


def xor_pairs(size, bits):
    return [(i, i ^ bits) for i in range(size)]


SWAP = [(0, 1), (1, 0)]


def sum_smp_slab(a, parts):
    b = lax.ppermute(a, "smp", xor_pairs(parts, 1))
    c = lax.ppermute(a, "slab", SWAP)
    d = lax.ppermute(
        a, ("smp", "slab"), [(2 * i + j, 2 * (i ^ 1) + (1 - j)) for i in range(parts) for j in range(2)]
    )
    a = (a + b) + (c + d)
    bit = 2
    while bit < parts:
        b = lax.ppermute(a, "smp", xor_pairs(parts, bit))
        if 2 * bit < parts:
            c = lax.ppermute(a, "smp", xor_pairs(parts, 2 * bit))
            d = lax.ppermute(a, "smp", xor_pairs(parts, 3 * bit))
            a = (a + b) + (c + d)
        else:
            a = a + b
        bit *= 4
    return a


def sum_small(a, parts):
    return sum_smp_slab(a + lax.ppermute(a, "col", SWAP), parts)


def sum_large(a, parts, ties):
    half = a.shape[0] // 2
    core = lax.axis_index("col")
    rounds = [("slab", SWAP)]
    bit = 1
    while bit < parts:
        rounds.append(("smp", xor_pairs(parts, bit)))
        bit *= 2
    mine = lax.dynamic_slice_in_dim(a, core * half, half, 0)
    other = lax.dynamic_slice_in_dim(a, (1 - core) * half, half, 0)
    if ties[0]:
        other, _ = lax.optimization_barrier((other, ties[0]))
    mine = mine + lax.ppermute(other, "col", SWAP)
    for (axis, pairs), tie in zip(rounds, ties[1:]):
        if tie:
            mine, _ = lax.optimization_barrier((mine, tie))
        mine = mine + lax.ppermute(mine, axis, pairs)
    other = lax.ppermute(mine, "col", SWAP)
    first = jnp.where(core == 0, mine, other)
    second = jnp.where(core == 0, other, mine)
    return jnp.concatenate([first, second], axis=0)


def shards(parts, slab_parts, col_parts, jacobian, local_energy):
    rows, slabs, columns = jacobian.shape
    samples = rows * parts
    params = slabs * slab_parts * columns * col_parts
    late = rows // 4
    early = rows - late
    total, late_total = early * parts, late * parts
    scale = 1.0 / float(samples) ** 0.5
    me = lax.axis_index("smp")

    width = columns // parts
    far = list(range(parts // 2, parts))
    base = me - me % (parts // 2)
    halves = [list(range(parts // 2)), list(range(parts // 2, parts))]
    far_sums, far_spread, *far_rows = pack(jacobian, me ^ jnp.array(far, jnp.int32), width, early, True)
    members = base + jnp.arange(parts // 2, dtype=jnp.int32)
    near_sums, near_spread, near_rows = pack(jacobian, members, width, early, False)

    def send(k, a, after=None):
        if after is not None:
            a, _ = lax.optimization_barrier((a, after))
        return lax.ppermute(a, "smp", xor_pairs(parts, k))

    far1 = [send(k, far_rows[2 * i]) for i, k in enumerate(far)]
    near_got = lax.all_to_all(
        near_rows, "smp", split_axis=0, concat_axis=0, axis_index_groups=halves, tiled=True
    )

    sums = jnp.concatenate([near_sums, far_sums], axis=0)
    spread = jnp.sum(near_spread + far_spread)
    swaps = [(me >> b) & 1 for b in range(parts.bit_length() - 2)]
    sums = sums.reshape((2, parts // 2) + sums.shape[1:])
    for b, odd in enumerate(swaps):
        x = sums[0].reshape((parts // 2 >> (b + 1), 2, 1 << b) + sums.shape[2:])
        x = jnp.where(odd == 1, x[:, ::-1], x).reshape(sums.shape[1:])
        sums = jnp.stack([x, sums[1]])
    sums = sums.reshape((parts,) + sums.shape[2:])
    bit, count = 1, rows
    while bit < parts:
        pairs = sums.reshape((sums.shape[0] // 2, 2) + sums.shape[1:])
        mine, other = pairs[:, 0], send(bit, pairs[:, 1])
        gap = mine - other
        spread = spread + jnp.sum(gap * gap) * (0.5 / count)
        sums = mine + other
        bit, count = 2 * bit, 2 * count
    mean = sums[0] * (1.0 / samples)

    lead = jnp.logical_and(lax.axis_index("col") == 0, lax.axis_index("slab") == 0)
    energies = jnp.where(lead, local_energy, 0.0)
    row = lax.dynamic_update_slice(jnp.zeros((samples,), F32), energies[early:], (me * late,))
    row = lax.dynamic_update_slice(row, energies[:early], (late_total + me * early,))
    spread_row = jnp.where(jnp.arange(samples) == 0, spread, 0.0)
    extra = jnp.concatenate(
        [row[None], spread_row[None], jnp.zeros((EXTRA - 2, samples), F32)], axis=0
    )

    source = jnp.concatenate([members, me ^ jnp.array(far, jnp.int32)])
    c1, gram1 = early_gram(near_got, far1, source, mean, extra, early, late_total, scale)

    far2 = [send(k, far_rows[2 * i + 1], far1) for i, k in enumerate(far)]

    rounds = parts.bit_length() + 1
    ties = [[] for _ in range(rounds)]
    for i, block in enumerate(far2):
        ties[i * 4 // len(far2)].append(block)
    summed = sum_large(gram1, parts, ties)
    inverse, aux = factor(summed, total, late_total, samples)

    c1, aux = lax.optimization_barrier((c1, aux))
    c2, gram2 = late_gram(near_got, far2, source, mean, c1, late, scale)
    strip = sum_small(gram2, parts)
    limit = 0.3 * float(params) ** 0.5
    x = solve(strip, summed, inverse, aux, total, late_total, limit)
    return update(x, c1, c2)


def solution(mesh):
    body = functools.partial(shards, mesh.shape["smp"], mesh.shape["slab"], mesh.shape["col"])
    in_specs = (P("smp", "slab", "col"), P("smp"))
    out_specs = P("slab", ("col", "smp"))
    return jax.shard_map(body, mesh=mesh, in_specs=in_specs, out_specs=out_specs, check_vma=False)
```

time: 637 us -> 287 us (0.45); the launches traced: 629 us -> 286 us
  blocking collectives: 202 us -> 0 us
  local copies, waits for them, and re-layouts: 166 us -> 3.71 us
  other arithmetic: 73.1 us -> 7.62 us
  Pallas kernels: 0 us -> 62.5 us
  starting transfers between devices: 7.42 us -> 41.8 us
  waiting for transfers between devices: 136 us -> 167 us
  matrix products: 26.6 us -> 0 us
  between operations: 17.8 us -> 2.68 us
    ppermute x0 -> x24, waiting for transfers between devices: none -> 167 us  [the longest x11 141 us: send(): return lax.ppermute(a, 'smp', xor_pairs(parts, k))]
    unnamed x1 -> x0, blocking collectives: 162 us -> none
    unnamed x13 -> x10, local copies, waits for them, and re-layouts: 122 us -> 0.83 us
    psum x1 -> x0, waiting for transfers between devices: 118 us -> none  [shards(): gram = lax.psum(partial_gram, ('smp', 'col', 'slab'))]
    pallas_call x0 -> x7, Pallas kernels: none -> 62.5 us  [the longest x1 18.1 us: factor(): call(functools.partial(factor_kernel, total, late_total, samples), (jax.S...]
    another operation x9 -> x2, other arithmetic: 53.9 us -> 1.02 us  [the longest x1 1 us: shards(): sums = jnp.stack([x, sums[1]])]
    convert_element_type x1 -> x0, local copies, waits for them, and re-layouts: 39.4 us -> none  [shards(): values = columns.astype(jnp.float32)]
    psum x1 -> x0, blocking collectives: 39.4 us -> none  [shards(): squared = lax.psum(jnp.sum(delta * delta), ('smp', 'col', 'slab'))]
  transfers between devices with their start and end apart: 2 -> 25, of which waited for: 2 -> 15; matrix products, arithmetic and copies ran while one was open for 3% -> 4% of each run, Pallas kernels for 0% -> 6%
where the time goes in v1:
time: 287 us; the launch traced here: 286 us
  waiting for transfers between devices  167 us (58%)
  Pallas kernels  62.5 us (22%)
  starting transfers between devices  41.8 us (15%)
  other arithmetic  7.62 us (3%)
  local copies, waits for them, and re-layouts  3.71 us (1%)
    ppermute x11, waiting for transfers between devices, send(): return lax.ppermute(a, 'smp', xor_pairs(parts, k))  141 us
    ppermute x11, starting transfers between devices, send(): return lax.ppermute(a, 'smp', xor_pairs(parts, k))  20.2 us
    pallas_call x1, Pallas kernels, factor(): call(functools.partial(factor_kernel, total, late_total, samples), (jax.S...  18.1 us
    ppermute x4, waiting for transfers between devices, sum_large(): mine = mine + lax.ppermute(mine, axis, pairs)  15.8 us
    pallas_call x2, Pallas kernels, pack(): call(functools.partial(pack_kernel, early, apart), [pltpu.HBM((count, sla...  14.8 us
    pallas_call x1, Pallas kernels, early_gram(): call(functools.partial(early_kernel, parts, count, late_total, scale), (j...  10 us
    ppermute x4, starting transfers between devices, sum_large(): mine = mine + lax.ppermute(mine, axis, pairs)  8.89 us
    pallas_call x1, Pallas kernels, late_gram(): call(functools.partial(late_kernel, parts, count, scale), (jax.ShapeDtype...  8.08 us
  transfers between devices with their start and end apart: 25, of which 15 were waited for; matrix products, arithmetic and copies ran while one was open for 4% of the time, Pallas kernels for 6%

profile of v1, /device:TPU:0, one launch (start us, length us, event | category | flops | bytes accessed | tf_op | source)
XLA Modules:
  0.0 285.7 jit_solution(672905695649147610)
XLA Ops:
  0.0 6.9 %shard_map.46 = (f32[4,16,1024]{2,1,0:T(8,128)}, f32[16,1024]{1,0:T(8,128)}, bf16[4,512,1024]{2,1,0:T(8,128)(2,1)}) custom-call(s32[4]{0:T(128)S(1)} %iota_add_fusion.dest, bf16[32,16,8192]{2,1,0:T(8,128)(2,1)} %j_ref.3), custom_call_target="tpu_custom_call" | custom-call | tf_op jit(solution)/shard_map/pallas_call | solution.py:81
  6.9 5.4 %all-to-all-start = ((bf16[4,512,1024]{2,1,0:T(8,128)(2,1)}), bf16[4,512,1024]{2,1,0:T(8,128)(2,1)}, u32[]{:S(2)}, u32[]{:S(2)}) async-start(bf16[4,512,1024]{2,1,0:T(8,128)(2,1)} %get-tuple-element.34), calls=%async_computation | async-start | bytes 8388608 | tf_op jit(solution)/shard_map/all_to_all | solution.py:476
  12.2 7.9 %shard_map.47 = (f32[4,16,1024]{2,1,0:T(8,128)}, f32[16,1024]{1,0:T(8,128)}, bf16[384,1024]{1,0:T(8,128)(2,1)}, bf16[128,1024]{1,0:T(8,128)(2,1)}, bf16[384,1024...) custom-call(s32[4]{0:T(128)S(1)} %broadcast_xor_fusion.dest, ...), custom_call_target="tpu_custom_call" | custom-call | tf_op jit(solution)/shard_map/pallas_call | solution.py:81
  20.1 3.7 %collective-permute-start = (bf16[384,1024]{1,0:T(8,128)(2,1)}, bf16[384,1024]{1,0:T(8,128)(2,1)S(1)}, u32[]{:S(2)}, u32[]{:S(2)}) collective-permute-start(bf16[384,1024]{1,0:T(8,128)(2,1)} %get-tuple-element.36), channel_id=1, source_target_pairs={{0,16},{4,20},{8,24},{12,28},{16,0},{20,4},{24,8},{28,12},{1,17},{... | collective-permute-start | bytes 2359304 | tf_op jit(solution)/shard_map/ppermute | solution.py:473
  23.8 1.5 collective-permute-start.1
  25.3 3.8 %collective-permute-start.2 = (bf16[384,1024]{1,0:T(8,128)(2,1)}, bf16[384,1024]{1,0:T(8,128)(2,1)S(1)}, u32[]{:S(2)}, u32[]{:S(2)}) collective-permute-start(bf16[384,1024]{1,0:T(8,128)(2,1)} %get-tuple-element.38), channel_id=1, source_target_pairs={{0,24},{4,28},{8,16},{12,20},{16,8},{20,12},{24,0},{28,4},{1,25},{... | collective-permute-start | bytes 2359304 | tf_op jit(solution)/shard_map/ppermute | solution.py:473
  29.1 1.0 pad_maximum_fusion
  30.1 0.8 copy-done.1
  30.9 1.6 collective-permute-start.8
  32.5 0.6 slice_bitcast_fusion.7
  33.2 50.1 %collective-permute-done.8 = f32[4,16,1024]{2,1,0:T(8,128)} collective-permute-done((f32[4,16,1024]{2,1,0:T(8,128)S(1)}, f32[4,16,1024]{2,1,0:T(8,128)}, u32[]{:S(2)}, u32[]{:S(2)}) %collective-permute-start.8) | collective-permute-done | bytes 262176 | tf_op jit(solution)/shard_map/ppermute | solution.py:473
  83.3 1.7 multiply_reduce_fusion
  85.7 0.8 dynamic_update_slice.8
  86.4 0.8 dynamic_update_slice.9
  87.2 1.5 add_reduce_fusion
  88.8 42.0 %collective-permute-done.9 = f32[2,16,1024]{2,1,0:T(8,128)} collective-permute-done((f32[2,16,1024]{2,1,0:T(8,128)S(1)}, f32[2,16,1024]{2,1,0:T(8,128)}, u32[]{:S(2)}, u32[]{:S(2)}) %collective-permute-start.9) | collective-permute-done | bytes 131104 | tf_op jit(solution)/shard_map/ppermute | solution.py:473
  130.8 1.6 multiply_reduce_fusion.1
  132.3 3.1 %collective-permute-start.10 = (f32[1,16,1024]{2,1,0:T(8,128)S(1)}, f32[1,16,1024]{2,1,0:T(8,128)S(1)}, u32[]{:S(2)}, u32[]{:S(2)}) collective-permute-start(f32[1,16,1024]{2,1,0:T(8,128)S(1)} %slice_bitcast_fusion.4), channel_id=1, source_target_pairs={{0,16},{4,20},{8,24},{12,28},{16,0},{20,4},{24,8},{28,12},{1,17},{... | collective-permute-start | bytes 196616 | tf_op jit(solution)/shard_map/ppermute | solution.py:473
  137.3 25.1 %collective-permute-done.10 = f32[1,16,1024]{2,1,0:T(8,128)S(1)} collective-permute-done((f32[1,16,1024]{2,1,0:T(8,128)S(1)}, f32[1,16,1024]{2,1,0:T(8,128)S(1)}, u32[]{:S(2)}, u32[]{:S(2)}) %collective-permute-start.10) | collective-permute-done | bytes 65568 | tf_op jit(solution)/shard_map/ppermute | solution.py:473
  163.8 1.8 collective-permute-start.4
  165.6 10.0 %shard_map.48 = (bf16[16,192,1024]{2,1,0:T(8,128)(2,1)}, f32[208,256]{1,0:T(8,128)S(1)}) custom-call(s32[8]{0:T(128)S(1)} %pad_add_fusion.source, bf16[4,512,1024]{2,1,0:T(8,128)(2,1)} %all-to-all-done.near_ref, bf16[384,1024]{1,0:T(8,128)(2,1)S(1)} %collective-permute-done.refs_0_, bf16[384,1024]{1,0:T(8,128)(2,1)S(1)} %collective-permute-done.1.refs_1_, ...), custom_call_target="tpu_custom_call" | custom-call | tf_op jit(solution)/shard_map/pallas_call | solution.py:160
  175.7 2.1 collective-permute-done.4.refs_0_
  177.8 0.9 collective-permute-start.5
  178.7 3.6 %collective-permute-start.6 = (bf16[128,1024]{1,0:T(8,128)(2,1)}, bf16[128,1024]{1,0:T(8,128)(2,1)S(1)}, u32[]{:S(2)}, u32[]{:S(2)}) collective-permute-start(bf16[128,1024]{1,0:T(8,128)(2,1)} %get-tuple-element.44), channel_id=1, source_target_pairs={{0,24},{4,28},{8,16},{12,20},{16,8},{20,12},{24,0},{28,4},{1,25},{... | collective-permute-start | bytes 786440 | tf_op jit(solution)/shard_map/ppermute | solution.py:473
  182.5 0.9 dynamic-slice_add_fusion
  183.4 22.1 %collective-permute-done.5.refs_1_ = bf16[128,1024]{1,0:T(8,128)(2,1)S(1)} collective-permute-done((bf16[128,1024]{1,0:T(8,128)(2,1)}, bf16[128,1024]{1,0:T(8,128)(2,1)S(1)}, u32[]{:S(2)}, u32[]{:S(2)}) %collective-permute-start.5) | collective-permute-done | bytes 262176 | tf_op jit(solution)/shard_map/ppermute | solution.py:473
  205.5 1.4 collective-permute-start.12
  207.0 3.3 %collective-permute-done.12 = f32[104,256]{1,0:T(8,128)S(1)} collective-permute-done((f32[104,256]{1,0:T(8,128)S(1)}, f32[104,256]{1,0:T(8,128)S(1)}, u32[]{:S(2)}, u32[]{:S(2)}) %collective-permute-start.12) | collective-permute-done | bytes 106528 | tf_op jit(solution)/shard_map/ppermute | solution.py:445
  210.2 1.5 collective-permute-start.13
  211.8 3.2 %collective-permute-done.13 = f32[104,256]{1,0:T(8,128)S(1)} collective-permute-done((f32[104,256]{1,0:T(8,128)S(1)}, f32[104,256]{1,0:T(8,128)S(1)}, u32[]{:S(2)}, u32[]{:S(2)}) %collective-permute-start.13) | collective-permute-done | bytes 106528 | tf_op jit(solution)/shard_map/ppermute | solution.py:445
  215.0 4.5 %collective-permute-start.14 = (f32[104,256]{1,0:T(8,128)S(1)}, f32[104,256]{1,0:T(8,128)S(1)}, u32[]{:S(2)}, u32[]{:S(2)}) collective-permute-start(f32[104,256]{1,0:T(8,128)S(1)} %add.97), channel_id=1, source_target_pairs={{0,8},{4,12},{8,0},{12,4},{16,24},{20,28},{24,16},{28,20},{1,9},{5... | collective-permute-start | bytes 319496 | tf_op jit(solution)/shard_map/ppermute | solution.py:445
  219.5 3.2 %collective-permute-done.14 = f32[104,256]{1,0:T(8,128)S(1)} collective-permute-done((f32[104,256]{1,0:T(8,128)S(1)}, f32[104,256]{1,0:T(8,128)S(1)}, u32[]{:S(2)}, u32[]{:S(2)}) %collective-permute-start.14) | collective-permute-done | bytes 106528 | tf_op jit(solution)/shard_map/ppermute | solution.py:445
  222.7 1.5 collective-permute-start.15
  224.1 6.2 %collective-permute-done.15 = f32[104,256]{1,0:T(8,128)S(1)} collective-permute-done((f32[104,256]{1,0:T(8,128)S(1)}, f32[104,256]{1,0:T(8,128)S(1)}, u32[]{:S(2)}, u32[]{:S(2)}) %collective-permute-start.15) | collective-permute-done | bytes 106528 | tf_op jit(solution)/shard_map/ppermute | solution.py:445
  230.4 1.3 collective-permute-done.16
  231.7 18.1 %shard_map.49 = (f32[256,256]{1,0:T(8,128)S(1)}, f32[8,256]{1,0:T(8,128)S(1)}) custom-call(f32[208,256]{1,0:T(8,128)S(1)} %pad_maximum_fusion.1.g_ref), custom_call_target="tpu_custom_call" | custom-call | tf_op jit(solution)/shard_map/pallas_call | solution.py:290
  249.8 8.1 %shard_map.50 = (bf16[16,64,1024]{2,1,0:T(8,128)(2,1)S(1)}, f32[64,256]{1,0:T(8,128)S(1)}) custom-call(s32[8]{0:T(128)S(1)} %pad_add_fusion.source, bf16[4,512,1024]{2,1,0:T(8,128)(2,1)} %all-to-all-done.near_ref, bf16[128,1024]{1,0:T(8,128)(2,1)S(1)} %collective-permute-done.4.refs_0_, bf16[128,1024]{1,0:T(8,128)(2,1)S(1)} %collective-permute-done.5.refs_1_, ...), custom_call_target="tpu_custom_call" | custom-call | tf_op jit(solution)/shard_map/pallas_call | solution.py:192
  258.1 1.1 collective-permute-done.17
  259.3 1.4 collective-permute-start.19
  260.6 1.6 collective-permute-start.20
  262.2 0.6 collective-permute-start.18
  262.8 0.8 collective-permute-done.19
  263.6 2.9 %collective-permute-done.20 = f32[64,256]{1,0:T(8,128)S(1)} collective-permute-done((f32[64,256]{1,0:T(8,128)S(1)}, f32[64,256]{1,0:T(8,128)S(1)}, u32[]{:S(2)}, u32[]{:S(2)}) %collective-permute-start.20) | collective-permute-done | bytes 65568 | tf_op jit(solution)/shard_map/ppermute | solution.py:408
  266.6 2.3 collective-permute-start.23
  268.8 1.2 collective-permute-start.21
  270.0 3.7 %collective-permute-done.22 = f32[64,256]{1,0:T(8,128)S(1)} collective-permute-done((f32[64,256]{1,0:T(8,128)S(1)}, f32[64,256]{1,0:T(8,128)S(1)}, u32[]{:S(2)}, u32[]{:S(2)}) %collective-permute-start.22) | collective-permute-done | bytes 65568 | tf_op jit(solution)/shard_map/ppermute | solution.py:416
  274.2 7.4 %shard_map.51.x_ref = f32[8,256]{1,0:T(8,128)S(1)} custom-call(f32[64,256]{1,0:T(8,128)S(1)} %add_add_fusion.p2_ref, f32[208,256]{1,0:T(8,128)S(1)} %pad_maximum_fusion.1.g_ref, f32[256,256]{1,0:T(8,128)S(1)} %get-tuple-element.60.x_ref, f32[8,256]{1,0:T(8,128)S(1)} %get-tuple-element.61.aux_ref), custom_call_target="tpu_custom_call" | custom-call | tf_op jit(solution)/shard_map/pallas_call | solution.py:355
  281.6 4.2 %shard_map.52 = f32[16,1024]{1,0:T(8,128)} custom-call(f32[8,256]{1,0:T(8,128)S(1)} %shard_map.51.x_ref, bf16[16,192,1024]{2,1,0:T(8,128)(2,1)} %get-tuple-element.58.refs_5_.c1_ref, bf16[16,64,1024]{2,1,0:T(8,128)(2,1)S(1)} %get-tuple-element.62.c2_ref), custom_call_target="tpu_custom_call" | custom-call | tf_op jit(solution)/shard_map/pallas_call | solution.py:383
  (53 shorter events, 2.8 us)
Async XLA Ops:
  6.9 5.4 %copy-start.4 = (s32[4]{0:T(128)S(1)}, s32[4]{0:T(128)}, u32[]{:S(2)}) copy-start(s32[4]{0:T(128)} %constant.58.clone) | copy-start | bytes 52
  6.9 158.8 %all-to-all-start = ((bf16[4,512,1024]{2,1,0:T(8,128)(2,1)}), bf16[4,512,1024]{2,1,0:T(8,128)(2,1)}, u32[]{:S(2)}, u32[]{:S(2)}) async-start(bf16[4,512,1024]{2,1,0:T(8,128)(2,1)} %get-tuple-element.34), calls=%async_computation | async-start | bytes 8388608 | tf_op jit(solution)/shard_map/all_to_all | solution.py:476
  12.2 16.8 %copy-start.2 = (f32[4,16,1024]{2,1,0:T(8,128)S(1)}, f32[4,16,1024]{2,1,0:T(8,128)}, u32[]{:S(2)}) copy-start(f32[4,16,1024]{2,1,0:T(8,128)} %get-tuple-element.47) | copy-start | bytes 786436
  12.2 20.3 %copy-start.3 = (f32[32]{0:T(128)S(1)}, f32[32]{0:T(128)}, u32[]{:S(2)}) copy-start(f32[32]{0:T(128)} %param.5) | copy-start | bytes 388
  20.1 143.6 %collective-permute-start = (bf16[384,1024]{1,0:T(8,128)(2,1)}, bf16[384,1024]{1,0:T(8,128)(2,1)S(1)}, u32[]{:S(2)}, u32[]{:S(2)}) collective-permute-start(bf16[384,1024]{1,0:T(8,128)(2,1)} %get-tuple-element.36), channel_id=1, source_target_pairs={{0,16},{4,20},{8,24},{12,28},{16,0},{20,4},{24,8},{28,12},{1,17},{... | collective-permute-start | bytes 2359304 | tf_op jit(solution)/shard_map/ppermute | solution.py:473
  23.8 139.9 %collective-permute-start.1 = (bf16[384,1024]{1,0:T(8,128)(2,1)}, bf16[384,1024]{1,0:T(8,128)(2,1)S(1)}, u32[]{:S(2)}, u32[]{:S(2)}) collective-permute-start(bf16[384,1024]{1,0:T(8,128)(2,1)} %get-tuple-element.37), channel_id=1, source_target_pairs={{0,20},{4,16},{8,28},{12,24},{16,4},{20,0},{24,12},{28,8},{1,21},{... | collective-permute-start | bytes 2359304 | tf_op jit(solution)/shard_map/ppermute | solution.py:473
  25.3 138.5 %collective-permute-start.2 = (bf16[384,1024]{1,0:T(8,128)(2,1)}, bf16[384,1024]{1,0:T(8,128)(2,1)S(1)}, u32[]{:S(2)}, u32[]{:S(2)}) collective-permute-start(bf16[384,1024]{1,0:T(8,128)(2,1)} %get-tuple-element.38), channel_id=1, source_target_pairs={{0,24},{4,28},{8,16},{12,20},{16,8},{20,12},{24,0},{28,4},{1,25},{... | collective-permute-start | bytes 2359304 | tf_op jit(solution)/shard_map/ppermute | solution.py:473
  29.0 134.7 %collective-permute-start.3 = (bf16[384,1024]{1,0:T(8,128)(2,1)}, bf16[384,1024]{1,0:T(8,128)(2,1)S(1)}, u32[]{:S(2)}, u32[]{:S(2)}) collective-permute-start(bf16[384,1024]{1,0:T(8,128)(2,1)} %get-tuple-element.39), channel_id=1, source_target_pairs={{0,28},{4,24},{8,20},{12,16},{16,12},{20,8},{24,4},{28,0},{1,29},{... | collective-permute-start | bytes 2359304 | tf_op jit(solution)/shard_map/ppermute | solution.py:473
  30.1 0.8 copy-start.1
  30.9 52.3 %collective-permute-start.8 = (f32[4,16,1024]{2,1,0:T(8,128)S(1)}, f32[4,16,1024]{2,1,0:T(8,128)}, u32[]{:S(2)}, u32[]{:S(2)}) collective-permute-start(f32[4,16,1024]{2,1,0:T(8,128)S(1)} %slice_bitcast_fusion), channel_id=1, source_target_pairs={{0,4},{4,0},{8,12},{12,8},{16,20},{20,16},{24,28},{28,24},{1,5},{5... | collective-permute-start | bytes 786440 | tf_op jit(solution)/shard_map/ppermute | solution.py:473
  85.0 45.8 %collective-permute-start.9 = (f32[2,16,1024]{2,1,0:T(8,128)S(1)}, f32[2,16,1024]{2,1,0:T(8,128)}, u32[]{:S(2)}, u32[]{:S(2)}) collective-permute-start(f32[2,16,1024]{2,1,0:T(8,128)S(1)} %slice_bitcast_fusion.2), channel_id=1, source_target_pairs={{0,8},{4,12},{8,0},{12,4},{16,24},{20,28},{24,16},{28,20},{1,9},{5... | collective-permute-start | bytes 393224 | tf_op jit(solution)/shard_map/ppermute | solution.py:473
  132.3 30.1 %collective-permute-start.10 = (f32[1,16,1024]{2,1,0:T(8,128)S(1)}, f32[1,16,1024]{2,1,0:T(8,128)S(1)}, u32[]{:S(2)}, u32[]{:S(2)}) collective-permute-start(f32[1,16,1024]{2,1,0:T(8,128)S(1)} %slice_bitcast_fusion.4), channel_id=1, source_target_pairs={{0,16},{4,20},{8,24},{12,28},{16,0},{20,4},{24,8},{28,12},{1,17},{... | collective-permute-start | bytes 196616 | tf_op jit(solution)/shard_map/ppermute | solution.py:473
  163.8 14.0 %collective-permute-start.4 = (bf16[128,1024]{1,0:T(8,128)(2,1)}, bf16[128,1024]{1,0:T(8,128)(2,1)S(1)}, u32[]{:S(2)}, u32[]{:S(2)}) collective-permute-start(bf16[128,1024]{1,0:T(8,128)(2,1)} %get-tuple-element.40), channel_id=1, source_target_pairs={{0,16},{4,20},{8,24},{12,28},{16,0},{20,4},{24,8},{28,12},{1,17},{... | collective-permute-start | bytes 786440 | tf_op jit(solution)/shard_map/ppermute | solution.py:473
  175.7 2.1 copy-start
  177.8 4.7 %collective-permute-start.11 = (f32[104,256]{1,0:T(8,128)S(1)}, f32[104,256]{1,0:T(8,128)S(1)}, u32[]{:S(2)}, u32[]{:S(2)}) collective-permute-start(f32[104,256]{1,0:T(8,128)S(1)} %constant_dynamic-slice_fusion), channel_id=1, source_target_pairs={{0,2},{2,0},{1,3},{3,1},{4,6},{6,4},{5,7},{7,5},{8,10},{10,8},{9,1... | collective-permute-start | bytes 319496 | tf_op jit(solution)/shard_map/ppermute | solution.py:441
  177.8 27.8 %collective-permute-start.5 = (bf16[128,1024]{1,0:T(8,128)(2,1)}, bf16[128,1024]{1,0:T(8,128)(2,1)S(1)}, u32[]{:S(2)}, u32[]{:S(2)}) collective-permute-start(bf16[128,1024]{1,0:T(8,128)(2,1)} %get-tuple-element.42), channel_id=1, source_target_pairs={{0,20},{4,16},{8,28},{12,24},{16,4},{20,0},{24,12},{28,8},{1,21},{... | collective-permute-start | bytes 786440 | tf_op jit(solution)/shard_map/ppermute | solution.py:473
  178.7 31.6 %collective-permute-start.6 = (bf16[128,1024]{1,0:T(8,128)(2,1)}, bf16[128,1024]{1,0:T(8,128)(2,1)S(1)}, u32[]{:S(2)}, u32[]{:S(2)}) collective-permute-start(bf16[128,1024]{1,0:T(8,128)(2,1)} %get-tuple-element.44), channel_id=1, source_target_pairs={{0,24},{4,28},{8,16},{12,20},{16,8},{20,12},{24,0},{28,4},{1,25},{... | collective-permute-start | bytes 786440 | tf_op jit(solution)/shard_map/ppermute | solution.py:473
  182.3 32.8 %collective-permute-start.7 = (bf16[128,1024]{1,0:T(8,128)(2,1)}, bf16[128,1024]{1,0:T(8,128)(2,1)S(1)}, u32[]{:S(2)}, u32[]{:S(2)}) collective-permute-start(bf16[128,1024]{1,0:T(8,128)(2,1)} %get-tuple-element.46), channel_id=1, source_target_pairs={{0,28},{4,24},{8,20},{12,16},{16,12},{20,8},{24,4},{28,0},{1,29},{... | collective-permute-start | bytes 786440 | tf_op jit(solution)/shard_map/ppermute | solution.py:473
  205.5 4.7 %collective-permute-start.12 = (f32[104,256]{1,0:T(8,128)S(1)}, f32[104,256]{1,0:T(8,128)S(1)}, u32[]{:S(2)}, u32[]{:S(2)}) collective-permute-start(f32[104,256]{1,0:T(8,128)S(1)} %dynamic-slice_add_fusion), channel_id=1, source_target_pairs={{0,1},{1,0},{2,3},{3,2},{4,5},{5,4},{6,7},{7,6},{8,9},{9,8},{10,11... | collective-permute-start | bytes 319496 | tf_op jit(solution)/shard_map/ppermute | solution.py:445
  210.2 4.8 %collective-permute-start.13 = (f32[104,256]{1,0:T(8,128)S(1)}, f32[104,256]{1,0:T(8,128)S(1)}, u32[]{:S(2)}, u32[]{:S(2)}) collective-permute-start(f32[104,256]{1,0:T(8,128)S(1)} %add.96), channel_id=1, source_target_pairs={{0,4},{4,0},{8,12},{12,8},{16,20},{20,16},{24,28},{28,24},{1,5},{5... | collective-permute-start | bytes 319496 | tf_op jit(solution)/shard_map/ppermute | solution.py:445
  215.0 7.6 %collective-permute-start.14 = (f32[104,256]{1,0:T(8,128)S(1)}, f32[104,256]{1,0:T(8,128)S(1)}, u32[]{:S(2)}, u32[]{:S(2)}) collective-permute-start(f32[104,256]{1,0:T(8,128)S(1)} %add.97), channel_id=1, source_target_pairs={{0,8},{4,12},{8,0},{12,4},{16,24},{20,28},{24,16},{28,20},{1,9},{5... | collective-permute-start | bytes 319496 | tf_op jit(solution)/shard_map/ppermute | solution.py:445
  222.7 7.6 %collective-permute-start.15 = (f32[104,256]{1,0:T(8,128)S(1)}, f32[104,256]{1,0:T(8,128)S(1)}, u32[]{:S(2)}, u32[]{:S(2)}) collective-permute-start(f32[104,256]{1,0:T(8,128)S(1)} %add.98), channel_id=1, source_target_pairs={{0,16},{4,20},{8,24},{12,28},{16,0},{20,4},{24,8},{28,12},{1,17},{... | collective-permute-start | bytes 319496 | tf_op jit(solution)/shard_map/ppermute | solution.py:445
  230.3 1.4 collective-permute-start.16
  257.9 1.3 collective-permute-start.17
  259.3 4.3 %collective-permute-start.19 = (f32[64,256]{1,0:T(8,128)S(1)}, f32[64,256]{1,0:T(8,128)S(1)}, u32[]{:S(2)}, u32[]{:S(2)}) collective-permute-start(f32[64,256]{1,0:T(8,128)S(1)} %add.100), channel_id=1, source_target_pairs={{0,1},{1,0},{2,3},{3,2},{4,5},{5,4},{6,7},{7,6},{8,9},{9,8},{10,11... | collective-permute-start | bytes 196616 | tf_op jit(solution)/shard_map/ppermute | solution.py:407
  260.6 5.8 %collective-permute-start.20 = (f32[64,256]{1,0:T(8,128)S(1)}, f32[64,256]{1,0:T(8,128)S(1)}, u32[]{:S(2)}, u32[]{:S(2)}) collective-permute-start(f32[64,256]{1,0:T(8,128)S(1)} %add.100), channel_id=1, source_target_pairs={{0,5},{1,4},{4,1},{5,0},{8,13},{9,12},{12,9},{13,8},{16,21},{17,20... | collective-permute-start | bytes 196616 | tf_op jit(solution)/shard_map/ppermute | solution.py:408
  262.2 4.3 %collective-permute-start.18 = (f32[64,256]{1,0:T(8,128)S(1)}, f32[64,256]{1,0:T(8,128)S(1)}, u32[]{:S(2)}, u32[]{:S(2)}) collective-permute-start(f32[64,256]{1,0:T(8,128)S(1)} %add.100), channel_id=1, source_target_pairs={{0,4},{4,0},{8,12},{12,8},{16,20},{20,16},{24,28},{28,24},{1,5},{5... | collective-permute-start | bytes 196616 | tf_op jit(solution)/shard_map/ppermute | solution.py:406
  266.5 7.2 %collective-permute-start.22 = (f32[64,256]{1,0:T(8,128)S(1)}, f32[64,256]{1,0:T(8,128)S(1)}, u32[]{:S(2)}, u32[]{:S(2)}) collective-permute-start(f32[64,256]{1,0:T(8,128)S(1)} %add_add_fusion.1), channel_id=1, source_target_pairs={{0,16},{4,20},{8,24},{12,28},{16,0},{20,4},{24,8},{28,12},{1,17},{... | collective-permute-start | bytes 196616 | tf_op jit(solution)/shard_map/ppermute | solution.py:416
  266.6 7.2 %collective-permute-start.23 = (f32[64,256]{1,0:T(8,128)S(1)}, f32[64,256]{1,0:T(8,128)S(1)}, u32[]{:S(2)}, u32[]{:S(2)}) collective-permute-start(f32[64,256]{1,0:T(8,128)S(1)} %add_add_fusion.1), channel_id=1, source_target_pairs={{0,24},{4,28},{8,16},{12,20},{16,8},{20,12},{24,0},{28,4},{1,25},{... | collective-permute-start | bytes 196616 | tf_op jit(solution)/shard_map/ppermute | solution.py:417
  268.8 5.4 %collective-permute-start.21 = (f32[64,256]{1,0:T(8,128)S(1)}, f32[64,256]{1,0:T(8,128)S(1)}, u32[]{:S(2)}, u32[]{:S(2)}) collective-permute-start(f32[64,256]{1,0:T(8,128)S(1)} %add_add_fusion.1), channel_id=1, source_target_pairs={{0,8},{4,12},{8,0},{12,4},{16,24},{20,28},{24,16},{28,20},{1,9},{5... | collective-permute-start | bytes 196616 | tf_op jit(solution)/shard_map/ppermute | solution.py:414

commit v2 on v0

v2 whole, which is shorter than its diff:
```python
import functools

import jax
import jax.numpy as jnp
from jax import lax
from jax.experimental import pallas as pl
from jax.experimental.pallas import tpu as pltpu
from jax.sharding import PartitionSpec as P

BLOCK = 64
LANES = 128
EXTRA = 16
CHUNK = 256
F32 = jnp.float32
BF16 = jnp.bfloat16
HIGHEST = lax.Precision.HIGHEST
MIB = 1024 * 1024
SWAP = [(0, 1), (1, 0)]


def mm(a, b, ca, cb):
    return lax.dot_general(
        a, b, (((ca,), (cb,)), ((), ())), precision=HIGHEST, preferred_element_type=F32
    )


def products(a, b):
    return lax.dot_general(a, b, (((1,), (1,)), ((), ())), preferred_element_type=F32)


def call(kernel, out_shape, grid_spec=None, vmem=58, **kw):
    if grid_spec is not None:
        kw["grid_spec"] = grid_spec
    return pl.pallas_call(
        kernel,
        out_shape=out_shape,
        compiler_params=pltpu.CompilerParams(vmem_limit_bytes=vmem * MIB),
        cost_estimate=pl.CostEstimate(flops=0, bytes_accessed=0, transcendentals=0),
        **kw,
    )


def lane_chunks(width):
    size = min(CHUNK, width)
    return [slice(c, c + size) for c in range(0, width, size)]


def pack_kernel(far_count, dest, j_ref, near_ref, *refs):
    far_refs, (buffer, out, in_sems, out_sems) = refs[:far_count], refs[far_count:]
    step = pl.program_id(0)
    count, rows, slabs, width = buffer.shape

    def read(k):
        columns = pl.ds(pl.multiple_of(dest[k] * width, LANES), width)
        return pltpu.make_async_copy(j_ref.at[:, :, columns], buffer.at[k], in_sems.at[k])

    def write(k):
        target = far_refs[k] if k < far_count else near_ref.at[k - far_count]
        return pltpu.make_async_copy(out.at[k], target, out_sems.at[k])

    @pl.when(step == 0)
    def _():
        for k in range(count):
            read(k).start()

    read(step).wait()
    for part in lane_chunks(width):
        x = jnp.swapaxes(buffer[step, :, :, part].astype(F32), 0, 1)
        out[step, :, part] = x.reshape(slabs * rows, x.shape[2]).astype(BF16)
    for k in range(count):

        @pl.when(step == k)
        def _():
            write(k).start()

    @pl.when(step == count - 1)
    def _():
        for k in range(count):
            write(k).wait()


def pack(jacobian, dests, width):
    rows, slabs, _ = jacobian.shape
    count = dests.shape[0]
    far_count = count // 2
    height = slabs * rows
    return call(
        functools.partial(pack_kernel, far_count),
        [pltpu.HBM((far_count, height, width), BF16)]
        + [pltpu.HBM((height, width), BF16)] * far_count,
        pltpu.PrefetchScalarGridSpec(
            num_scalar_prefetch=1,
            grid=(count,),
            in_specs=[pl.BlockSpec(memory_space=pl.ANY)],
            out_specs=[pl.BlockSpec(memory_space=pl.ANY)] * (1 + far_count),
            scratch_shapes=[
                pltpu.VMEM((count, rows, slabs, width), BF16),
                pltpu.VMEM((count, height, width), BF16),
                pltpu.SemaphoreType.DMA((count,)),
                pltpu.SemaphoreType.DMA((count,)),
            ],
        ),
    )(dests, jacobian)


def near_kernel(rows, near_ref, c_ref, base_ref, gram_ref):
    step = pl.program_id(0)
    parts, height, width = near_ref.shape
    total = parts * rows

    @pl.when(step == 0)
    def _():
        gram_ref[...] = jnp.zeros_like(gram_ref)

    for half in range(height // rows):
        slab = pl.ds(half * rows, rows)
        for part in lane_chunks(width):
            sums = 0.0
            for k in range(parts):
                sums = sums + jnp.sum(near_ref[k, slab, part].astype(F32), axis=0, keepdims=True)
            base = sums * (1.0 / total)
            base_ref[half, :, part] = base
            for k in range(parts):
                x = near_ref[k, slab, part].astype(F32) - base
                c_ref[half, k * rows : (k + 1) * rows, part] = x.astype(BF16)
        c = c_ref[half]
        gram_ref[...] += products(c, c)


def near_products(near, slabs):
    parts, height, width = near.shape
    rows = height // slabs
    total = parts * rows
    group = 2
    return call(
        functools.partial(near_kernel, rows),
        (
            jax.ShapeDtypeStruct((slabs, total, width), BF16),
            jax.ShapeDtypeStruct((slabs, 1, width), F32),
            jax.ShapeDtypeStruct((total, total), F32),
        ),
        pl.GridSpec(
            grid=(slabs // group,),
            in_specs=[pl.BlockSpec((parts, group * rows, width), lambda i: (0, i, 0))],
            out_specs=[
                pl.BlockSpec((group, total, width), lambda i: (i, 0, 0)),
                pl.BlockSpec((group, 1, width), lambda i: (i, 0, 0)),
                pl.BlockSpec((total, total), lambda i: (0, 0)),
            ],
        ),
    )(near)


def far_kernel(rows, place, *refs):
    far_count = len(refs) - 12
    far_refs = refs[:far_count]
    cn_ref, base_ref, near_ref, extra_ref, cf_ref, mine_ref, other_ref, blocks, near, gram, acc, sems = refs[
        far_count:
    ]
    step = pl.program_id(0)
    steps = pl.num_programs(0)
    group, total, width = cf_ref.shape

    def copies(i):
        span = pl.ds(pl.multiple_of(i * group * rows, 16), group * rows)
        return [
            pltpu.make_async_copy(far_refs[k].at[span, :], blocks.at[i, place[k]], sems.at[i, k])
            for k in range(far_count)
        ] + [pltpu.make_async_copy(cn_ref.at[pl.ds(i * group, group)], near.at[i], sems.at[i, far_count])]

    @pl.when(step == 0)
    def _():
        acc[...] = jnp.zeros_like(acc)

        @pl.loop(0, steps)
        def _(i):
            for c in copies(i):
                c.start()

    for c in copies(step):
        c.wait()
    for half in range(group):
        for part in lane_chunks(width):
            base = base_ref[half, :, part]
            for k in range(far_count):
                x = blocks[step, k, half * rows : (half + 1) * rows, part].astype(F32) - base
                cf_ref[half, k * rows : (k + 1) * rows, part] = x.astype(BF16)
        c = cf_ref[half]
        acc[:total, :] += products(near[step, half], c)
        acc[total:, :] += products(c, c)

    @pl.when(step == steps - 1)
    def _():
        low = place[far_count] == 0
        cross, far, near_gram = acc[:total, :], acc[total:, :], near_ref[...]
        gram[:total, :] = jnp.where(low, near_gram, far)
        gram[total : 2 * total, :] = jnp.where(low, far, near_gram)
        gram[2 * total : 3 * total, :] = jnp.where(low, cross, cross.T)
        gram[3 * total :, :] = extra_ref[...]
        count = mine_ref.shape[0]
        core = place[far_count + 1]
        mine_ref[...] = gram[pl.ds(pl.multiple_of(core * count, 8), count), :]
        other_ref[...] = gram[pl.ds(pl.multiple_of((1 - core) * count, 8), count), :]


def far_products(far_blocks, place, cn, base, near_gram, extra):
    slabs, total, width = cn.shape
    far_count = len(far_blocks)
    rows = total // far_count
    group = 2
    steps = slabs // group
    height = 3 * total + EXTRA
    share = jax.ShapeDtypeStruct((height // 2, total), F32)
    return call(
        functools.partial(far_kernel, rows),
        (jax.ShapeDtypeStruct((slabs, total, width), BF16), share, share),
        pltpu.PrefetchScalarGridSpec(
            num_scalar_prefetch=1,
            grid=(steps,),
            in_specs=[pl.BlockSpec(memory_space=pl.ANY)] * (far_count + 1)
            + [
                pl.BlockSpec((group, 1, width), lambda i, s: (i, 0, 0)),
                pl.BlockSpec((total, total), lambda i, s: (0, 0)),
                pl.BlockSpec((EXTRA, total), lambda i, s: (0, 0)),
            ],
            out_specs=[
                pl.BlockSpec((group, total, width), lambda i, s: (i, 0, 0)),
                pl.BlockSpec(share.shape, lambda i, s: (0, 0)),
                pl.BlockSpec(share.shape, lambda i, s: (0, 0)),
            ],
            scratch_shapes=[
                pltpu.VMEM((steps, far_count, group * rows, width), BF16),
                pltpu.VMEM((steps, group, total, width), BF16),
                pltpu.VMEM((height, total), F32),
                pltpu.VMEM((2 * total, total), F32),
                pltpu.SemaphoreType.DMA((steps, far_count + 1)),
            ],
        ),
    )(place, *far_blocks, cn, base, near_gram, extra)


def inverse(block):
    size = block.shape[0]
    shape = (8, 2 * size)
    lane = lax.broadcasted_iota(jnp.int32, shape, 1)
    sub = lax.broadcasted_iota(jnp.int32, shape, 0)
    wide = jnp.concatenate([block, jnp.zeros_like(block)], axis=1)
    count = size // 8
    tiles = [
        wide[8 * t : 8 * t + 8] + jnp.where(lane - size == sub + 8 * t, 1.0, 0.0) for t in range(count)
    ]
    scaled = []

    def pair(c0, c1, at):
        a, b, c = c0[0][at : at + 1], c1[0][at : at + 1], c1[0][at + 1 : at + 2]
        d = 1.0 / (a * c - b * b)
        a, b, c = a * d, b * d, c * d
        g0 = [x * c - y * b for x, y in zip(c0, c1)]
        g1 = [y * a - x * b for x, y in zip(c0, c1)]
        g0[0] = jnp.where(sub > at + 1, g0[0], 0.0)
        g1[0] = jnp.where(sub > at + 1, g1[0], 0.0)
        return g0, g1, (a, b, c)

    for t in range(count):
        normal = jnp.zeros(shape, F32)
        for r in (0, 4):
            k = 8 * t + r
            live = tiles[t:]
            cols = [[jnp.broadcast_to(x[:, k + j : k + j + 1], shape) for x in live] for j in range(4)]
            g0, g1, p = pair(cols[0], cols[1], r)
            r0, r1 = live[0][r : r + 1], live[0][r + 1 : r + 2]
            rest = []
            for j in (2, 3):
                u0, u1 = cols[j][0][r : r + 1], cols[j][0][r + 1 : r + 2]
                rest.append([x - (y * u0 + z * u1) for x, y, z in zip(cols[j], g0, g1)])
            live = [x - (y * r0 + z * r1) for x, y, z in zip(live, g0, g1)]
            h0, h1, q = pair(rest[0], rest[1], r + 2)
            r2, r3 = live[0][r + 2 : r + 3], live[0][r + 3 : r + 4]
            tiles[t:] = [x - (y * r2 + z * r3) for x, y, z in zip(live, h0, h1)]
            for at, (x, y), (a, b, c) in ((r, (r0, r1), p), (r + 2, (r2, r3), q)):
                normal = jnp.where(sub == at, x * c - y * b, normal)
                normal = jnp.where(sub == at + 1, y * a - x * b, normal)
        scaled.append(normal)
    w = jnp.concatenate(tiles, axis=0)[:, size:]
    n = jnp.concatenate(scaled, axis=0)[:, size:]
    return mm(w, n, 0, 0)


def solve_kernel(limit, core, mine_ref, other_ref, x_ref, sums, gram):
    count = mine_ref.shape[0]
    sums[pl.ds(pl.multiple_of(core[0] * count, 8), count), :] = mine_ref[...]
    sums[pl.ds(pl.multiple_of((1 - core[0]) * count, 8), count), :] = other_ref[...]
    half = sums.shape[1]
    samples = 2 * half
    low, high = sums[:half, :], sums[half : 2 * half, :]
    cross = sums[2 * half : 3 * half, :]
    turned = cross.T
    inv = 1.0 / samples
    col_low = (jnp.sum(low, axis=1, keepdims=True) + jnp.sum(cross, axis=1, keepdims=True)) * inv
    col_high = (jnp.sum(high, axis=1, keepdims=True) + jnp.sum(turned, axis=1, keepdims=True)) * inv
    row_low = (jnp.sum(low, axis=0, keepdims=True) + jnp.sum(turned, axis=0, keepdims=True)) * inv
    row_high = (jnp.sum(high, axis=0, keepdims=True) + jnp.sum(cross, axis=0, keepdims=True)) * inv
    mean = (jnp.sum(row_low, axis=1, keepdims=True) + jnp.sum(row_high, axis=1, keepdims=True)) * inv
    gram[:half, :half] = (low - col_low - row_low + mean) * inv
    gram[half:, half:] = (high - col_high - row_high + mean) * inv
    gram[half:, :half] = (turned - col_high - row_low + mean) * inv
    gram[:half, half:] = (cross - col_low - row_high + mean) * inv
    n = samples // BLOCK
    spans = [slice(BLOCK * i, BLOCK * (i + 1)) for i in range(n)]
    on = lax.broadcasted_iota(jnp.int32, (BLOCK, BLOCK), 0) == lax.broadcasted_iota(
        jnp.int32, (BLOCK, BLOCK), 1
    )
    diagonal = sum(jnp.where(on, gram[s, s], 0.0) for s in spans)
    diagonal = jnp.sum(diagonal, axis=0, keepdims=True)
    shift = jnp.sum(diagonal, axis=1, keepdims=True) * (0.01 * inv)

    e = sums[3 * half : 3 * half + 8, :]
    energies = jnp.concatenate([e[0:1], e[1:2]], axis=1)
    center = jnp.sum(energies, axis=1, keepdims=True) * inv
    eps = jnp.broadcast_to((energies - center) * (inv**0.5), (8, samples))

    left, factor, solved = {}, {}, []
    for j in range(n):
        for i in range(j, n):
            block = gram[spans[i], spans[j]]
            if i == j:
                block = jnp.where(on, block + shift, block)
            for k in range(j):
                block = block - mm(factor[i, k], left[j, k], 1, 1)
            left[i, j] = block
        diag = inverse(left[j, j])
        for i in range(j + 1, n):
            factor[i, j] = mm(left[i, j], diag, 1, 0)
        z = eps[:, spans[j]]
        for k in range(j):
            z = z - mm(solved[k][0], factor[j, k], 1, 1)
        solved.append((z, mm(z, diag, 1, 0)))
    xs = [w for _, w in solved]
    for i in reversed(range(n)):
        for j in range(i):
            xs[j] = xs[j] - mm(xs[i], factor[i, j], 1, 0)
    x = jnp.concatenate(xs, axis=1)
    x = x - jnp.sum(x, axis=1, keepdims=True) * inv
    size = jnp.sum(mm(x, gram[...], 1, 0) * x, axis=1, keepdims=True)
    clip = jnp.minimum(1.0, limit / jnp.sqrt(jnp.maximum(size, 0.0)))
    x_ref[...] = x * (clip * -(inv**0.5))


def solve(core, mine, other, limit):
    count, half = mine.shape
    samples = 2 * half
    return call(
        functools.partial(solve_kernel, limit),
        jax.ShapeDtypeStruct((8, samples), F32),
        pltpu.PrefetchScalarGridSpec(
            num_scalar_prefetch=1,
            grid=(1,),
            in_specs=[pl.BlockSpec((count, half), lambda i, s: (0, 0))] * 2,
            out_specs=pl.BlockSpec((8, samples), lambda i, s: (0, 0)),
            scratch_shapes=[
                pltpu.VMEM((2 * count, half), F32),
                pltpu.VMEM((samples, samples), F32),
            ],
        ),
    )(core, mine, other)


def update_kernel(high, x_ref, cn_ref, cf_ref, out_ref):
    total = cn_ref.shape[1]
    sub = lax.broadcasted_iota(jnp.int32, (8, total), 0)

    def split(x):
        first = x.astype(BF16).astype(F32)
        rest = x - first
        second = rest.astype(BF16).astype(F32)
        third = rest - second
        x = jnp.where(sub == 0, first, jnp.where(sub == 1, second, third))
        return jnp.where(sub < 3, x, 0.0).astype(BF16)

    low, up = split(x_ref[:, :total]), split(x_ref[:, total:])
    near = jnp.where(high[0] == 1, up.astype(F32), low.astype(F32)).astype(BF16)
    far = jnp.where(high[0] == 1, low.astype(F32), up.astype(F32)).astype(BF16)
    step = pl.program_id(0)
    group = cn_ref.shape[0]
    for slab in range(group):
        y = jnp.dot(near, cn_ref[slab], preferred_element_type=F32)
        y = y + jnp.dot(far, cf_ref[slab], preferred_element_type=F32)
        out_ref[pl.ds(step * group + slab, 1), :] = jnp.sum(y, axis=0, keepdims=True)


def update(x, high, cn, cf):
    slabs, total, width = cn.shape
    group = 4
    return call(
        update_kernel,
        jax.ShapeDtypeStruct((slabs, width), F32),
        pltpu.PrefetchScalarGridSpec(
            num_scalar_prefetch=1,
            grid=(slabs // group,),
            in_specs=[
                pl.BlockSpec((8, 2 * total), lambda i, s: (0, 0)),
                pl.BlockSpec((group, total, width), lambda i, s: (i, 0, 0)),
                pl.BlockSpec((group, total, width), lambda i, s: (i, 0, 0)),
            ],
            out_specs=pl.BlockSpec((slabs, width), lambda i, s: (0, 0)),
        ),
    )(high, x, cn, cf)


def xor_pairs(size, bits):
    return [(i, i ^ bits) for i in range(size)]


def sum_all(mine, other, parts):
    mine = mine + lax.ppermute(other, "col", SWAP)
    mine = mine + lax.ppermute(mine, "slab", SWAP)
    bit = 1
    while bit < parts:
        mine = mine + lax.ppermute(mine, "smp", xor_pairs(parts, bit))
        bit *= 2
    return mine, lax.ppermute(mine, "col", SWAP)


def shards(parts, slab_parts, col_parts, jacobian, local_energy):
    rows, slabs, columns = jacobian.shape
    params = slabs * slab_parts * columns * col_parts
    half = rows * parts // 2
    me = lax.axis_index("smp")
    count = parts // 2
    far = list(range(count, parts))
    high = me // count
    distance = jnp.arange(count, dtype=jnp.int32)
    partners = me ^ (distance + count)
    members = high * count + distance

    near_rows, *far_rows = pack(jacobian, jnp.concatenate([partners, members]), columns // parts)
    near = lax.all_to_all(
        near_rows,
        "smp",
        split_axis=0,
        concat_axis=0,
        axis_index_groups=[list(range(count)), far],
        tiled=True,
    )
    far_blocks = [lax.ppermute(r, "smp", xor_pairs(parts, k)) for k, r in zip(far, far_rows)]

    lead = jnp.logical_and(lax.axis_index("col") == 0, lax.axis_index("slab") == 0)
    energies = jnp.where(lead, local_energy, 0.0)[None]
    extra = lax.dynamic_update_slice(
        jnp.zeros((EXTRA, half), F32), energies, (high, (me % count) * rows)
    )

    cn, base, near_gram = near_products(near, slabs)
    core = lax.axis_index("col")[None]
    place = jnp.concatenate([partners % count, high[None], core])
    cf, mine, other = far_products(far_blocks, place, cn, base, near_gram, extra)
    mine, other = sum_all(mine, other, parts)
    x = solve(core, mine, other, 0.3 * float(params) ** 0.5)
    return update(x, high[None], cn, cf)


def solution(mesh):
    body = functools.partial(shards, mesh.shape["smp"], mesh.shape["slab"], mesh.shape["col"])
    in_specs = (P("smp", "slab", "col"), P("smp"))
    out_specs = P("slab", ("col", "smp"))
    return jax.shard_map(body, mesh=mesh, in_specs=in_specs, out_specs=out_specs, check_vma=False)
```

time: 637 us -> 257 us (0.40); the launches traced: 629 us -> 256 us
  blocking collectives: 202 us -> 0 us
  local copies, waits for them, and re-layouts: 166 us -> 2.16 us
  other arithmetic: 73.1 us -> 2.23 us
  starting transfers between devices: 7.42 us -> 64.3 us
  Pallas kernels: 0 us -> 45.8 us
  matrix products: 26.6 us -> 0 us
  between operations: 17.8 us -> 0.14 us
    unnamed x1 -> x0, blocking collectives: 162 us -> none
    unnamed x13 -> x14, local copies, waits for them, and re-layouts: 122 us -> 1.97 us
    psum x1 -> x0, waiting for transfers between devices: 118 us -> none  [shards(): gram = lax.psum(partial_gram, ('smp', 'col', 'slab'))]
    all_to_all x1, waiting for transfers between devices: 18.2 us -> 83.7 us  [shards(): lax.all_to_all(near_rows, 'smp', split_axis=0, concat_axis=0, axis_index_...]
    ppermute x0 -> x10, starting transfers between devices: none -> 59.1 us  [the longest x3 48.1 us: sum_all(): mine = mine + lax.ppermute(mine, 'smp', xor_pairs(parts, bit))]
    ppermute x0 -> x10, waiting for transfers between devices: none -> 57.4 us  [the longest x4 40.8 us: shards(): lax.ppermute(r, 'smp', xor_pairs(parts, k))]
    another operation x9 -> x0, other arithmetic: 53.9 us -> none  [the longest x6 34.2 us: shards(): jnp.linalg.cholesky(gram + shift * jnp.eye(samples, dtype=jnp.float32))]
    pallas_call x0 -> x5, Pallas kernels: none -> 45.8 us  [the longest x1 15.1 us: solve(): call(functools.partial(solve_kernel, limit), jax.ShapeDtypeStruct((8, sam...]
  transfers between devices with their start and end apart: 2 -> 11, of which waited for: 2 -> 8; matrix products, arithmetic and copies ran while one was open for 3% -> 0% of each run, Pallas kernels for 0% -> 3%
where the time goes in v2:
time: 257 us; the launch traced here: 256 us
  waiting for transfers between devices  141 us (55%)
  starting transfers between devices  64.3 us (25%)
  Pallas kernels  45.8 us (18%)
    all_to_all x1, waiting for transfers between devices, shards(): lax.all_to_all(near_rows, 'smp', split_axis=0, concat_axis=0, axis_index_...  83.7 us
    ppermute x3, starting transfers between devices, sum_all(): mine = mine + lax.ppermute(mine, 'smp', xor_pairs(parts, bit))  48.1 us
    ppermute x4, waiting for transfers between devices, shards(): lax.ppermute(r, 'smp', xor_pairs(parts, k))  40.8 us
    pallas_call x1, Pallas kernels, solve(): call(functools.partial(solve_kernel, limit), jax.ShapeDtypeStruct((8, sam...  15.1 us
    ppermute x3, waiting for transfers between devices, sum_all(): mine = mine + lax.ppermute(mine, 'smp', xor_pairs(parts, bit))  10.6 us
    pallas_call x1, Pallas kernels, far_products(): call(functools.partial(far_kernel, rows), (jax.ShapeDtypeStruct((slabs, t...  10.5 us
    ppermute x4, starting transfers between devices, shards(): lax.ppermute(r, 'smp', xor_pairs(parts, k))  8.92 us
    pallas_call x1, Pallas kernels, pack(): call(functools.partial(pack_kernel, far_count), [pltpu.HBM((far_count, he...  7.65 us
  transfers between devices with their start and end apart: 11, of which 8 were waited for; matrix products, arithmetic and copies ran while one was open for 0% of the time, Pallas kernels for 3%

profile of v2, /device:TPU:0, one launch (start us, length us, event | category | flops | bytes accessed | tf_op | source)
XLA Modules:
  0.0 255.8 jit_solution(5747870594437545944)
XLA Ops:
  0.0 0.6 pad_add_fusion.1.dest
  0.6 7.6 %shard_map.28 = (bf16[4,512,1024]{2,1,0:T(8,128)(2,1)}, bf16[512,1024]{1,0:T(8,128)(2,1)}, bf16[512,1024]{1,0:T(8,128)(2,1)}, bf16[512,1024]{1,0:T(8,128)(2,1)}, bf16[512,1024]{1,0:T(8,128)(2,1)}) custom-call(s32[8]{0:T(128)} %pad_add_fusion.1.dest, bf16[32,16,8192]{2,1,0:T(8,128)(2,1)} %j_ref.1), custom_call_target="tpu_custom_call" | custom-call | tf_op jit(solution)/shard_map/pallas_call | solution.py:87
  8.2 0.0 copy-start.6
  8.3 5.2 %all-to-all-start = ((bf16[4,512,1024]{2,1,0:T(8,128)(2,1)}), bf16[4,512,1024]{2,1,0:T(8,128)(2,1)}, u32[]{:S(2)}, u32[]{:S(2)}) async-start(bf16[4,512,1024]{2,1,0:T(8,128)(2,1)} %get-tuple-element.20), calls=%async_computation | async-start | bytes 8388608 | tf_op jit(solution)/shard_map/all_to_all | solution.py:437
  13.5 3.7 %collective-permute-start = (bf16[512,1024]{1,0:T(8,128)(2,1)}, bf16[512,1024]{1,0:T(8,128)(2,1)S(1)}, u32[]{:S(2)}, u32[]{:S(2)}) collective-permute-start(bf16[512,1024]{1,0:T(8,128)(2,1)} %get-tuple-element.16), channel_id=1, source_target_pairs={{0,16},{4,20},{8,24},{12,28},{16,0},{20,4},{24,8},{28,12},{1,17},{... | collective-permute-start | bytes 3145736 | tf_op jit(solution)/shard_map/ppermute | solution.py:445
  17.2 1.3 collective-permute-start.1
  18.6 3.8 %collective-permute-start.2 = (bf16[512,1024]{1,0:T(8,128)(2,1)}, bf16[512,1024]{1,0:T(8,128)(2,1)S(1)}, u32[]{:S(2)}, u32[]{:S(2)}) collective-permute-start(bf16[512,1024]{1,0:T(8,128)(2,1)} %get-tuple-element.18), channel_id=1, source_target_pairs={{0,24},{4,28},{8,16},{12,20},{16,8},{20,12},{24,0},{28,4},{1,25},{... | collective-permute-start | bytes 3145736 | tf_op jit(solution)/shard_map/ppermute | solution.py:445
  22.4 0.0 collective-permute-start.3
  22.4 0.0 copy-done.6
  22.4 0.2 dynamic_update_slice.3.refs_7_
  22.6 0.0 copy-start.5
  22.7 0.7 pad_add_fusion.place
  23.3 83.7 %all-to-all-done.near_ref = bf16[4,512,1024]{2,1,0:T(8,128)(2,1)} async-done(((bf16[4,512,1024]{2,1,0:T(8,128)(2,1)}), bf16[4,512,1024]{2,1,0:T(8,128)(2,1)}, u32[]{:S(2)}, u32[]{:S(2)}) %all-to-all-start) | async-done | bytes 4194336 | tf_op jit(solution)/shard_map/all_to_all | solution.py:437
  107.0 7.3 %shard_map.29 = (bf16[16,128,1024]{2,1,0:T(8,128)(2,1)}, f32[16,1,1024]{2,1,0:T(1,128)}, f32[128,128]{1,0:T(8,128)}) custom-call(bf16[4,512,1024]{2,1,0:T(8,128)(2,1)} %all-to-all-done.near_ref), custom_call_target="tpu_custom_call" | custom-call | tf_op jit(solution)/shard_map/pallas_call | solution.py:135
  114.3 0.0 collective-permute-done.refs_0_
  114.3 0.0 copy-start
  114.3 40.8 %collective-permute-done.1.refs_1_ = bf16[512,1024]{1,0:T(8,128)(2,1)S(1)} collective-permute-done((bf16[512,1024]{1,0:T(8,128)(2,1)}, bf16[512,1024]{1,0:T(8,128)(2,1)S(1)}, u32[]{:S(2)}, u32[]{:S(2)}) %collective-permute-start.1) | collective-permute-done | bytes 1048608 | tf_op jit(solution)/shard_map/ppermute | solution.py:445
  155.2 0.0 copy-start.1
  155.2 0.0 collective-permute-done.2.refs_2_
  155.2 0.0 copy-start.2
  155.2 0.0 collective-permute-done.3.refs_3_
  155.2 0.0 copy-done.5
  155.2 0.0 copy-done
  155.2 1.0 copy-done.1
  156.2 0.3 copy-done.2
  156.5 10.5 %shard_map.30 = (bf16[16,128,1024]{2,1,0:T(8,128)(2,1)}, f32[200,128]{1,0:T(8,128)}, f32[200,128]{1,0:T(8,128)}) custom-call(s32[6]{0:T(128)} %pad_add_fusion.place, bf16[512,1024]{1,0:T(8,128)(2,1)} %copy-done, bf16[512,1024]{1,0:T(8,128)(2,1)} %copy-done.1, bf16[512,1024]{1,0:T(8,128)(2,1)} %copy-done.2, bf16[512,1024]{1,0:T(8,128)(2,1)} %collective-permute-done.3.refs_3_, ...), custom_call_target="tpu_custom_call" | custom-call | tf_op jit(solution)/shard_map/pallas_call | solution.py:214
  167.0 0.1 collective-permute-start.4
  167.0 1.5 collective-permute-done.4
  168.6 0.9 add.48
  169.5 1.9 collective-permute-start.5
  171.4 3.2 %collective-permute-done.5 = f32[200,128]{1,0:T(8,128)S(1)} collective-permute-done((f32[200,128]{1,0:T(8,128)S(1)}, f32[200,128]{1,0:T(8,128)S(1)}, u32[]{:S(2)}, u32[]{:S(2)}) %collective-permute-start.5) | collective-permute-done | bytes 102432 | tf_op jit(solution)/shard_map/ppermute | solution.py:416
  174.6 0.1 collective-permute-start.6
  174.7 4.6 %collective-permute-done.6 = f32[200,128]{1,0:T(8,128)S(1)} collective-permute-done((f32[200,128]{1,0:T(8,128)S(1)}, f32[200,128]{1,0:T(8,128)S(1)}, u32[]{:S(2)}, u32[]{:S(2)}) %collective-permute-start.6) | collective-permute-done | bytes 102432 | tf_op jit(solution)/shard_map/ppermute | solution.py:419
  179.4 43.1 %collective-permute-start.7 = (f32[200,128]{1,0:T(8,128)S(1)}, f32[200,128]{1,0:T(8,128)S(1)}, u32[]{:S(2)}, u32[]{:S(2)}) collective-permute-start(f32[200,128]{1,0:T(8,128)S(1)} %add.50), channel_id=1, source_target_pairs={{0,8},{4,12},{8,0},{12,4},{16,24},{20,28},{24,16},{28,20},{1,9},{5... | collective-permute-start | bytes 307208 | tf_op jit(solution)/shard_map/ppermute | solution.py:419
  222.5 2.6 %collective-permute-done.7 = f32[200,128]{1,0:T(8,128)S(1)} collective-permute-done((f32[200,128]{1,0:T(8,128)S(1)}, f32[200,128]{1,0:T(8,128)S(1)}, u32[]{:S(2)}, u32[]{:S(2)}) %collective-permute-start.7) | collective-permute-done | bytes 102432 | tf_op jit(solution)/shard_map/ppermute | solution.py:419
  225.2 4.9 %collective-permute-start.8 = (f32[200,128]{1,0:T(8,128)S(1)}, f32[200,128]{1,0:T(8,128)S(1)}, u32[]{:S(2)}, u32[]{:S(2)}) collective-permute-start(f32[200,128]{1,0:T(8,128)S(1)} %add.51), channel_id=1, source_target_pairs={{0,16},{4,20},{8,24},{12,28},{16,0},{20,4},{24,8},{28,12},{1,17},{... | collective-permute-start | bytes 307208 | tf_op jit(solution)/shard_map/ppermute | solution.py:419
  230.0 3.3 %collective-permute-done.8 = f32[200,128]{1,0:T(8,128)S(1)} collective-permute-done((f32[200,128]{1,0:T(8,128)S(1)}, f32[200,128]{1,0:T(8,128)S(1)}, u32[]{:S(2)}, u32[]{:S(2)}) %collective-permute-start.8) | collective-permute-done | bytes 102432 | tf_op jit(solution)/shard_map/ppermute | solution.py:419
  233.4 0.0 copy-start.3
  233.4 0.1 collective-permute-start.9
  233.4 1.3 collective-permute-done.9.other_ref
  234.7 0.0 copy-done.3
  234.7 0.0 copy-start.4
  234.7 0.6 copy-done.4
  235.4 15.1 %shard_map.31.x_ref = f32[8,256]{1,0:T(8,128)} custom-call(s32[1]{0:T(128)} %bitcast.1.core, f32[200,128]{1,0:T(8,128)} %copy-done.3, f32[200,128]{1,0:T(8,128)} %copy-done.4), custom_call_target="tpu_custom_call" | custom-call | tf_op jit(solution)/shard_map/pallas_call | solution.py:352
  250.5 5.3 %shard_map.32 = f32[16,1024]{1,0:T(8,128)} custom-call(s32[1]{0:T(128)} %bitcast.high, f32[8,256]{1,0:T(8,128)} %shard_map.31.x_ref, bf16[16,128,1024]{2,1,0:T(8,128)(2,1)} %get-tuple-element.21.refs_4_.cn_ref, bf16[16,128,1024]{2,1,0:T(8,128)(2,1)} %get-tuple-element.26.cf_ref), custom_call_target="tpu_custom_call" | custom-call | tf_op jit(solution)/shard_map/pallas_call | solution.py:394
  (8 shorter events, 0.1 us)
Async XLA Ops:
  8.2 14.2 %copy-start.6 = (f32[32]{0:T(128)S(1)}, f32[32]{0:T(128)}, u32[]{:S(2)}) copy-start(f32[32]{0:T(128)} %param.3) | copy-start | bytes 388
  8.3 98.8 %all-to-all-start = ((bf16[4,512,1024]{2,1,0:T(8,128)(2,1)}), bf16[4,512,1024]{2,1,0:T(8,128)(2,1)}, u32[]{:S(2)}, u32[]{:S(2)}) async-start(bf16[4,512,1024]{2,1,0:T(8,128)(2,1)} %get-tuple-element.20), calls=%async_computation | async-start | bytes 8388608 | tf_op jit(solution)/shard_map/all_to_all | solution.py:437
  13.5 100.8 %collective-permute-start = (bf16[512,1024]{1,0:T(8,128)(2,1)}, bf16[512,1024]{1,0:T(8,128)(2,1)S(1)}, u32[]{:S(2)}, u32[]{:S(2)}) collective-permute-start(bf16[512,1024]{1,0:T(8,128)(2,1)} %get-tuple-element.16), channel_id=1, source_target_pairs={{0,16},{4,20},{8,24},{12,28},{16,0},{20,4},{24,8},{28,12},{1,17},{... | collective-permute-start | bytes 3145736 | tf_op jit(solution)/shard_map/ppermute | solution.py:445
  17.2 137.9 %collective-permute-start.1 = (bf16[512,1024]{1,0:T(8,128)(2,1)}, bf16[512,1024]{1,0:T(8,128)(2,1)S(1)}, u32[]{:S(2)}, u32[]{:S(2)}) collective-permute-start(bf16[512,1024]{1,0:T(8,128)(2,1)} %get-tuple-element.17), channel_id=1, source_target_pairs={{0,20},{4,16},{8,28},{12,24},{16,4},{20,0},{24,12},{28,8},{1,21},{... | collective-permute-start | bytes 3145736 | tf_op jit(solution)/shard_map/ppermute | solution.py:445
  18.6 136.6 %collective-permute-start.2 = (bf16[512,1024]{1,0:T(8,128)(2,1)}, bf16[512,1024]{1,0:T(8,128)(2,1)S(1)}, u32[]{:S(2)}, u32[]{:S(2)}) collective-permute-start(bf16[512,1024]{1,0:T(8,128)(2,1)} %get-tuple-element.18), channel_id=1, source_target_pairs={{0,24},{4,28},{8,16},{12,20},{16,8},{20,12},{24,0},{28,4},{1,25},{... | collective-permute-start | bytes 3145736 | tf_op jit(solution)/shard_map/ppermute | solution.py:445
  22.4 132.8 %collective-permute-start.3 = (bf16[512,1024]{1,0:T(8,128)(2,1)}, bf16[512,1024]{1,0:T(8,128)(2,1)}, u32[]{:S(2)}, u32[]{:S(2)}) collective-permute-start(bf16[512,1024]{1,0:T(8,128)(2,1)} %get-tuple-element.19), channel_id=1, source_target_pairs={{0,28},{4,24},{8,20},{12,16},{16,12},{20,8},{24,4},{28,0},{1,29},{... | collective-permute-start | bytes 3145736 | tf_op jit(solution)/shard_map/ppermute | solution.py:445
  22.6 132.6 %copy-start.5 = (f32[16,128]{1,0:T(8,128)}, f32[16,128]{1,0:T(8,128)S(1)}, u32[]{:S(2)}) copy-start(f32[16,128]{1,0:T(8,128)S(1)} %dynamic_update_slice.3.refs_7_) | copy-start | bytes 24580
  114.3 40.9 %copy-start = (bf16[512,1024]{1,0:T(8,128)(2,1)}, bf16[512,1024]{1,0:T(8,128)(2,1)S(1)}, u32[]{:S(2)}) copy-start(bf16[512,1024]{1,0:T(8,128)(2,1)S(1)} %collective-permute-done.refs_0_) | copy-start | bytes 3145732
  155.2 1.0 copy-start.1
  155.2 1.3 copy-start.2
  167.0 1.6 collective-permute-start.4
  169.5 5.1 %collective-permute-start.5 = (f32[200,128]{1,0:T(8,128)S(1)}, f32[200,128]{1,0:T(8,128)S(1)}, u32[]{:S(2)}, u32[]{:S(2)}) collective-permute-start(f32[200,128]{1,0:T(8,128)S(1)} %add.48), channel_id=1, source_target_pairs={{0,1},{1,0},{2,3},{3,2},{4,5},{5,4},{6,7},{7,6},{8,9},{9,8},{10,11... | collective-permute-start | bytes 307208 | tf_op jit(solution)/shard_map/ppermute | solution.py:416
  174.6 4.7 %collective-permute-start.6 = (f32[200,128]{1,0:T(8,128)S(1)}, f32[200,128]{1,0:T(8,128)S(1)}, u32[]{:S(2)}, u32[]{:S(2)}) collective-permute-start(f32[200,128]{1,0:T(8,128)S(1)} %add.49), channel_id=1, source_target_pairs={{0,4},{4,0},{8,12},{12,8},{16,20},{20,16},{24,28},{28,24},{1,5},{5... | collective-permute-start | bytes 307208 | tf_op jit(solution)/shard_map/ppermute | solution.py:419
  179.4 45.8 %collective-permute-start.7 = (f32[200,128]{1,0:T(8,128)S(1)}, f32[200,128]{1,0:T(8,128)S(1)}, u32[]{:S(2)}, u32[]{:S(2)}) collective-permute-start(f32[200,128]{1,0:T(8,128)S(1)} %add.50), channel_id=1, source_target_pairs={{0,8},{4,12},{8,0},{12,4},{16,24},{20,28},{24,16},{28,20},{1,9},{5... | collective-permute-start | bytes 307208 | tf_op jit(solution)/shard_map/ppermute | solution.py:419
  225.2 8.2 %collective-permute-start.8 = (f32[200,128]{1,0:T(8,128)S(1)}, f32[200,128]{1,0:T(8,128)S(1)}, u32[]{:S(2)}, u32[]{:S(2)}) collective-permute-start(f32[200,128]{1,0:T(8,128)S(1)} %add.51), channel_id=1, source_target_pairs={{0,16},{4,20},{8,24},{12,28},{16,0},{20,4},{24,8},{28,12},{1,17},{... | collective-permute-start | bytes 307208 | tf_op jit(solution)/shard_map/ppermute | solution.py:419
  233.4 1.4 copy-start.3
  233.4 1.4 collective-permute-start.9
  234.7 0.6 copy-start.4

commit v3 on v2

v3 whole, which is shorter than its diff:
```python
import functools

import jax
import jax.numpy as jnp
from jax import lax
from jax.experimental import pallas as pl
from jax.experimental.pallas import tpu as pltpu
from jax.sharding import PartitionSpec as P

BLOCK = 64
LANES = 128
EXTRA = 16
TRANSFER_FLOPS = 10**11
CHUNK = 256
F32 = jnp.float32
BF16 = jnp.bfloat16
HIGHEST = lax.Precision.HIGHEST
MIB = 1024 * 1024
SWAP = [(0, 1), (1, 0)]


def mm(a, b, ca, cb):
    return lax.dot_general(
        a, b, (((ca,), (cb,)), ((), ())), precision=HIGHEST, preferred_element_type=F32
    )


def products(a, b):
    return lax.dot_general(a, b, (((1,), (1,)), ((), ())), preferred_element_type=F32)


def call(kernel, out_shape, grid_spec=None, vmem=58, flops=0, **kw):
    if grid_spec is not None:
        kw["grid_spec"] = grid_spec
    return pl.pallas_call(
        kernel,
        out_shape=out_shape,
        compiler_params=pltpu.CompilerParams(vmem_limit_bytes=vmem * MIB),
        cost_estimate=pl.CostEstimate(flops=flops, bytes_accessed=0, transcendentals=0),
        **kw,
    )


def kernel_mib(half):
    return 16 if half <= 128 else 40


def lane_chunks(width):
    size = min(CHUNK, width)
    return [slice(c, c + size) for c in range(0, width, size)]


def pack_kernel(far_count, j_ref, near_ref, *refs):
    far_refs, (buffer, out, in_sems, out_sems) = refs[:far_count], refs[far_count:]
    count, rows, slabs, width = buffer.shape
    me = lax.axis_index("smp")
    high = me // far_count
    dests = [high * far_count + k for k in range(far_count)]
    dests += [me ^ (far_count + k) for k in range(far_count)]

    def read(k):
        columns = pl.ds(pl.multiple_of(dests[k] * width, LANES), width)
        return pltpu.make_async_copy(j_ref.at[:, :, columns], buffer.at[k], in_sems.at[k])

    def write(k):
        return pltpu.make_async_copy(out.at[k], near_ref.at[k], out_sems.at[k])

    for k in range(count):
        read(k).start()
    for k in range(count):
        read(k).wait()
        for part in lane_chunks(width):
            x = jnp.swapaxes(buffer[k, :, :, part].astype(F32), 0, 1)
            x = x.reshape(slabs * rows, x.shape[2]).astype(BF16)
            if k < far_count:
                out[k, :, part] = x
            else:
                far_refs[k - far_count][:, part] = x
        if k < far_count:
            write(k).start()
    for k in range(far_count):
        write(k).wait()


def pack(jacobian, parts):
    rows, slabs, columns = jacobian.shape
    far_count, width = parts // 2, columns // parts
    height = slabs * rows
    return call(
        functools.partial(pack_kernel, far_count),
        [pltpu.HBM((far_count, height, width), BF16)]
        + [jax.ShapeDtypeStruct((height, width), BF16)] * far_count,
        pl.GridSpec(
            grid=(),
            in_specs=[pl.BlockSpec(memory_space=pl.ANY)],
            out_specs=[pl.BlockSpec(memory_space=pl.ANY)]
            + [pl.BlockSpec(memory_space=pltpu.VMEM)] * far_count,
            scratch_shapes=[
                pltpu.VMEM((parts, rows, slabs, width), BF16),
                pltpu.VMEM((far_count, height, width), BF16),
                pltpu.SemaphoreType.DMA((parts,)),
                pltpu.SemaphoreType.DMA((far_count,)),
            ],
        ),
        vmem=52,
    )(jacobian)


def near_kernel(rows, near_ref, c_ref, base_ref, gram_ref):
    step = pl.program_id(0)
    parts, height, width = near_ref.shape
    total = parts * rows

    @pl.when(step == 0)
    def _():
        gram_ref[...] = jnp.zeros_like(gram_ref)

    for half in range(height // rows):
        slab = pl.ds(half * rows, rows)
        for part in lane_chunks(width):
            sums = 0.0
            for k in range(parts):
                sums = sums + jnp.sum(near_ref[k, slab, part].astype(F32), axis=0, keepdims=True)
            base = sums * (1.0 / total)
            base_ref[half, :, part] = base
            for k in range(parts):
                x = near_ref[k, slab, part].astype(F32) - base
                c_ref[half, k * rows : (k + 1) * rows, part] = x.astype(BF16)
        c = c_ref[half]
        gram_ref[...] += products(c, c)


def near_products(near, slabs):
    parts, height, width = near.shape
    rows = height // slabs
    total = parts * rows
    group = 2
    return call(
        functools.partial(near_kernel, rows),
        (
            jax.ShapeDtypeStruct((slabs, total, width), BF16),
            jax.ShapeDtypeStruct((slabs, 1, width), F32),
            jax.ShapeDtypeStruct((total, total), F32),
        ),
        pl.GridSpec(
            grid=(slabs // group,),
            in_specs=[pl.BlockSpec((parts, group * rows, width), lambda i: (0, i, 0))],
            out_specs=[
                pl.BlockSpec((group, total, width), lambda i: (i, 0, 0)),
                pl.BlockSpec((group, 1, width), lambda i: (i, 0, 0)),
                pl.BlockSpec((total, total), lambda i: (0, 0)),
            ],
        ),
        vmem=kernel_mib(total),
    )(near)


def by_distance(x, axis, size, place):
    blocks = x.shape[axis] // size
    bit = 1
    while bit < blocks:
        parts = [lax.slice_in_dim(x, size * (i ^ bit), size * ((i ^ bit) + 1), axis=axis) for i in range(blocks)]
        x = jnp.where((place & bit) > 0, jnp.concatenate(parts, axis=axis), x)
        bit *= 2
    return x


def far_kernel(rows, place, *refs):
    far_refs, (cn_ref, base_ref, near_ref, extra_ref, mine_ref, other_ref, gram, far) = refs[:-8], refs[-8:]
    slabs, total, width = cn_ref.shape

    def add(slab):
        span = slice(slab * rows, (slab + 1) * rows)
        for part in lane_chunks(width):
            base = base_ref[slab, :, part]
            for k, ref in enumerate(far_refs):
                x = ref[span, part].astype(F32) - base
                far[k * rows : (k + 1) * rows, part] = x.astype(BF16)
        c = far[...]
        return products(jnp.concatenate([cn_ref[slab], c], axis=0), c)

    total_products = add(0)
    for slab in range(1, slabs):
        total_products = total_products + add(slab)
    low = place[0] == 0
    products_far = by_distance(total_products, 1, rows, place[2])
    cross, far_far = products_far[:total], by_distance(products_far[total:], 0, rows, place[2])
    near_near = near_ref[...]
    gram[:total, :] = jnp.where(low, near_near, far_far)
    gram[total : 2 * total, :] = jnp.where(low, far_far, near_near)
    gram[2 * total : 3 * total, :] = jnp.where(low, cross, cross.T)
    gram[3 * total :, :] = extra_ref[...]
    count = mine_ref.shape[0]
    mine_ref[...] = gram[pl.ds(pl.multiple_of(place[1] * count, 8), count), :]
    other_ref[...] = gram[pl.ds(pl.multiple_of((1 - place[1]) * count, 8), count), :]


def far_products(far_blocks, place, cn, base, near_gram, extra):
    _, total, width = cn.shape
    rows = total // len(far_blocks)
    height = 3 * total + EXTRA
    share = jax.ShapeDtypeStruct((height // 2, total), F32)
    whole = pl.BlockSpec(memory_space=pltpu.VMEM)
    return call(
        functools.partial(far_kernel, rows),
        (share, share),
        pltpu.PrefetchScalarGridSpec(
            num_scalar_prefetch=1,
            grid=(),
            in_specs=[whole] * (len(far_blocks) + 4),
            out_specs=[whole] * 2,
            scratch_shapes=[
                pltpu.VMEM((height, total), F32),
                pltpu.VMEM((total, width), BF16),
            ],
        ),
        vmem=kernel_mib(total),
    )(place, *far_blocks, cn, base, near_gram, extra)


def energy_kernel(parts, e_ref, out_ref):
    rows = e_ref.shape[1]
    me = lax.axis_index("smp")
    count = parts // 2
    lead = jnp.logical_and(lax.axis_index("col") == 0, lax.axis_index("slab") == 0)
    shape = out_ref.shape
    wide = jnp.concatenate([e_ref[...]] * count, axis=1)
    row = lax.broadcasted_iota(jnp.int32, shape, 0)
    block = lax.broadcasted_iota(jnp.int32, shape, 1) // rows
    mine = jnp.logical_and(row == me // count, block == me % count)
    out_ref[...] = jnp.where(jnp.logical_and(mine, lead), jnp.broadcast_to(wide, shape), 0.0)


def energy_rows(local_energy, parts):
    rows = local_energy.shape[0]
    return call(
        functools.partial(energy_kernel, parts),
        jax.ShapeDtypeStruct((EXTRA, rows * parts // 2), F32),
        vmem=16,
        flops=TRANSFER_FLOPS,
    )(local_energy[None])


def inverse(block):
    size = block.shape[0]
    shape = (8, 2 * size)
    lane = lax.broadcasted_iota(jnp.int32, shape, 1)
    sub = lax.broadcasted_iota(jnp.int32, shape, 0)
    wide = jnp.concatenate([block, jnp.zeros_like(block)], axis=1)
    count = size // 8
    tiles = [
        wide[8 * t : 8 * t + 8] + jnp.where(lane - size == sub + 8 * t, 1.0, 0.0) for t in range(count)
    ]
    scaled = []
    for t in range(count):
        normal = jnp.zeros(shape, F32)
        live = tiles[t:]
        cols = [[jnp.broadcast_to(x[:, 8 * t + j : 8 * t + j + 1], shape) for x in live] for j in range(8)]
        for at in range(0, 8, 2):
            c0, c1 = cols[at], cols[at + 1]
            a, b, c = c0[0][at : at + 1], c1[0][at : at + 1], c1[0][at + 1 : at + 2]
            d = 1.0 / (a * c - b * b)
            g0 = [(x * c - y * b) * d for x, y in zip(c0, c1)]
            g1 = [(y * a - x * b) * d for x, y in zip(c0, c1)]
            g0[0] = jnp.where(sub > at + 1, g0[0], 0.0)
            g1[0] = jnp.where(sub > at + 1, g1[0], 0.0)
            for j in range(at + 2, 8):
                u0, u1 = cols[j][0][at : at + 1], cols[j][0][at + 1 : at + 2]
                cols[j] = [x - (y * u0 + z * u1) for x, y, z in zip(cols[j], g0, g1)]
            r0, r1 = live[0][at : at + 1], live[0][at + 1 : at + 2]
            live = [x - (y * r0 + z * r1) for x, y, z in zip(live, g0, g1)]
            normal = jnp.where(sub == at, (r0 * c - r1 * b) * d, normal)
            normal = jnp.where(sub == at + 1, (r1 * a - r0 * b) * d, normal)
        tiles[t:] = live
        scaled.append(normal)
    w = jnp.concatenate(tiles, axis=0)[:, size:]
    n = jnp.concatenate(scaled, axis=0)[:, size:]
    return mm(w, n, 0, 0)


def solve_kernel(limit, core, mine_ref, other_ref, x_ref, sums, gram):
    count = mine_ref.shape[0]
    sums[pl.ds(pl.multiple_of(core[0] * count, 8), count), :] = mine_ref[...]
    sums[pl.ds(pl.multiple_of((1 - core[0]) * count, 8), count), :] = other_ref[...]
    half = sums.shape[1]
    samples = 2 * half
    low, high = sums[:half, :], sums[half : 2 * half, :]
    cross = sums[2 * half : 3 * half, :]
    turned = cross.T
    inv = 1.0 / samples
    col_low = (jnp.sum(low, axis=1, keepdims=True) + jnp.sum(cross, axis=1, keepdims=True)) * inv
    col_high = (jnp.sum(high, axis=1, keepdims=True) + jnp.sum(turned, axis=1, keepdims=True)) * inv
    row_low = (jnp.sum(low, axis=0, keepdims=True) + jnp.sum(turned, axis=0, keepdims=True)) * inv
    row_high = (jnp.sum(high, axis=0, keepdims=True) + jnp.sum(cross, axis=0, keepdims=True)) * inv
    mean = (jnp.sum(row_low, axis=1, keepdims=True) + jnp.sum(row_high, axis=1, keepdims=True)) * inv
    gram[:half, :half] = (low - col_low - row_low + mean) * inv
    gram[half:, half:] = (high - col_high - row_high + mean) * inv
    gram[half:, :half] = (turned - col_high - row_low + mean) * inv
    gram[:half, half:] = (cross - col_low - row_high + mean) * inv
    n = samples // BLOCK
    spans = [slice(BLOCK * i, BLOCK * (i + 1)) for i in range(n)]
    on = lax.broadcasted_iota(jnp.int32, (BLOCK, BLOCK), 0) == lax.broadcasted_iota(
        jnp.int32, (BLOCK, BLOCK), 1
    )
    diagonal = sum(jnp.where(on, gram[s, s], 0.0) for s in spans)
    diagonal = jnp.sum(diagonal, axis=0, keepdims=True)
    shift = jnp.sum(diagonal, axis=1, keepdims=True) * (0.01 * inv)

    e = sums[3 * half : 3 * half + 8, :]
    energies = jnp.concatenate([e[0:1], e[1:2]], axis=1)
    center = jnp.sum(energies, axis=1, keepdims=True) * inv
    eps = jnp.broadcast_to((energies - center) * (inv**0.5), (8, samples))

    left, factor, solved = {}, {}, []
    for j in range(n):
        for i in range(j, n):
            block = gram[spans[i], spans[j]]
            if i == j:
                block = jnp.where(on, block + shift, block)
            for k in range(j):
                block = block - mm(factor[i, k], left[j, k], 1, 1)
            left[i, j] = block
        diag = inverse(left[j, j])
        for i in range(j + 1, n):
            factor[i, j] = mm(left[i, j], diag, 1, 0)
        z = eps[:, spans[j]]
        for k in range(j):
            z = z - mm(solved[k][0], factor[j, k], 1, 1)
        solved.append((z, mm(z, diag, 1, 0)))
    xs = [w for _, w in solved]
    for i in reversed(range(n)):
        for j in range(i):
            xs[j] = xs[j] - mm(xs[i], factor[i, j], 1, 0)
    x = jnp.concatenate(xs, axis=1)
    x = x - jnp.sum(x, axis=1, keepdims=True) * inv
    size = jnp.sum(mm(x, gram[...], 1, 0) * x, axis=1, keepdims=True)
    clip = jnp.minimum(1.0, limit / jnp.sqrt(jnp.maximum(size, 0.0)))
    x_ref[...] = x * (clip * -(inv**0.5))


def solve(core, mine, other, limit):
    count, half = mine.shape
    samples = 2 * half
    return call(
        functools.partial(solve_kernel, limit),
        jax.ShapeDtypeStruct((8, samples), F32),
        pltpu.PrefetchScalarGridSpec(
            num_scalar_prefetch=1,
            grid=(1,),
            in_specs=[pl.BlockSpec((count, half), lambda i, s: (0, 0))] * 2,
            out_specs=pl.BlockSpec((8, samples), lambda i, s: (0, 0)),
            scratch_shapes=[
                pltpu.VMEM((2 * count, half), F32),
                pltpu.VMEM((samples, samples), F32),
            ],
        ),
        vmem=kernel_mib(half),
    )(core, mine, other)


def update_kernel(rows, place, x_ref, cn_ref, base_ref, *refs):
    far_refs, out_ref = refs[:-1], refs[-1]
    slabs, total, _ = cn_ref.shape
    sub = lax.broadcasted_iota(jnp.int32, (8, total), 0)

    def split(x):
        first = x.astype(BF16).astype(F32)
        rest = x - first
        second = rest.astype(BF16).astype(F32)
        x = jnp.where(sub == 0, first, jnp.where(sub == 1, second, rest - second))
        return jnp.where(sub < 3, x, 0.0).astype(BF16)

    low, high = x_ref[:, :total], x_ref[:, total:]
    is_low = place[0] == 0
    near = jnp.where(is_low, low, high)
    far = by_distance(jnp.where(is_low, high, low), 1, rows, place[2])
    weight = jnp.sum(far[:1], axis=1, keepdims=True)
    both = jnp.concatenate([split(near), split(far)], axis=1)

    def one(slab):
        span = slice(slab * rows, (slab + 1) * rows)
        block = jnp.concatenate([cn_ref[slab]] + [ref[span, :] for ref in far_refs], axis=0)
        y = jnp.dot(both, block, preferred_element_type=F32)
        out_ref[slab : slab + 1, :] = jnp.sum(y, axis=0, keepdims=True) - weight * base_ref[slab]

    for slab in range(slabs):
        one(slab)


def update(x, place, cn, base, far_blocks):
    slabs, total, width = cn.shape
    whole = pl.BlockSpec(memory_space=pltpu.VMEM)
    return call(
        functools.partial(update_kernel, total // len(far_blocks)),
        jax.ShapeDtypeStruct((slabs, width), F32),
        pltpu.PrefetchScalarGridSpec(
            num_scalar_prefetch=1,
            grid=(),
            in_specs=[whole] * (3 + len(far_blocks)),
            out_specs=whole,
        ),
        vmem=kernel_mib(total),
    )(place, x, cn, base, *far_blocks)


def xor_pairs(size, bits):
    return [(i, i ^ bits) for i in range(size)]


def sum_all(mine, other, parts):
    mine = mine + lax.ppermute(other, "col", SWAP)
    mine = mine + lax.ppermute(mine, "slab", SWAP)
    bit = 1
    while bit < parts:
        mine = mine + lax.ppermute(mine, "smp", xor_pairs(parts, bit))
        bit *= 2
    return mine, lax.ppermute(mine, "col", SWAP)


def shards(parts, slab_parts, col_parts, jacobian, local_energy):
    rows, slabs, columns = jacobian.shape
    params = slabs * slab_parts * columns * col_parts
    half = rows * parts // 2
    me = lax.axis_index("smp")
    count = parts // 2
    far = list(range(count, parts))
    high = me // count

    near_rows, *far_rows = pack(jacobian, parts)
    near = lax.all_to_all(
        near_rows,
        "smp",
        split_axis=0,
        concat_axis=0,
        axis_index_groups=[list(range(count)), far],
        tiled=True,
    )
    far_blocks = [lax.ppermute(r, "smp", xor_pairs(parts, k)) for k, r in zip(far, far_rows)]

    extra = energy_rows(local_energy, parts)
    cn, base, near_gram = near_products(near, slabs)
    core = lax.axis_index("col")
    place = jnp.stack([high, core, me % count])
    mine, other = far_products(far_blocks, place, cn, base, near_gram, extra)
    mine, other = sum_all(mine, other, parts)
    x = solve(core[None], mine, other, 0.3 * float(params) ** 0.5)
    return update(x, place, cn, base, far_blocks)


def solution(mesh):
    body = functools.partial(shards, mesh.shape["smp"], mesh.shape["slab"], mesh.shape["col"])
    in_specs = (P("smp", "slab", "col"), P("smp"))
    out_specs = P("slab", ("col", "smp"))
    return jax.shard_map(body, mesh=mesh, in_specs=in_specs, out_specs=out_specs, check_vma=False)
```

time: 257 us -> 237 us (0.922)
  Pallas kernels: 45.8 us -> 33 us
  starting transfers between devices: 64.3 us -> 52.9 us
  waiting for transfers between devices: 141 us -> 150 us
    all_to_all x1, waiting for transfers between devices: 83.7 us -> 135 us  [shards(): lax.all_to_all(near_rows, 'smp', split_axis=0, concat_axis=0, axis_index_...]
    ppermute x4, waiting for transfers between devices: 40.8 us -> 0.01 us  [shards(): lax.ppermute(r, 'smp', xor_pairs(parts, k))]
    ppermute x3, starting transfers between devices: 48.1 us -> 37 us  [sum_all(): mine = mine + lax.ppermute(mine, 'smp', xor_pairs(parts, bit))]
    pallas_call x2 -> x3, Pallas kernels: 15.8 us -> 8.12 us  [the longest x1 4.29 us: far_products(): call(functools.partial(far_kernel, rows), (share, share), pltpu.PrefetchS...]
    pallas_call x1, Pallas kernels: 15.1 us -> 10.9 us  [solve(): call(functools.partial(solve_kernel, limit), jax.ShapeDtypeStruct((8, sam...]
  transfers between devices with their start and end apart: 11 -> 11, of which waited for: 8 -> 7; matrix products, arithmetic and copies ran while one was open for 0% -> 0% of each run, Pallas kernels for 3% -> 3%
where the time goes in v3:
time: 237 us; the launch traced here: 236 us
  waiting for transfers between devices  150 us (63%)
  starting transfers between devices  52.9 us (22%)
  Pallas kernels  33 us (14%)
    all_to_all x1, waiting for transfers between devices, shards(): lax.all_to_all(near_rows, 'smp', split_axis=0, concat_axis=0, axis_index_...  135 us
    ppermute x3, starting transfers between devices, sum_all(): mine = mine + lax.ppermute(mine, 'smp', xor_pairs(parts, bit))  37 us
    pallas_call x1, Pallas kernels, solve(): call(functools.partial(solve_kernel, limit), jax.ShapeDtypeStruct((8, sam...  10.9 us
    ppermute x3, waiting for transfers between devices, sum_all(): mine = mine + lax.ppermute(mine, 'smp', xor_pairs(parts, bit))  9.09 us
    ppermute x4, starting transfers between devices, shards(): lax.ppermute(r, 'smp', xor_pairs(parts, k))  8.97 us
    pallas_call x1, Pallas kernels, pack(): call(functools.partial(pack_kernel, far_count), [pltpu.HBM((far_count, he...  7.6 us
    pallas_call x1, Pallas kernels, near_products(): call(functools.partial(near_kernel, rows), (jax.ShapeDtypeStruct((slabs,...  6.43 us
    all_to_all x1, starting transfers between devices, shards(): lax.all_to_all(near_rows, 'smp', split_axis=0, concat_axis=0, axis_index_...  5.15 us
  transfers between devices with their start and end apart: 11, of which 7 were waited for; matrix products, arithmetic and copies ran while one was open for 0% of the time, Pallas kernels for 3%

profile of v3, /device:TPU:0, one launch (start us, length us, event | category | flops | bytes accessed | tf_op | source)
XLA Modules:
  0.0 236.4 jit_solution(7831892261497145658)
XLA Ops:
  0.0 7.6 %shard_map.28 = (bf16[4,512,1024]{2,1,0:T(8,128)(2,1)}, bf16[512,1024]{1,0:T(8,128)(2,1)}, bf16[512,1024]{1,0:T(8,128)(2,1)}, bf16[512,1024]{1,0:T(8,128)(2,1)}, bf16[512,1024]{1,0:T(8,128)(2,1)}) custom-call(bf16[32,16,8192]{2,1,0:T(8,128)(2,1)} %j_ref.1), custom_call_target="tpu_custom_call" | custom-call | tf_op jit(solution)/shard_map/pallas_call | solution.py:89
  7.6 4.1 %collective-permute-start = (bf16[512,1024]{1,0:T(8,128)(2,1)}, bf16[512,1024]{1,0:T(8,128)(2,1)S(1)}, u32[]{:S(2)}, u32[]{:S(2)}) collective-permute-start(bf16[512,1024]{1,0:T(8,128)(2,1)} %get-tuple-element.15), channel_id=1, source_target_pairs={{0,16},{4,20},{8,24},{12,28},{16,0},{20,4},{24,8},{28,12},{1,17},{... | collective-permute-start | bytes 3145736 | tf_op jit(solution)/shard_map/ppermute | solution.py:438
  11.7 1.3 collective-permute-start.1
  13.0 3.6 %collective-permute-start.2 = (bf16[512,1024]{1,0:T(8,128)(2,1)}, bf16[512,1024]{1,0:T(8,128)(2,1)S(1)}, u32[]{:S(2)}, u32[]{:S(2)}) collective-permute-start(bf16[512,1024]{1,0:T(8,128)(2,1)} %get-tuple-element.17), channel_id=1, source_target_pairs={{0,24},{4,28},{8,16},{12,20},{16,8},{20,12},{24,0},{28,4},{1,25},{... | collective-permute-start | bytes 3145736 | tf_op jit(solution)/shard_map/ppermute | solution.py:438
  16.6 0.0 collective-permute-start.3
  16.6 0.0 copy-start
  16.6 5.2 %all-to-all-start = ((bf16[4,512,1024]{2,1,0:T(8,128)(2,1)}), bf16[4,512,1024]{2,1,0:T(8,128)(2,1)}, u32[]{:S(2)}, u32[]{:S(2)}) async-start(bf16[4,512,1024]{2,1,0:T(8,128)(2,1)} %get-tuple-element.19), calls=%async_computation | async-start | bytes 8388608 | tf_op jit(solution)/shard_map/all_to_all | solution.py:430
  21.7 0.0 copy-done
  21.8 0.1 shard_map.30.refs_7_
  21.8 0.1 pad_add_fusion.place
  21.9 135.2 %all-to-all-done.near_ref = bf16[4,512,1024]{2,1,0:T(8,128)(2,1)} async-done(((bf16[4,512,1024]{2,1,0:T(8,128)(2,1)}), bf16[4,512,1024]{2,1,0:T(8,128)(2,1)}, u32[]{:S(2)}, u32[]{:S(2)}) %all-to-all-start) | async-done | bytes 4194336 | tf_op jit(solution)/shard_map/all_to_all | solution.py:430
  157.1 6.4 %shard_map.29 = (bf16[16,128,1024]{2,1,0:T(8,128)(2,1)S(1)}, f32[16,1,1024]{2,1,0:T(1,128)S(1)}, f32[128,128]{1,0:T(8,128)S(1)}) custom-call(bf16[4,512,1024]{2,1,0:T(8,128)(2,1)} %all-to-all-done.near_ref), custom_call_target="tpu_custom_call" | custom-call | tf_op jit(solution)/shard_map/pallas_call | solution.py:138
  163.6 0.0 collective-permute-done.refs_0_
  163.6 0.0 collective-permute-done.1.refs_1_
  163.6 0.0 collective-permute-done.2.refs_2_
  163.6 0.0 collective-permute-done.3.refs_3_
  163.6 4.3 %shard_map.31 = (f32[200,128]{1,0:T(8,128)S(1)}, f32[200,128]{1,0:T(8,128)S(1)}) custom-call(s32[3]{0:T(128)S(1)} %pad_add_fusion.place, bf16[512,1024]{1,0:T(8,128)(2,1)S(1)} %collective-permute-done.refs_0_, bf16[512,1024]{1,0:T(8,128)(2,1)S(1)} %collective-permute-done.1.refs_1_, bf16[512,1024]{1,0:T(8,128)(2,1)S(1)} %collective-permute-done.2.refs_2_, ...), custom_call_target="tpu_custom_call" | custom-call | tf_op jit(solution)/shard_map/pallas_call | solution.py:204
  167.9 0.1 collective-permute-start.4
  168.0 1.3 collective-permute-done.4
  169.3 1.6 collective-permute-start.5
  170.9 3.4 %collective-permute-done.5 = f32[200,128]{1,0:T(8,128)S(1)} collective-permute-done((f32[200,128]{1,0:T(8,128)S(1)}, f32[200,128]{1,0:T(8,128)S(1)}, u32[]{:S(2)}, u32[]{:S(2)}) %collective-permute-start.5) | collective-permute-done | bytes 102432 | tf_op jit(solution)/shard_map/ppermute | solution.py:412
  174.3 1.6 collective-permute-start.6
  175.9 3.1 %collective-permute-done.6 = f32[200,128]{1,0:T(8,128)S(1)} collective-permute-done((f32[200,128]{1,0:T(8,128)S(1)}, f32[200,128]{1,0:T(8,128)S(1)}, u32[]{:S(2)}, u32[]{:S(2)}) %collective-permute-start.6) | collective-permute-done | bytes 102432 | tf_op jit(solution)/shard_map/ppermute | solution.py:415
  179.1 30.5 %collective-permute-start.7 = (f32[200,128]{1,0:T(8,128)S(1)}, f32[200,128]{1,0:T(8,128)S(1)}, u32[]{:S(2)}, u32[]{:S(2)}) collective-permute-start(f32[200,128]{1,0:T(8,128)S(1)} %add.23), channel_id=1, source_target_pairs={{0,8},{4,12},{8,0},{12,4},{16,24},{20,28},{24,16},{28,20},{1,9},{5... | collective-permute-start | bytes 307208 | tf_op jit(solution)/shard_map/ppermute | solution.py:415
  209.6 2.6 %collective-permute-done.7 = f32[200,128]{1,0:T(8,128)S(1)} collective-permute-done((f32[200,128]{1,0:T(8,128)S(1)}, f32[200,128]{1,0:T(8,128)S(1)}, u32[]{:S(2)}, u32[]{:S(2)}) %collective-permute-start.7) | collective-permute-done | bytes 102432 | tf_op jit(solution)/shard_map/ppermute | solution.py:415
  212.2 4.9 %collective-permute-start.8 = (f32[200,128]{1,0:T(8,128)S(1)}, f32[200,128]{1,0:T(8,128)S(1)}, u32[]{:S(2)}, u32[]{:S(2)}) collective-permute-start(f32[200,128]{1,0:T(8,128)S(1)} %add.24), channel_id=1, source_target_pairs={{0,16},{4,20},{8,24},{12,28},{16,0},{20,4},{24,8},{28,12},{1,17},{... | collective-permute-start | bytes 307208 | tf_op jit(solution)/shard_map/ppermute | solution.py:415
  217.1 3.3 %collective-permute-done.8 = f32[200,128]{1,0:T(8,128)S(1)} collective-permute-done((f32[200,128]{1,0:T(8,128)S(1)}, f32[200,128]{1,0:T(8,128)S(1)}, u32[]{:S(2)}, u32[]{:S(2)}) %collective-permute-start.8) | collective-permute-done | bytes 102432 | tf_op jit(solution)/shard_map/ppermute | solution.py:415
  220.4 0.1 collective-permute-start.9
  220.5 1.3 collective-permute-done.9.other_ref
  221.8 10.9 %shard_map.32.x_ref = f32[8,256]{1,0:T(8,128)S(1)} custom-call(s32[1]{0:T(128)} %bitcast.1.core, f32[200,128]{1,0:T(8,128)S(1)} %add.25.mine_ref, f32[200,128]{1,0:T(8,128)S(1)} %collective-permute-done.9.other_ref), custom_call_target="tpu_custom_call" | custom-call | tf_op jit(solution)/shard_map/pallas_call | solution.py:344
  232.7 3.8 %shard_map.33 = f32[16,1024]{1,0:T(8,128)} custom-call(s32[3]{0:T(128)S(1)} %pad_add_fusion.place, f32[8,256]{1,0:T(8,128)S(1)} %shard_map.32.x_ref, bf16[16,128,1024]{2,1,0:T(8,128)(2,1)S(1)} %get-tuple-element.20.refs_4_.cn_ref, f32[16,1,1024]{2,1,0:T(1,128)S(1)} %get-tuple-element.21.refs_5_.base_ref, bf16[512,1024]{1,0:T(8,128)(2,1)S(1)} %collective-permute-done.refs_0_, ...), custom_call_target="tpu_custom_call" | custom-call | tf_op jit(solution)/shard_map/pallas_call | solution.py:393
  (5 shorter events, 0.1 us)
Async XLA Ops:
  7.6 155.9 %collective-permute-start = (bf16[512,1024]{1,0:T(8,128)(2,1)}, bf16[512,1024]{1,0:T(8,128)(2,1)S(1)}, u32[]{:S(2)}, u32[]{:S(2)}) collective-permute-start(bf16[512,1024]{1,0:T(8,128)(2,1)} %get-tuple-element.15), channel_id=1, source_target_pairs={{0,16},{4,20},{8,24},{12,28},{16,0},{20,4},{24,8},{28,12},{1,17},{... | collective-permute-start | bytes 3145736 | tf_op jit(solution)/shard_map/ppermute | solution.py:438
  11.7 151.9 %collective-permute-start.1 = (bf16[512,1024]{1,0:T(8,128)(2,1)}, bf16[512,1024]{1,0:T(8,128)(2,1)S(1)}, u32[]{:S(2)}, u32[]{:S(2)}) collective-permute-start(bf16[512,1024]{1,0:T(8,128)(2,1)} %get-tuple-element.16), channel_id=1, source_target_pairs={{0,20},{4,16},{8,28},{12,24},{16,4},{20,0},{24,12},{28,8},{1,21},{... | collective-permute-start | bytes 3145736 | tf_op jit(solution)/shard_map/ppermute | solution.py:438
  13.0 150.6 %collective-permute-start.2 = (bf16[512,1024]{1,0:T(8,128)(2,1)}, bf16[512,1024]{1,0:T(8,128)(2,1)S(1)}, u32[]{:S(2)}, u32[]{:S(2)}) collective-permute-start(bf16[512,1024]{1,0:T(8,128)(2,1)} %get-tuple-element.17), channel_id=1, source_target_pairs={{0,24},{4,28},{8,16},{12,20},{16,8},{20,12},{24,0},{28,4},{1,25},{... | collective-permute-start | bytes 3145736 | tf_op jit(solution)/shard_map/ppermute | solution.py:438
  16.6 147.0 %collective-permute-start.3 = (bf16[512,1024]{1,0:T(8,128)(2,1)}, bf16[512,1024]{1,0:T(8,128)(2,1)}, u32[]{:S(2)}, u32[]{:S(2)}) collective-permute-start(bf16[512,1024]{1,0:T(8,128)(2,1)} %get-tuple-element.18), channel_id=1, source_target_pairs={{0,28},{4,24},{8,20},{12,16},{16,12},{20,8},{24,4},{28,0},{1,29},{... | collective-permute-start | bytes 3145736 | tf_op jit(solution)/shard_map/ppermute | solution.py:438
  16.6 5.2 %copy-start = (f32[32]{0:T(128)S(1)}, f32[32]{0:T(128)}, u32[]{:S(2)}) copy-start(f32[32]{0:T(128)} %param.3) | copy-start | bytes 388
  16.6 140.5 %all-to-all-start = ((bf16[4,512,1024]{2,1,0:T(8,128)(2,1)}), bf16[4,512,1024]{2,1,0:T(8,128)(2,1)}, u32[]{:S(2)}, u32[]{:S(2)}) async-start(bf16[4,512,1024]{2,1,0:T(8,128)(2,1)} %get-tuple-element.19), calls=%async_computation | async-start | bytes 8388608 | tf_op jit(solution)/shard_map/all_to_all | solution.py:430
  167.9 1.4 collective-permute-start.4
  169.3 5.0 %collective-permute-start.5 = (f32[200,128]{1,0:T(8,128)S(1)}, f32[200,128]{1,0:T(8,128)S(1)}, u32[]{:S(2)}, u32[]{:S(2)}) collective-permute-start(f32[200,128]{1,0:T(8,128)S(1)} %add.21), channel_id=1, source_target_pairs={{0,1},{1,0},{2,3},{3,2},{4,5},{5,4},{6,7},{7,6},{8,9},{9,8},{10,11... | collective-permute-start | bytes 307208 | tf_op jit(solution)/shard_map/ppermute | solution.py:412
  174.3 4.7 %collective-permute-start.6 = (f32[200,128]{1,0:T(8,128)S(1)}, f32[200,128]{1,0:T(8,128)S(1)}, u32[]{:S(2)}, u32[]{:S(2)}) collective-permute-start(f32[200,128]{1,0:T(8,128)S(1)} %add.22), channel_id=1, source_target_pairs={{0,4},{4,0},{8,12},{12,8},{16,20},{20,16},{24,28},{28,24},{1,5},{5... | collective-permute-start | bytes 307208 | tf_op jit(solution)/shard_map/ppermute | solution.py:415
  179.1 33.2 %collective-permute-start.7 = (f32[200,128]{1,0:T(8,128)S(1)}, f32[200,128]{1,0:T(8,128)S(1)}, u32[]{:S(2)}, u32[]{:S(2)}) collective-permute-start(f32[200,128]{1,0:T(8,128)S(1)} %add.23), channel_id=1, source_target_pairs={{0,8},{4,12},{8,0},{12,4},{16,24},{20,28},{24,16},{28,20},{1,9},{5... | collective-permute-start | bytes 307208 | tf_op jit(solution)/shard_map/ppermute | solution.py:415
  212.2 8.2 %collective-permute-start.8 = (f32[200,128]{1,0:T(8,128)S(1)}, f32[200,128]{1,0:T(8,128)S(1)}, u32[]{:S(2)}, u32[]{:S(2)}) collective-permute-start(f32[200,128]{1,0:T(8,128)S(1)} %add.24), channel_id=1, source_target_pairs={{0,16},{4,20},{8,24},{12,28},{16,0},{20,4},{24,8},{28,12},{1,17},{... | collective-permute-start | bytes 307208 | tf_op jit(solution)/shard_map/ppermute | solution.py:415
  220.4 1.4 collective-permute-start.9

commit v4 on v3

--- a/solution.py
+++ b/solution.py
@@ -50,20 +50,20 @@
     return [slice(c, c + size) for c in range(0, width, size)]
 
 
-def pack_kernel(far_count, j_ref, near_ref, *refs):
-    far_refs, (buffer, out, in_sems, out_sems) = refs[:far_count], refs[far_count:]
+def pack_kernel(parts, far, j_ref, *refs):
+    half = parts // 2
+    out_refs, (buffer, out, in_sems, out_sems) = refs[:-4], refs[-4:]
     count, rows, slabs, width = buffer.shape
     me = lax.axis_index("smp")
-    high = me // far_count
-    dests = [high * far_count + k for k in range(far_count)]
-    dests += [me ^ (far_count + k) for k in range(far_count)]
 
     def read(k):
-        columns = pl.ds(pl.multiple_of(dests[k] * width, LANES), width)
+        dest = me ^ far[k] if far else me // half * half + k
+        columns = pl.ds(pl.multiple_of(dest * width, LANES), width)
         return pltpu.make_async_copy(j_ref.at[:, :, columns], buffer.at[k], in_sems.at[k])
 
     def write(k):
-        return pltpu.make_async_copy(out.at[k], near_ref.at[k], out_sems.at[k])
+        target = out_refs[k] if far else out_refs[0].at[k]
+        return pltpu.make_async_copy(out.at[k], target, out_sems.at[k])
 
     for k in range(count):
         read(k).start()
@@ -71,38 +71,32 @@
         read(k).wait()
         for part in lane_chunks(width):
             x = jnp.swapaxes(buffer[k, :, :, part].astype(F32), 0, 1)
-            x = x.reshape(slabs * rows, x.shape[2]).astype(BF16)
-            if k < far_count:
-                out[k, :, part] = x
-            else:
-                far_refs[k - far_count][:, part] = x
-        if k < far_count:
-            write(k).start()
-    for k in range(far_count):
+            out[k, :, part] = x.reshape(slabs * rows, x.shape[2]).astype(BF16)
+        write(k).start()
+    for k in range(count):
         write(k).wait()
 
 
-def pack(jacobian, parts):
+def pack(jacobian, parts, far):
     rows, slabs, columns = jacobian.shape
-    far_count, width = parts // 2, columns // parts
+    count, width = len(far) or parts // 2, columns // parts
     height = slabs * rows
-    return call(
-        functools.partial(pack_kernel, far_count),
-        [pltpu.HBM((far_count, height, width), BF16)]
-        + [jax.ShapeDtypeStruct((height, width), BF16)] * far_count,
+    shapes = [(height, width)] * count if far else [(count, height, width)]
+    return call(
+        functools.partial(pack_kernel, parts, far),
+        [pltpu.HBM(shape, BF16) for shape in shapes],
         pl.GridSpec(
             grid=(),
             in_specs=[pl.BlockSpec(memory_space=pl.ANY)],
-            out_specs=[pl.BlockSpec(memory_space=pl.ANY)]
-            + [pl.BlockSpec(memory_space=pltpu.VMEM)] * far_count,
+            out_specs=[pl.BlockSpec(memory_space=pl.ANY)] * len(shapes),
             scratch_shapes=[
-                pltpu.VMEM((parts, rows, slabs, width), BF16),
-                pltpu.VMEM((far_count, height, width), BF16),
-                pltpu.SemaphoreType.DMA((parts,)),
-                pltpu.SemaphoreType.DMA((far_count,)),
+                pltpu.VMEM((count, rows, slabs, width), BF16),
+                pltpu.VMEM((count, height, width), BF16),
+                pltpu.SemaphoreType.DMA((count,)),
+                pltpu.SemaphoreType.DMA((count,)),
             ],
         ),
-        vmem=52,
+        vmem=58,
     )(jacobian)
 
 
@@ -186,10 +180,14 @@
     products_far = by_distance(total_products, 1, rows, place[2])
     cross, far_far = products_far[:total], by_distance(products_far[total:], 0, rows, place[2])
     near_near = near_ref[...]
-    gram[:total, :] = jnp.where(low, near_near, far_far)
-    gram[total : 2 * total, :] = jnp.where(low, far_far, near_near)
-    gram[2 * total : 3 * total, :] = jnp.where(low, cross, cross.T)
-    gram[3 * total :, :] = extra_ref[...]
+    low_low = jnp.where(low, near_near, far_far)
+    high_high = jnp.where(low, far_far, near_near)
+    row = lax.broadcasted_iota(jnp.int32, (total, total), 0)
+    lane = lax.broadcasted_iota(jnp.int32, (total, total), 1)
+    gram[:total, :] = jnp.where(row >= lane, low_low, high_high)
+    gram[total : 2 * total, :] = jnp.where(low, cross, cross.T)
+    diagonal = jnp.sum(jnp.where(row == lane, high_high, 0.0), axis=0, keepdims=True)
+    gram[2 * total :, :] = jnp.where(row[:EXTRA] == 2, diagonal, extra_ref[...])
     count = mine_ref.shape[0]
     mine_ref[...] = gram[pl.ds(pl.multiple_of(place[1] * count, 8), count), :]
     other_ref[...] = gram[pl.ds(pl.multiple_of((1 - place[1]) * count, 8), count), :]
@@ -198,7 +196,7 @@
 def far_products(far_blocks, place, cn, base, near_gram, extra):
     _, total, width = cn.shape
     rows = total // len(far_blocks)
-    height = 3 * total + EXTRA
+    height = 2 * total + EXTRA
     share = jax.ShapeDtypeStruct((height // 2, total), F32)
     whole = pl.BlockSpec(memory_space=pltpu.VMEM)
     return call(
@@ -284,9 +282,13 @@
     sums[pl.ds(pl.multiple_of((1 - core[0]) * count, 8), count), :] = other_ref[...]
     half = sums.shape[1]
     samples = 2 * half
-    low, high = sums[:half, :], sums[half : 2 * half, :]
-    cross = sums[2 * half : 3 * half, :]
-    turned = cross.T
+    both, cross = sums[:half, :], sums[half : 2 * half, :]
+    e = sums[2 * half : 2 * half + 8, :]
+    flipped, turned = both.T, cross.T
+    row = lax.broadcasted_iota(jnp.int32, (half, half), 0)
+    lane = lax.broadcasted_iota(jnp.int32, (half, half), 1)
+    low = jnp.where(row >= lane, both, flipped)
+    high = jnp.where(row < lane, both, jnp.where(row > lane, flipped, e[2:3]))
     inv = 1.0 / samples
     col_low = (jnp.sum(low, axis=1, keepdims=True) + jnp.sum(cross, axis=1, keepdims=True)) * inv
     col_high = (jnp.sum(high, axis=1, keepdims=True) + jnp.sum(turned, axis=1, keepdims=True)) * inv
@@ -306,7 +308,6 @@
     diagonal = jnp.sum(diagonal, axis=0, keepdims=True)
     shift = jnp.sum(diagonal, axis=1, keepdims=True) * (0.01 * inv)
 
-    e = sums[3 * half : 3 * half + 8, :]
     energies = jnp.concatenate([e[0:1], e[1:2]], axis=1)
     center = jnp.sum(energies, axis=1, keepdims=True) * inv
     eps = jnp.broadcast_to((energies - center) * (inv**0.5), (8, samples))
@@ -426,7 +427,12 @@
     far = list(range(count, parts))
     high = me // count
 
-    near_rows, *far_rows = pack(jacobian, parts)
+    far_rows, after = [], jacobian
+    group = max(1, count // 2)
+    for k in range(0, count, group):
+        far_rows += pack(after, parts, far[k : k + group])
+        after, _ = lax.optimization_barrier((after, far_rows[-1]))
+    (near_rows,) = pack(after, parts, [])
     near = lax.all_to_all(
         near_rows,
         "smp",

time: 237 us -> 230 us (0.970)
  starting transfers between devices: 52.9 us -> 44.7 us
  Pallas kernels: 33 us -> 35.9 us
    ppermute x3, starting transfers between devices: 37 us -> 28.8 us  [sum_all(): mine = mine + lax.ppermute(mine, 'smp', xor_pairs(parts, bit))]
    pallas_call x1 -> x3, Pallas kernels: 7.6 us -> 10.5 us  [pack(): call(functools.partial(pack_kernel, parts, far), [pltpu.HBM(shape, BF16)...]
  transfers between devices with their start and end apart: 11 -> 11, of which waited for: 7 -> 7; matrix products, arithmetic and copies ran while one was open for 0% -> 0% of each run, Pallas kernels for 3% -> 6%
where the time goes in v4:
time: 230 us; the launch traced here: 229 us
  waiting for transfers between devices  149 us (65%)
  starting transfers between devices  44.7 us (19%)
  Pallas kernels  35.9 us (16%)
    all_to_all x1, waiting for transfers between devices, shards(): lax.all_to_all(near_rows, 'smp', split_axis=0, concat_axis=0, axis_index_...  135 us
    ppermute x3, starting transfers between devices, sum_all(): mine = mine + lax.ppermute(mine, 'smp', xor_pairs(parts, bit))  28.8 us
    pallas_call x1, Pallas kernels, solve(): call(functools.partial(solve_kernel, limit), jax.ShapeDtypeStruct((8, sam...  10.9 us
    pallas_call x3, Pallas kernels, pack(): call(functools.partial(pack_kernel, parts, far), [pltpu.HBM(shape, BF16)...  10.5 us
    ppermute x4, starting transfers between devices, shards(): lax.ppermute(r, 'smp', xor_pairs(parts, k))  9.08 us
    ppermute x3, waiting for transfers between devices, sum_all(): mine = mine + lax.ppermute(mine, 'smp', xor_pairs(parts, bit))  8.12 us
    pallas_call x1, Pallas kernels, near_products(): call(functools.partial(near_kernel, rows), (jax.ShapeDtypeStruct((slabs,...  6.43 us
    all_to_all x1, starting transfers between devices, shards(): lax.all_to_all(near_rows, 'smp', split_axis=0, concat_axis=0, axis_index_...  5.04 us
  transfers between devices with their start and end apart: 11, of which 7 were waited for; matrix products, arithmetic and copies ran while one was open for 0% of the time, Pallas kernels for 6%

profile of v4, /device:TPU:0, one launch (start us, length us, event | category | flops | bytes accessed | tf_op | source)
XLA Modules:
  0.0 229.5 jit_solution(8155008459595750869)
XLA Ops:
  0.0 3.1 %shard_map.28 = (bf16[512,1024]{1,0:T(8,128)(2,1)}, bf16[512,1024]{1,0:T(8,128)(2,1)}) custom-call(bf16[32,16,8192]{2,1,0:T(8,128)(2,1)} %j_ref.3), custom_call_target="tpu_custom_call" | custom-call | tf_op jit(solution)/shard_map/pallas_call | solution.py:85
  3.1 4.1 %collective-permute-start = (bf16[512,1024]{1,0:T(8,128)(2,1)}, bf16[512,1024]{1,0:T(8,128)(2,1)S(1)}, u32[]{:S(2)}, u32[]{:S(2)}) collective-permute-start(bf16[512,1024]{1,0:T(8,128)(2,1)} %get-tuple-element.16), channel_id=1, source_target_pairs={{0,16},{4,20},{8,24},{12,28},{16,0},{20,4},{24,8},{28,12},{1,17},{... | collective-permute-start | bytes 3145736 | tf_op jit(solution)/shard_map/ppermute | solution.py:444
  7.2 1.3 collective-permute-start.1
  8.5 3.2 %shard_map.29 = (bf16[512,1024]{1,0:T(8,128)(2,1)}, bf16[512,1024]{1,0:T(8,128)(2,1)}) custom-call(bf16[32,16,8192]{2,1,0:T(8,128)(2,1)} %j_ref.3), custom_call_target="tpu_custom_call" | custom-call | tf_op jit(solution)/shard_map/pallas_call | solution.py:85
  11.7 3.7 %collective-permute-start.2 = (bf16[512,1024]{1,0:T(8,128)(2,1)}, bf16[512,1024]{1,0:T(8,128)(2,1)S(1)}, u32[]{:S(2)}, u32[]{:S(2)}) collective-permute-start(bf16[512,1024]{1,0:T(8,128)(2,1)} %get-tuple-element.19), channel_id=1, source_target_pairs={{0,24},{4,28},{8,16},{12,20},{16,8},{20,12},{24,0},{28,4},{1,25},{... | collective-permute-start | bytes 3145736 | tf_op jit(solution)/shard_map/ppermute | solution.py:444
  15.4 0.0 collective-permute-start.3
  15.4 4.2 %shard_map.30 = bf16[4,512,1024]{2,1,0:T(8,128)(2,1)} custom-call(bf16[32,16,8192]{2,1,0:T(8,128)(2,1)} %j_ref.3), custom_call_target="tpu_custom_call" | custom-call | tf_op jit(solution)/shard_map/pallas_call | solution.py:85
  19.6 0.0 copy-start
  19.6 5.0 %all-to-all-start = ((bf16[4,512,1024]{2,1,0:T(8,128)(2,1)}), bf16[4,512,1024]{2,1,0:T(8,128)(2,1)}, u32[]{:S(2)}, u32[]{:S(2)}) async-start(bf16[4,512,1024]{2,1,0:T(8,128)(2,1)} %shard_map.30), calls=%async_computation | async-start | bytes 8388608 | tf_op jit(solution)/shard_map/all_to_all | solution.py:436
  24.7 0.0 copy-done
  24.7 0.1 shard_map.32.refs_7_
  24.7 0.1 pad_add_fusion.place
  24.8 135.2 %all-to-all-done.near_ref = bf16[4,512,1024]{2,1,0:T(8,128)(2,1)} async-done(((bf16[4,512,1024]{2,1,0:T(8,128)(2,1)}), bf16[4,512,1024]{2,1,0:T(8,128)(2,1)}, u32[]{:S(2)}, u32[]{:S(2)}) %all-to-all-start) | async-done | bytes 4194336 | tf_op jit(solution)/shard_map/all_to_all | solution.py:436
  160.0 6.4 %shard_map.31 = (bf16[16,128,1024]{2,1,0:T(8,128)(2,1)S(1)}, f32[16,1,1024]{2,1,0:T(1,128)S(1)}, f32[128,128]{1,0:T(8,128)S(1)}) custom-call(bf16[4,512,1024]{2,1,0:T(8,128)(2,1)} %all-to-all-done.near_ref), custom_call_target="tpu_custom_call" | custom-call | tf_op jit(solution)/shard_map/pallas_call | solution.py:132
  166.5 0.0 collective-permute-done.refs_0_
  166.5 0.0 collective-permute-done.1.refs_1_
  166.5 0.0 collective-permute-done.2.refs_2_
  166.5 0.0 collective-permute-done.3.refs_3_
  166.5 4.3 %shard_map.33 = (f32[136,128]{1,0:T(8,128)S(1)}, f32[136,128]{1,0:T(8,128)S(1)}) custom-call(s32[3]{0:T(128)S(1)} %pad_add_fusion.place, bf16[512,1024]{1,0:T(8,128)(2,1)S(1)} %collective-permute-done.refs_0_, bf16[512,1024]{1,0:T(8,128)(2,1)S(1)} %collective-permute-done.1.refs_1_, bf16[512,1024]{1,0:T(8,128)(2,1)S(1)} %collective-permute-done.2.refs_2_, ...), custom_call_target="tpu_custom_call" | custom-call | tf_op jit(solution)/shard_map/pallas_call | solution.py:202
  170.8 0.1 collective-permute-start.4
  170.9 1.2 collective-permute-done.4
  172.1 1.6 collective-permute-start.5
  173.8 2.7 %collective-permute-done.5 = f32[136,128]{1,0:T(8,128)S(1)} collective-permute-done((f32[136,128]{1,0:T(8,128)S(1)}, f32[136,128]{1,0:T(8,128)S(1)}, u32[]{:S(2)}, u32[]{:S(2)}) %collective-permute-start.5) | collective-permute-done | bytes 69664 | tf_op jit(solution)/shard_map/ppermute | solution.py:413
  176.5 1.6 collective-permute-start.6
  178.1 2.8 %collective-permute-done.6 = f32[136,128]{1,0:T(8,128)S(1)} collective-permute-done((f32[136,128]{1,0:T(8,128)S(1)}, f32[136,128]{1,0:T(8,128)S(1)}, u32[]{:S(2)}, u32[]{:S(2)}) %collective-permute-start.6) | collective-permute-done | bytes 69664 | tf_op jit(solution)/shard_map/ppermute | solution.py:416
  180.9 23.2 %collective-permute-start.7 = (f32[136,128]{1,0:T(8,128)S(1)}, f32[136,128]{1,0:T(8,128)S(1)}, u32[]{:S(2)}, u32[]{:S(2)}) collective-permute-start(f32[136,128]{1,0:T(8,128)S(1)} %add.23), channel_id=1, source_target_pairs={{0,8},{4,12},{8,0},{12,4},{16,24},{20,28},{24,16},{28,20},{1,9},{5... | collective-permute-start | bytes 208904 | tf_op jit(solution)/shard_map/ppermute | solution.py:416
  204.1 2.3 collective-permute-done.7
  206.4 4.1 %collective-permute-start.8 = (f32[136,128]{1,0:T(8,128)S(1)}, f32[136,128]{1,0:T(8,128)S(1)}, u32[]{:S(2)}, u32[]{:S(2)}) collective-permute-start(f32[136,128]{1,0:T(8,128)S(1)} %add.24), channel_id=1, source_target_pairs={{0,16},{4,20},{8,24},{12,28},{16,0},{20,4},{24,8},{28,12},{1,17},{... | collective-permute-start | bytes 208904 | tf_op jit(solution)/shard_map/ppermute | solution.py:416
  210.5 3.0 %collective-permute-done.8 = f32[136,128]{1,0:T(8,128)S(1)} collective-permute-done((f32[136,128]{1,0:T(8,128)S(1)}, f32[136,128]{1,0:T(8,128)S(1)}, u32[]{:S(2)}, u32[]{:S(2)}) %collective-permute-start.8) | collective-permute-done | bytes 69664 | tf_op jit(solution)/shard_map/ppermute | solution.py:416
  213.5 0.1 collective-permute-start.9
  213.6 1.2 collective-permute-done.9.other_ref
  214.9 10.9 %shard_map.34.x_ref = f32[8,256]{1,0:T(8,128)S(1)} custom-call(s32[1]{0:T(128)} %bitcast.1.core, f32[136,128]{1,0:T(8,128)S(1)} %add.25.mine_ref, f32[136,128]{1,0:T(8,128)S(1)} %collective-permute-done.9.other_ref), custom_call_target="tpu_custom_call" | custom-call | tf_op jit(solution)/shard_map/pallas_call | solution.py:345
  225.7 3.8 %shard_map.35 = f32[16,1024]{1,0:T(8,128)} custom-call(s32[3]{0:T(128)S(1)} %pad_add_fusion.place, f32[8,256]{1,0:T(8,128)S(1)} %shard_map.34.x_ref, bf16[16,128,1024]{2,1,0:T(8,128)(2,1)S(1)} %get-tuple-element.22.refs_4_.cn_ref, f32[16,1,1024]{2,1,0:T(1,128)S(1)} %get-tuple-element.23.refs_5_.base_ref, bf16[512,1024]{1,0:T(8,128)(2,1)S(1)} %collective-permute-done.refs_0_, ...), custom_call_target="tpu_custom_call" | custom-call | tf_op jit(solution)/shard_map/pallas_call | solution.py:394
  (5 shorter events, 0.0 us)
Async XLA Ops:
  3.1 163.3 %collective-permute-start = (bf16[512,1024]{1,0:T(8,128)(2,1)}, bf16[512,1024]{1,0:T(8,128)(2,1)S(1)}, u32[]{:S(2)}, u32[]{:S(2)}) collective-permute-start(bf16[512,1024]{1,0:T(8,128)(2,1)} %get-tuple-element.16), channel_id=1, source_target_pairs={{0,16},{4,20},{8,24},{12,28},{16,0},{20,4},{24,8},{28,12},{1,17},{... | collective-permute-start | bytes 3145736 | tf_op jit(solution)/shard_map/ppermute | solution.py:444
  7.2 159.2 %collective-permute-start.1 = (bf16[512,1024]{1,0:T(8,128)(2,1)}, bf16[512,1024]{1,0:T(8,128)(2,1)S(1)}, u32[]{:S(2)}, u32[]{:S(2)}) collective-permute-start(bf16[512,1024]{1,0:T(8,128)(2,1)} %get-tuple-element.17), channel_id=1, source_target_pairs={{0,20},{4,16},{8,28},{12,24},{16,4},{20,0},{24,12},{28,8},{1,21},{... | collective-permute-start | bytes 3145736 | tf_op jit(solution)/shard_map/ppermute | solution.py:444
  11.7 154.8 %collective-permute-start.2 = (bf16[512,1024]{1,0:T(8,128)(2,1)}, bf16[512,1024]{1,0:T(8,128)(2,1)S(1)}, u32[]{:S(2)}, u32[]{:S(2)}) collective-permute-start(bf16[512,1024]{1,0:T(8,128)(2,1)} %get-tuple-element.19), channel_id=1, source_target_pairs={{0,24},{4,28},{8,16},{12,20},{16,8},{20,12},{24,0},{28,4},{1,25},{... | collective-permute-start | bytes 3145736 | tf_op jit(solution)/shard_map/ppermute | solution.py:444
  15.4 151.1 %collective-permute-start.3 = (bf16[512,1024]{1,0:T(8,128)(2,1)}, bf16[512,1024]{1,0:T(8,128)(2,1)}, u32[]{:S(2)}, u32[]{:S(2)}) collective-permute-start(bf16[512,1024]{1,0:T(8,128)(2,1)} %get-tuple-element.20), channel_id=1, source_target_pairs={{0,28},{4,24},{8,20},{12,16},{16,12},{20,8},{24,4},{28,0},{1,29},{... | collective-permute-start | bytes 3145736 | tf_op jit(solution)/shard_map/ppermute | solution.py:444
  19.6 5.1 %copy-start = (f32[32]{0:T(128)S(1)}, f32[32]{0:T(128)}, u32[]{:S(2)}) copy-start(f32[32]{0:T(128)} %param.3) | copy-start | bytes 388
  19.6 140.4 %all-to-all-start = ((bf16[4,512,1024]{2,1,0:T(8,128)(2,1)}), bf16[4,512,1024]{2,1,0:T(8,128)(2,1)}, u32[]{:S(2)}, u32[]{:S(2)}) async-start(bf16[4,512,1024]{2,1,0:T(8,128)(2,1)} %shard_map.30), calls=%async_computation | async-start | bytes 8388608 | tf_op jit(solution)/shard_map/all_to_all | solution.py:436
  170.8 1.3 collective-permute-start.4
  172.1 4.4 %collective-permute-start.5 = (f32[136,128]{1,0:T(8,128)S(1)}, f32[136,128]{1,0:T(8,128)S(1)}, u32[]{:S(2)}, u32[]{:S(2)}) collective-permute-start(f32[136,128]{1,0:T(8,128)S(1)} %add.21), channel_id=1, source_target_pairs={{0,1},{1,0},{2,3},{3,2},{4,5},{5,4},{6,7},{7,6},{8,9},{9,8},{10,11... | collective-permute-start | bytes 208904 | tf_op jit(solution)/shard_map/ppermute | solution.py:413
  176.5 4.4 %collective-permute-start.6 = (f32[136,128]{1,0:T(8,128)S(1)}, f32[136,128]{1,0:T(8,128)S(1)}, u32[]{:S(2)}, u32[]{:S(2)}) collective-permute-start(f32[136,128]{1,0:T(8,128)S(1)} %add.22), channel_id=1, source_target_pairs={{0,4},{4,0},{8,12},{12,8},{16,20},{20,16},{24,28},{28,24},{1,5},{5... | collective-permute-start | bytes 208904 | tf_op jit(solution)/shard_map/ppermute | solution.py:416
  180.9 25.4 %collective-permute-start.7 = (f32[136,128]{1,0:T(8,128)S(1)}, f32[136,128]{1,0:T(8,128)S(1)}, u32[]{:S(2)}, u32[]{:S(2)}) collective-permute-start(f32[136,128]{1,0:T(8,128)S(1)} %add.23), channel_id=1, source_target_pairs={{0,8},{4,12},{8,0},{12,4},{16,24},{20,28},{24,16},{28,20},{1,9},{5... | collective-permute-start | bytes 208904 | tf_op jit(solution)/shard_map/ppermute | solution.py:416
  206.4 7.1 %collective-permute-start.8 = (f32[136,128]{1,0:T(8,128)S(1)}, f32[136,128]{1,0:T(8,128)S(1)}, u32[]{:S(2)}, u32[]{:S(2)}) collective-permute-start(f32[136,128]{1,0:T(8,128)S(1)} %add.24), channel_id=1, source_target_pairs={{0,16},{4,20},{8,24},{12,28},{16,0},{20,4},{24,8},{28,12},{1,17},{... | collective-permute-start | bytes 208904 | tf_op jit(solution)/shard_map/ppermute | solution.py:416
  213.5 1.3 collective-permute-start.9

commit v5 on v4

--- a/solution.py
+++ b/solution.py
@@ -160,7 +160,7 @@
 
 
 def far_kernel(rows, place, *refs):
-    far_refs, (cn_ref, base_ref, near_ref, extra_ref, mine_ref, other_ref, gram, far) = refs[:-8], refs[-8:]
+    far_refs, (cn_ref, base_ref, near_ref, extra_ref, mine_ref, other_ref, last_ref, gram, far) = refs[:-9], refs[-9:]
     slabs, total, width = cn_ref.shape
 
     def add(slab):
@@ -170,6 +170,7 @@
             for k, ref in enumerate(far_refs):
                 x = ref[span, part].astype(F32) - base
                 far[k * rows : (k + 1) * rows, part] = x.astype(BF16)
+        last_ref[span, :] = far_refs[-1][span, :]
         c = far[...]
         return products(jnp.concatenate([cn_ref[slab], c], axis=0), c)
 
@@ -201,12 +202,12 @@
     whole = pl.BlockSpec(memory_space=pltpu.VMEM)
     return call(
         functools.partial(far_kernel, rows),
-        (share, share),
+        (share, share, pltpu.VMEM(far_blocks[-1].shape, BF16)),
         pltpu.PrefetchScalarGridSpec(
             num_scalar_prefetch=1,
             grid=(),
             in_specs=[whole] * (len(far_blocks) + 4),
-            out_specs=[whole] * 2,
+            out_specs=[whole] * 3,
             scratch_shapes=[
                 pltpu.VMEM((height, total), F32),
                 pltpu.VMEM((total, width), BF16),
@@ -447,10 +448,10 @@
     cn, base, near_gram = near_products(near, slabs)
     core = lax.axis_index("col")
     place = jnp.stack([high, core, me % count])
-    mine, other = far_products(far_blocks, place, cn, base, near_gram, extra)
+    mine, other, last = far_products(far_blocks, place, cn, base, near_gram, extra)
     mine, other = sum_all(mine, other, parts)
     x = solve(core[None], mine, other, 0.3 * float(params) ** 0.5)
-    return update(x, place, cn, base, far_blocks)
+    return update(x, place, cn, base, [*far_blocks[:-1], last])
 
 
 def solution(mesh):

time: 230 us -> 229 us (level)
  no operation moved by 1% of the time
where the time goes in v5:
time: 229 us; the launch traced here: 228 us
  waiting for transfers between devices  149 us (65%)
  starting transfers between devices  44.8 us (20%)
  Pallas kernels  34.7 us (15%)
    all_to_all x1, waiting for transfers between devices, shards(): lax.all_to_all(near_rows, 'smp', split_axis=0, concat_axis=0, axis_index_...  135 us
    ppermute x3, starting transfers between devices, sum_all(): mine = mine + lax.ppermute(mine, 'smp', xor_pairs(parts, bit))  28.9 us
    pallas_call x1, Pallas kernels, solve(): call(functools.partial(solve_kernel, limit), jax.ShapeDtypeStruct((8, sam...  10.9 us
    pallas_call x3, Pallas kernels, pack(): call(functools.partial(pack_kernel, parts, far), [pltpu.HBM(shape, BF16)...  10.5 us
    ppermute x4, starting transfers between devices, shards(): lax.ppermute(r, 'smp', xor_pairs(parts, k))  9.08 us
    ppermute x3, waiting for transfers between devices, sum_all(): mine = mine + lax.ppermute(mine, 'smp', xor_pairs(parts, bit))  8.12 us
    pallas_call x1, Pallas kernels, near_products(): call(functools.partial(near_kernel, rows), (jax.ShapeDtypeStruct((slabs,...  6.43 us
    all_to_all x1, starting transfers between devices, shards(): lax.all_to_all(near_rows, 'smp', split_axis=0, concat_axis=0, axis_index_...  5.04 us
  transfers between devices with their start and end apart: 11, of which 7 were waited for; matrix products, arithmetic and copies ran while one was open for 0% of the time, Pallas kernels for 6%

profile of v5, /device:TPU:0, one launch (start us, length us, event | category | flops | bytes accessed | tf_op | source)
XLA Modules:
  0.0 228.3 jit_solution(14223477390073479794)
XLA Ops:
  0.0 3.1 %shard_map.28 = (bf16[512,1024]{1,0:T(8,128)(2,1)}, bf16[512,1024]{1,0:T(8,128)(2,1)}) custom-call(bf16[32,16,8192]{2,1,0:T(8,128)(2,1)} %j_ref.3), custom_call_target="tpu_custom_call" | custom-call | tf_op jit(solution)/shard_map/pallas_call | solution.py:85
  3.2 4.1 %collective-permute-start = (bf16[512,1024]{1,0:T(8,128)(2,1)}, bf16[512,1024]{1,0:T(8,128)(2,1)S(1)}, u32[]{:S(2)}, u32[]{:S(2)}) collective-permute-start(bf16[512,1024]{1,0:T(8,128)(2,1)} %get-tuple-element.17), channel_id=1, source_target_pairs={{0,16},{4,20},{8,24},{12,28},{16,0},{20,4},{24,8},{28,12},{1,17},{... | collective-permute-start | bytes 3145736 | tf_op jit(solution)/shard_map/ppermute | solution.py:445
  7.3 1.3 collective-permute-start.1
  8.5 3.2 %shard_map.29 = (bf16[512,1024]{1,0:T(8,128)(2,1)}, bf16[512,1024]{1,0:T(8,128)(2,1)}) custom-call(bf16[32,16,8192]{2,1,0:T(8,128)(2,1)} %j_ref.3), custom_call_target="tpu_custom_call" | custom-call | tf_op jit(solution)/shard_map/pallas_call | solution.py:85
  11.7 3.7 %collective-permute-start.2 = (bf16[512,1024]{1,0:T(8,128)(2,1)}, bf16[512,1024]{1,0:T(8,128)(2,1)S(1)}, u32[]{:S(2)}, u32[]{:S(2)}) collective-permute-start(bf16[512,1024]{1,0:T(8,128)(2,1)} %get-tuple-element.20), channel_id=1, source_target_pairs={{0,24},{4,28},{8,16},{12,20},{16,8},{20,12},{24,0},{28,4},{1,25},{... | collective-permute-start | bytes 3145736 | tf_op jit(solution)/shard_map/ppermute | solution.py:445
  15.4 0.0 collective-permute-start.3
  15.4 4.2 %shard_map.30 = bf16[4,512,1024]{2,1,0:T(8,128)(2,1)} custom-call(bf16[32,16,8192]{2,1,0:T(8,128)(2,1)} %j_ref.3), custom_call_target="tpu_custom_call" | custom-call | tf_op jit(solution)/shard_map/pallas_call | solution.py:85
  19.6 0.0 copy-start
  19.6 5.0 %all-to-all-start = ((bf16[4,512,1024]{2,1,0:T(8,128)(2,1)}), bf16[4,512,1024]{2,1,0:T(8,128)(2,1)}, u32[]{:S(2)}, u32[]{:S(2)}) async-start(bf16[4,512,1024]{2,1,0:T(8,128)(2,1)} %shard_map.30), calls=%async_computation | async-start | bytes 8388608 | tf_op jit(solution)/shard_map/all_to_all | solution.py:437
  24.6 0.0 copy-done
  24.6 0.1 shard_map.32.refs_7_
  24.7 0.1 pad_add_fusion.place
  24.8 135.2 %all-to-all-done.near_ref = bf16[4,512,1024]{2,1,0:T(8,128)(2,1)} async-done(((bf16[4,512,1024]{2,1,0:T(8,128)(2,1)}), bf16[4,512,1024]{2,1,0:T(8,128)(2,1)}, u32[]{:S(2)}, u32[]{:S(2)}) %all-to-all-start) | async-done | bytes 4194336 | tf_op jit(solution)/shard_map/all_to_all | solution.py:437
  160.0 6.4 %shard_map.31 = (bf16[16,128,1024]{2,1,0:T(8,128)(2,1)S(1)}, f32[16,1,1024]{2,1,0:T(1,128)S(1)}, f32[128,128]{1,0:T(8,128)S(1)}) custom-call(bf16[4,512,1024]{2,1,0:T(8,128)(2,1)} %all-to-all-done.near_ref), custom_call_target="tpu_custom_call" | custom-call | tf_op jit(solution)/shard_map/pallas_call | solution.py:132
  166.4 0.0 collective-permute-done.refs_0_
  166.5 0.0 collective-permute-done.1.refs_1_
  166.5 0.0 collective-permute-done.2.refs_2_
  166.5 0.0 collective-permute-done.3.refs_3_
  166.5 4.4 %shard_map.33 = (f32[136,128]{1,0:T(8,128)S(1)}, f32[136,128]{1,0:T(8,128)S(1)}, bf16[512,1024]{1,0:T(8,128)(2,1)S(1)}) custom-call(s32[3]{0:T(128)S(1)} %pad_add_fusion.place, bf16[512,1024]{1,0:T(8,128)(2,1)S(1)} %collective-permute-done.refs_0_, bf16[512,1024]{1,0:T(8,128)(2,1)S(1)} %collective-permute-done.1.refs_1_, ...), custom_call_target="tpu_custom_call" | custom-call | tf_op jit(solution)/shard_map/pallas_call | solution.py:203
  170.8 0.1 collective-permute-start.4
  170.9 1.2 collective-permute-done.4
  172.2 1.6 collective-permute-start.5
  173.8 2.7 %collective-permute-done.5 = f32[136,128]{1,0:T(8,128)S(1)} collective-permute-done((f32[136,128]{1,0:T(8,128)S(1)}, f32[136,128]{1,0:T(8,128)S(1)}, u32[]{:S(2)}, u32[]{:S(2)}) %collective-permute-start.5) | collective-permute-done | bytes 69664 | tf_op jit(solution)/shard_map/ppermute | solution.py:414
  176.6 1.6 collective-permute-start.6
  178.2 2.8 %collective-permute-done.6 = f32[136,128]{1,0:T(8,128)S(1)} collective-permute-done((f32[136,128]{1,0:T(8,128)S(1)}, f32[136,128]{1,0:T(8,128)S(1)}, u32[]{:S(2)}, u32[]{:S(2)}) %collective-permute-start.6) | collective-permute-done | bytes 69664 | tf_op jit(solution)/shard_map/ppermute | solution.py:417
  181.0 23.2 %collective-permute-start.7 = (f32[136,128]{1,0:T(8,128)S(1)}, f32[136,128]{1,0:T(8,128)S(1)}, u32[]{:S(2)}, u32[]{:S(2)}) collective-permute-start(f32[136,128]{1,0:T(8,128)S(1)} %add.23), channel_id=1, source_target_pairs={{0,8},{4,12},{8,0},{12,4},{16,24},{20,28},{24,16},{28,20},{1,9},{5... | collective-permute-start | bytes 208904 | tf_op jit(solution)/shard_map/ppermute | solution.py:417
  204.1 2.3 %collective-permute-done.7 = f32[136,128]{1,0:T(8,128)S(1)} collective-permute-done((f32[136,128]{1,0:T(8,128)S(1)}, f32[136,128]{1,0:T(8,128)S(1)}, u32[]{:S(2)}, u32[]{:S(2)}) %collective-permute-start.7) | collective-permute-done | bytes 69664 | tf_op jit(solution)/shard_map/ppermute | solution.py:417
  206.4 4.1 %collective-permute-start.8 = (f32[136,128]{1,0:T(8,128)S(1)}, f32[136,128]{1,0:T(8,128)S(1)}, u32[]{:S(2)}, u32[]{:S(2)}) collective-permute-start(f32[136,128]{1,0:T(8,128)S(1)} %add.24), channel_id=1, source_target_pairs={{0,16},{4,20},{8,24},{12,28},{16,0},{20,4},{24,8},{28,12},{1,17},{... | collective-permute-start | bytes 208904 | tf_op jit(solution)/shard_map/ppermute | solution.py:417
  210.6 3.0 %collective-permute-done.8 = f32[136,128]{1,0:T(8,128)S(1)} collective-permute-done((f32[136,128]{1,0:T(8,128)S(1)}, f32[136,128]{1,0:T(8,128)S(1)}, u32[]{:S(2)}, u32[]{:S(2)}) %collective-permute-start.8) | collective-permute-done | bytes 69664 | tf_op jit(solution)/shard_map/ppermute | solution.py:417
  213.6 0.1 collective-permute-start.9
  213.7 1.2 collective-permute-done.9.other_ref
  214.9 10.9 %shard_map.34.x_ref = f32[8,256]{1,0:T(8,128)S(1)} custom-call(s32[1]{0:T(128)} %bitcast.1.core, f32[136,128]{1,0:T(8,128)S(1)} %add.25.mine_ref, f32[136,128]{1,0:T(8,128)S(1)} %collective-permute-done.9.other_ref), custom_call_target="tpu_custom_call" | custom-call | tf_op jit(solution)/shard_map/pallas_call | solution.py:346
  225.8 2.5 %shard_map.35 = f32[16,1024]{1,0:T(8,128)} custom-call(s32[3]{0:T(128)S(1)} %pad_add_fusion.place, f32[8,256]{1,0:T(8,128)S(1)} %shard_map.34.x_ref, bf16[16,128,1024]{2,1,0:T(8,128)(2,1)S(1)} %get-tuple-element.23.refs_4_.cn_ref, f32[16,1,1024]{2,1,0:T(1,128)S(1)} %get-tuple-element.24.refs_5_.base_ref, bf16[512,1024]{1,0:T(8,128)(2,1)S(1)} %collective-permute-done.refs_0_, ...), custom_call_target="tpu_custom_call" | custom-call | tf_op jit(solution)/shard_map/pallas_call | solution.py:395
  (5 shorter events, 0.0 us)
Async XLA Ops:
  3.2 163.3 %collective-permute-start = (bf16[512,1024]{1,0:T(8,128)(2,1)}, bf16[512,1024]{1,0:T(8,128)(2,1)S(1)}, u32[]{:S(2)}, u32[]{:S(2)}) collective-permute-start(bf16[512,1024]{1,0:T(8,128)(2,1)} %get-tuple-element.17), channel_id=1, source_target_pairs={{0,16},{4,20},{8,24},{12,28},{16,0},{20,4},{24,8},{28,12},{1,17},{... | collective-permute-start | bytes 3145736 | tf_op jit(solution)/shard_map/ppermute | solution.py:445
  7.3 159.2 %collective-permute-start.1 = (bf16[512,1024]{1,0:T(8,128)(2,1)}, bf16[512,1024]{1,0:T(8,128)(2,1)S(1)}, u32[]{:S(2)}, u32[]{:S(2)}) collective-permute-start(bf16[512,1024]{1,0:T(8,128)(2,1)} %get-tuple-element.18), channel_id=1, source_target_pairs={{0,20},{4,16},{8,28},{12,24},{16,4},{20,0},{24,12},{28,8},{1,21},{... | collective-permute-start | bytes 3145736 | tf_op jit(solution)/shard_map/ppermute | solution.py:445
  11.7 154.8 %collective-permute-start.2 = (bf16[512,1024]{1,0:T(8,128)(2,1)}, bf16[512,1024]{1,0:T(8,128)(2,1)S(1)}, u32[]{:S(2)}, u32[]{:S(2)}) collective-permute-start(bf16[512,1024]{1,0:T(8,128)(2,1)} %get-tuple-element.20), channel_id=1, source_target_pairs={{0,24},{4,28},{8,16},{12,20},{16,8},{20,12},{24,0},{28,4},{1,25},{... | collective-permute-start | bytes 3145736 | tf_op jit(solution)/shard_map/ppermute | solution.py:445
  15.4 151.1 %collective-permute-start.3 = (bf16[512,1024]{1,0:T(8,128)(2,1)}, bf16[512,1024]{1,0:T(8,128)(2,1)}, u32[]{:S(2)}, u32[]{:S(2)}) collective-permute-start(bf16[512,1024]{1,0:T(8,128)(2,1)} %get-tuple-element.21), channel_id=1, source_target_pairs={{0,28},{4,24},{8,20},{12,16},{16,12},{20,8},{24,4},{28,0},{1,29},{... | collective-permute-start | bytes 3145736 | tf_op jit(solution)/shard_map/ppermute | solution.py:445
  19.6 5.1 %copy-start = (f32[32]{0:T(128)S(1)}, f32[32]{0:T(128)}, u32[]{:S(2)}) copy-start(f32[32]{0:T(128)} %param.3) | copy-start | bytes 388
  19.6 140.4 %all-to-all-start = ((bf16[4,512,1024]{2,1,0:T(8,128)(2,1)}), bf16[4,512,1024]{2,1,0:T(8,128)(2,1)}, u32[]{:S(2)}, u32[]{:S(2)}) async-start(bf16[4,512,1024]{2,1,0:T(8,128)(2,1)} %shard_map.30), calls=%async_computation | async-start | bytes 8388608 | tf_op jit(solution)/shard_map/all_to_all | solution.py:437
  170.8 1.3 collective-permute-start.4
  172.2 4.4 %collective-permute-start.5 = (f32[136,128]{1,0:T(8,128)S(1)}, f32[136,128]{1,0:T(8,128)S(1)}, u32[]{:S(2)}, u32[]{:S(2)}) collective-permute-start(f32[136,128]{1,0:T(8,128)S(1)} %add.21), channel_id=1, source_target_pairs={{0,1},{1,0},{2,3},{3,2},{4,5},{5,4},{6,7},{7,6},{8,9},{9,8},{10,11... | collective-permute-start | bytes 208904 | tf_op jit(solution)/shard_map/ppermute | solution.py:414
  176.6 4.4 %collective-permute-start.6 = (f32[136,128]{1,0:T(8,128)S(1)}, f32[136,128]{1,0:T(8,128)S(1)}, u32[]{:S(2)}, u32[]{:S(2)}) collective-permute-start(f32[136,128]{1,0:T(8,128)S(1)} %add.22), channel_id=1, source_target_pairs={{0,4},{4,0},{8,12},{12,8},{16,20},{20,16},{24,28},{28,24},{1,5},{5... | collective-permute-start | bytes 208904 | tf_op jit(solution)/shard_map/ppermute | solution.py:417
  181.0 25.5 %collective-permute-start.7 = (f32[136,128]{1,0:T(8,128)S(1)}, f32[136,128]{1,0:T(8,128)S(1)}, u32[]{:S(2)}, u32[]{:S(2)}) collective-permute-start(f32[136,128]{1,0:T(8,128)S(1)} %add.23), channel_id=1, source_target_pairs={{0,8},{4,12},{8,0},{12,4},{16,24},{20,28},{24,16},{28,20},{1,9},{5... | collective-permute-start | bytes 208904 | tf_op jit(solution)/shard_map/ppermute | solution.py:417
  206.4 7.2 %collective-permute-start.8 = (f32[136,128]{1,0:T(8,128)S(1)}, f32[136,128]{1,0:T(8,128)S(1)}, u32[]{:S(2)}, u32[]{:S(2)}) collective-permute-start(f32[136,128]{1,0:T(8,128)S(1)} %add.24), channel_id=1, source_target_pairs={{0,16},{4,20},{8,24},{12,28},{16,0},{20,4},{24,8},{28,12},{1,17},{... | collective-permute-start | bytes 208904 | tf_op jit(solution)/shard_map/ppermute | solution.py:417
  213.6 1.3 collective-permute-start.9

commit v6 on v5

--- a/solution.py
+++ b/solution.py
@@ -411,11 +411,22 @@
 
 def sum_all(mine, other, parts):
     mine = mine + lax.ppermute(other, "col", SWAP)
-    mine = mine + lax.ppermute(mine, "slab", SWAP)
-    bit = 1
+    b = lax.ppermute(mine, "slab", SWAP)
+    c = lax.ppermute(mine, "smp", xor_pairs(parts, 1))
+    d = lax.ppermute(
+        mine, ("smp", "slab"), [(2 * i + j, 2 * (i ^ 1) + 1 - j) for i in range(parts) for j in range(2)]
+    )
+    mine = (mine + b) + (c + d)
+    bit = 2
     while bit < parts:
-        mine = mine + lax.ppermute(mine, "smp", xor_pairs(parts, bit))
-        bit *= 2
+        b = lax.ppermute(mine, "smp", xor_pairs(parts, bit))
+        if 2 * bit < parts:
+            c = lax.ppermute(mine, "smp", xor_pairs(parts, 2 * bit))
+            d = lax.ppermute(mine, "smp", xor_pairs(parts, 3 * bit))
+            mine = (mine + b) + (c + d)
+        else:
+            mine = mine + b
+        bit *= 4
     return mine, lax.ppermute(mine, "col", SWAP)
 
 

time: 229 us -> 227 us (level)
    ppermute x4 -> x6, starting transfers between devices: 30.5 us -> 29.2 us  [the longest x1 25 us: sum_all(): c = lax.ppermute(mine, 'smp', xor_pairs(parts, 2 * bit))]
    ppermute x4 -> x6, waiting for transfers between devices: 10.9 us -> 10.1 us  [the longest x1 3.95 us: sum_all(): c = lax.ppermute(mine, 'smp', xor_pairs(parts, 2 * bit))]
  transfers between devices with their start and end apart: 11 -> 13, of which waited for: 7 -> 8; matrix products, arithmetic and copies ran while one was open for 0% -> 0% of each run, Pallas kernels for 6% -> 6%
where the time goes in v6:
time: 227 us; the launch traced here: 226 us
  waiting for transfers between devices  148 us (65%)
  starting transfers between devices  43.4 us (19%)
  Pallas kernels  34.7 us (15%)
    all_to_all x1, waiting for transfers between devices, shards(): lax.all_to_all(near_rows, 'smp', split_axis=0, concat_axis=0, axis_index_...  135 us
    ppermute x1, starting transfers between devices, sum_all(): c = lax.ppermute(mine, 'smp', xor_pairs(parts, 2 * bit))  25 us
    pallas_call x1, Pallas kernels, solve(): call(functools.partial(solve_kernel, limit), jax.ShapeDtypeStruct((8, sam...  10.9 us
    pallas_call x3, Pallas kernels, pack(): call(functools.partial(pack_kernel, parts, far), [pltpu.HBM(shape, BF16)...  10.5 us
    ppermute x4, starting transfers between devices, shards(): lax.ppermute(r, 'smp', xor_pairs(parts, k))  9.08 us
    pallas_call x1, Pallas kernels, near_products(): call(functools.partial(near_kernel, rows), (jax.ShapeDtypeStruct((slabs,...  6.42 us
    all_to_all x1, starting transfers between devices, shards(): lax.all_to_all(near_rows, 'smp', split_axis=0, concat_axis=0, axis_index_...  5.04 us
  transfers between devices with their start and end apart: 13, of which 8 were waited for; matrix products, arithmetic and copies ran while one was open for 0% of the time, Pallas kernels for 6%

profile of v6, /device:TPU:0, one launch (start us, length us, event | category | flops | bytes accessed | tf_op | source)
XLA Modules:
  0.0 226.2 jit_solution(13610571457780170846)
XLA Ops:
  0.0 3.2 %shard_map.28 = (bf16[512,1024]{1,0:T(8,128)(2,1)}, bf16[512,1024]{1,0:T(8,128)(2,1)}) custom-call(bf16[32,16,8192]{2,1,0:T(8,128)(2,1)} %j_ref.3), custom_call_target="tpu_custom_call" | custom-call | tf_op jit(solution)/shard_map/pallas_call | solution.py:85
  3.2 4.1 %collective-permute-start = (bf16[512,1024]{1,0:T(8,128)(2,1)}, bf16[512,1024]{1,0:T(8,128)(2,1)S(1)}, u32[]{:S(2)}, u32[]{:S(2)}) collective-permute-start(bf16[512,1024]{1,0:T(8,128)(2,1)} %get-tuple-element.17), channel_id=1, source_target_pairs={{0,16},{4,20},{8,24},{12,28},{16,0},{20,4},{24,8},{28,12},{1,17},{... | collective-permute-start | bytes 3145736 | tf_op jit(solution)/shard_map/ppermute | solution.py:456
  7.3 1.3 collective-permute-start.1
  8.5 3.2 %shard_map.29 = (bf16[512,1024]{1,0:T(8,128)(2,1)}, bf16[512,1024]{1,0:T(8,128)(2,1)}) custom-call(bf16[32,16,8192]{2,1,0:T(8,128)(2,1)} %j_ref.3), custom_call_target="tpu_custom_call" | custom-call | tf_op jit(solution)/shard_map/pallas_call | solution.py:85
  11.7 3.7 %collective-permute-start.2 = (bf16[512,1024]{1,0:T(8,128)(2,1)}, bf16[512,1024]{1,0:T(8,128)(2,1)S(1)}, u32[]{:S(2)}, u32[]{:S(2)}) collective-permute-start(bf16[512,1024]{1,0:T(8,128)(2,1)} %get-tuple-element.20), channel_id=1, source_target_pairs={{0,24},{4,28},{8,16},{12,20},{16,8},{20,12},{24,0},{28,4},{1,25},{... | collective-permute-start | bytes 3145736 | tf_op jit(solution)/shard_map/ppermute | solution.py:456
  15.4 0.0 collective-permute-start.3
  15.4 4.1 %shard_map.30 = bf16[4,512,1024]{2,1,0:T(8,128)(2,1)} custom-call(bf16[32,16,8192]{2,1,0:T(8,128)(2,1)} %j_ref.3), custom_call_target="tpu_custom_call" | custom-call | tf_op jit(solution)/shard_map/pallas_call | solution.py:85
  19.6 0.0 copy-start
  19.6 5.0 %all-to-all-start = ((bf16[4,512,1024]{2,1,0:T(8,128)(2,1)}), bf16[4,512,1024]{2,1,0:T(8,128)(2,1)}, u32[]{:S(2)}, u32[]{:S(2)}) async-start(bf16[4,512,1024]{2,1,0:T(8,128)(2,1)} %shard_map.30), calls=%async_computation | async-start | bytes 8388608 | tf_op jit(solution)/shard_map/all_to_all | solution.py:448
  24.6 0.0 copy-done
  24.6 0.1 shard_map.32.refs_7_
  24.7 0.1 pad_add_fusion.place
  24.8 135.2 %all-to-all-done.near_ref = bf16[4,512,1024]{2,1,0:T(8,128)(2,1)} async-done(((bf16[4,512,1024]{2,1,0:T(8,128)(2,1)}), bf16[4,512,1024]{2,1,0:T(8,128)(2,1)}, u32[]{:S(2)}, u32[]{:S(2)}) %all-to-all-start) | async-done | bytes 4194336 | tf_op jit(solution)/shard_map/all_to_all | solution.py:448
  160.0 6.4 %shard_map.31 = (bf16[16,128,1024]{2,1,0:T(8,128)(2,1)S(1)}, f32[16,1,1024]{2,1,0:T(1,128)S(1)}, f32[128,128]{1,0:T(8,128)S(1)}) custom-call(bf16[4,512,1024]{2,1,0:T(8,128)(2,1)} %all-to-all-done.near_ref), custom_call_target="tpu_custom_call" | custom-call | tf_op jit(solution)/shard_map/pallas_call | solution.py:132
  166.4 0.0 collective-permute-done.refs_0_
  166.4 0.0 collective-permute-done.1.refs_1_
  166.5 0.0 collective-permute-done.2.refs_2_
  166.5 0.0 collective-permute-done.3.refs_3_
  166.5 4.4 %shard_map.33 = (f32[136,128]{1,0:T(8,128)S(1)}, f32[136,128]{1,0:T(8,128)S(1)}, bf16[512,1024]{1,0:T(8,128)(2,1)S(1)}) custom-call(s32[3]{0:T(128)S(1)} %pad_add_fusion.place, bf16[512,1024]{1,0:T(8,128)(2,1)S(1)} %collective-permute-done.refs_0_, bf16[512,1024]{1,0:T(8,128)(2,1)S(1)} %collective-permute-done.1.refs_1_, ...), custom_call_target="tpu_custom_call" | custom-call | tf_op jit(solution)/shard_map/pallas_call | solution.py:203
  170.8 0.1 collective-permute-start.4
  170.9 1.2 collective-permute-done.4
  172.2 1.6 collective-permute-start.6
  173.8 1.5 collective-permute-start.7
  175.3 0.5 collective-permute-start.5
  175.7 0.8 collective-permute-done.6
  176.6 2.6 %collective-permute-done.7 = f32[136,128]{1,0:T(8,128)S(1)} collective-permute-done((f32[136,128]{1,0:T(8,128)S(1)}, f32[136,128]{1,0:T(8,128)S(1)}, u32[]{:S(2)}, u32[]{:S(2)}) %collective-permute-start.7) | collective-permute-done | bytes 69664 | tf_op jit(solution)/shard_map/ppermute | solution.py:416
  179.2 1.1 collective-permute-done.5
  180.3 25.0 %collective-permute-start.9 = (f32[136,128]{1,0:T(8,128)S(1)}, f32[136,128]{1,0:T(8,128)S(1)}, u32[]{:S(2)}, u32[]{:S(2)}) collective-permute-start(f32[136,128]{1,0:T(8,128)S(1)} %add_add_fusion.1), channel_id=1, source_target_pairs={{0,16},{4,20},{8,24},{12,28},{16,0},{20,4},{24,8},{28,12},{1,17},{... | collective-permute-start | bytes 208904 | tf_op jit(solution)/shard_map/ppermute | solution.py:424
  205.3 0.3 collective-permute-start.10
  205.6 0.3 collective-permute-start.8
  205.9 4.0 %collective-permute-done.9 = f32[136,128]{1,0:T(8,128)S(1)} collective-permute-done((f32[136,128]{1,0:T(8,128)S(1)}, f32[136,128]{1,0:T(8,128)S(1)}, u32[]{:S(2)}, u32[]{:S(2)}) %collective-permute-start.9) | collective-permute-done | bytes 69664 | tf_op jit(solution)/shard_map/ppermute | solution.py:424
  209.9 1.6 collective-permute-done.10
  211.5 0.0 collective-permute-done.8
  211.5 0.1 collective-permute-start.11
  211.6 1.2 collective-permute-done.11.other_ref
  212.8 10.9 %shard_map.34.x_ref = f32[8,256]{1,0:T(8,128)S(1)} custom-call(s32[1]{0:T(128)} %bitcast.1.core, f32[136,128]{1,0:T(8,128)S(1)} %add_add_fusion.mine_ref, f32[136,128]{1,0:T(8,128)S(1)} %collective-permute-done.11.other_ref), custom_call_target="tpu_custom_call" | custom-call | tf_op jit(solution)/shard_map/pallas_call | solution.py:346
  223.7 2.5 %shard_map.35 = f32[16,1024]{1,0:T(8,128)} custom-call(s32[3]{0:T(128)S(1)} %pad_add_fusion.place, f32[8,256]{1,0:T(8,128)S(1)} %shard_map.34.x_ref, bf16[16,128,1024]{2,1,0:T(8,128)(2,1)S(1)} %get-tuple-element.23.refs_4_.cn_ref, f32[16,1,1024]{2,1,0:T(1,128)S(1)} %get-tuple-element.24.refs_5_.base_ref, bf16[512,1024]{1,0:T(8,128)(2,1)S(1)} %collective-permute-done.refs_0_, ...), custom_call_target="tpu_custom_call" | custom-call | tf_op jit(solution)/shard_map/pallas_call | solution.py:395
  (3 shorter events, 0.0 us)
Async XLA Ops:
  3.2 163.3 %collective-permute-start = (bf16[512,1024]{1,0:T(8,128)(2,1)}, bf16[512,1024]{1,0:T(8,128)(2,1)S(1)}, u32[]{:S(2)}, u32[]{:S(2)}) collective-permute-start(bf16[512,1024]{1,0:T(8,128)(2,1)} %get-tuple-element.17), channel_id=1, source_target_pairs={{0,16},{4,20},{8,24},{12,28},{16,0},{20,4},{24,8},{28,12},{1,17},{... | collective-permute-start | bytes 3145736 | tf_op jit(solution)/shard_map/ppermute | solution.py:456
  7.3 159.2 %collective-permute-start.1 = (bf16[512,1024]{1,0:T(8,128)(2,1)}, bf16[512,1024]{1,0:T(8,128)(2,1)S(1)}, u32[]{:S(2)}, u32[]{:S(2)}) collective-permute-start(bf16[512,1024]{1,0:T(8,128)(2,1)} %get-tuple-element.18), channel_id=1, source_target_pairs={{0,20},{4,16},{8,28},{12,24},{16,4},{20,0},{24,12},{28,8},{1,21},{... | collective-permute-start | bytes 3145736 | tf_op jit(solution)/shard_map/ppermute | solution.py:456
  11.7 154.8 %collective-permute-start.2 = (bf16[512,1024]{1,0:T(8,128)(2,1)}, bf16[512,1024]{1,0:T(8,128)(2,1)S(1)}, u32[]{:S(2)}, u32[]{:S(2)}) collective-permute-start(bf16[512,1024]{1,0:T(8,128)(2,1)} %get-tuple-element.20), channel_id=1, source_target_pairs={{0,24},{4,28},{8,16},{12,20},{16,8},{20,12},{24,0},{28,4},{1,25},{... | collective-permute-start | bytes 3145736 | tf_op jit(solution)/shard_map/ppermute | solution.py:456
  15.4 151.1 %collective-permute-start.3 = (bf16[512,1024]{1,0:T(8,128)(2,1)}, bf16[512,1024]{1,0:T(8,128)(2,1)}, u32[]{:S(2)}, u32[]{:S(2)}) collective-permute-start(bf16[512,1024]{1,0:T(8,128)(2,1)} %get-tuple-element.21), channel_id=1, source_target_pairs={{0,28},{4,24},{8,20},{12,16},{16,12},{20,8},{24,4},{28,0},{1,29},{... | collective-permute-start | bytes 3145736 | tf_op jit(solution)/shard_map/ppermute | solution.py:456
  19.6 5.1 %copy-start = (f32[32]{0:T(128)S(1)}, f32[32]{0:T(128)}, u32[]{:S(2)}) copy-start(f32[32]{0:T(128)} %param.3) | copy-start | bytes 388
  19.6 140.4 %all-to-all-start = ((bf16[4,512,1024]{2,1,0:T(8,128)(2,1)}), bf16[4,512,1024]{2,1,0:T(8,128)(2,1)}, u32[]{:S(2)}, u32[]{:S(2)}) async-start(bf16[4,512,1024]{2,1,0:T(8,128)(2,1)} %shard_map.30), calls=%async_computation | async-start | bytes 8388608 | tf_op jit(solution)/shard_map/all_to_all | solution.py:448
  170.8 1.3 collective-permute-start.4
  172.2 4.4 %collective-permute-start.6 = (f32[136,128]{1,0:T(8,128)S(1)}, f32[136,128]{1,0:T(8,128)S(1)}, u32[]{:S(2)}, u32[]{:S(2)}) collective-permute-start(f32[136,128]{1,0:T(8,128)S(1)} %add.27), channel_id=1, source_target_pairs={{0,4},{4,0},{8,12},{12,8},{16,20},{20,16},{24,28},{28,24},{1,5},{5... | collective-permute-start | bytes 208904 | tf_op jit(solution)/shard_map/ppermute | solution.py:415
  173.8 5.4 %collective-permute-start.7 = (f32[136,128]{1,0:T(8,128)S(1)}, f32[136,128]{1,0:T(8,128)S(1)}, u32[]{:S(2)}, u32[]{:S(2)}) collective-permute-start(f32[136,128]{1,0:T(8,128)S(1)} %add.27), channel_id=1, source_target_pairs={{0,5},{1,4},{4,1},{5,0},{8,13},{9,12},{12,9},{13,8},{16,21},{17,20... | collective-permute-start | bytes 208904 | tf_op jit(solution)/shard_map/ppermute | solution.py:416
  175.3 5.0 %collective-permute-start.5 = (f32[136,128]{1,0:T(8,128)S(1)}, f32[136,128]{1,0:T(8,128)S(1)}, u32[]{:S(2)}, u32[]{:S(2)}) collective-permute-start(f32[136,128]{1,0:T(8,128)S(1)} %add.27), channel_id=1, source_target_pairs={{0,1},{1,0},{2,3},{3,2},{4,5},{5,4},{6,7},{7,6},{8,9},{9,8},{10,11... | collective-permute-start | bytes 208904 | tf_op jit(solution)/shard_map/ppermute | solution.py:414
  180.3 29.6 %collective-permute-start.9 = (f32[136,128]{1,0:T(8,128)S(1)}, f32[136,128]{1,0:T(8,128)S(1)}, u32[]{:S(2)}, u32[]{:S(2)}) collective-permute-start(f32[136,128]{1,0:T(8,128)S(1)} %add_add_fusion.1), channel_id=1, source_target_pairs={{0,16},{4,20},{8,24},{12,28},{16,0},{20,4},{24,8},{28,12},{1,17},{... | collective-permute-start | bytes 208904 | tf_op jit(solution)/shard_map/ppermute | solution.py:424
  205.3 6.2 %collective-permute-start.10 = (f32[136,128]{1,0:T(8,128)S(1)}, f32[136,128]{1,0:T(8,128)S(1)}, u32[]{:S(2)}, u32[]{:S(2)}) collective-permute-start(f32[136,128]{1,0:T(8,128)S(1)} %add_add_fusion.1), channel_id=1, source_target_pairs={{0,24},{4,28},{8,16},{12,20},{16,8},{20,12},{24,0},{28,4},{1,25},{... | collective-permute-start | bytes 208904 | tf_op jit(solution)/shard_map/ppermute | solution.py:425
  205.6 5.9 %collective-permute-start.8 = (f32[136,128]{1,0:T(8,128)S(1)}, f32[136,128]{1,0:T(8,128)S(1)}, u32[]{:S(2)}, u32[]{:S(2)}) collective-permute-start(f32[136,128]{1,0:T(8,128)S(1)} %add_add_fusion.1), channel_id=1, source_target_pairs={{0,8},{4,12},{8,0},{12,4},{16,24},{20,28},{24,16},{28,20},{1,9},{5... | collective-permute-start | bytes 208904 | tf_op jit(solution)/shard_map/ppermute | solution.py:422
  211.5 1.3 collective-permute-start.11
